TPU v7x, 32 devices: a whole 2x2x4 slice. The times are simulated.
32 devices in a mesh: dp: 16 (over z, y, core), tensor: 2 (over x).
Axes of the slice: x: 2, y: 2, z: 4, core: 2. Of those that a mesh axis runs over, the one named last changes fastest.
Arguments:
- tokens: bfloat16 [32768, 1024], P(('dp', 'tensor')), may hold values from -6 to 6
- lengths: int32 [16, 16], P('dp'), may hold values from 1 to 1024, 2048 in all within a row
- routes: int32 [32768, 8], P('dp'), may hold values from 0 to 31, all different within a row; in each aligned block of 2048 rows (0 to 2047, 2048 to 4095, ...) at most 768 rows name the same one
- norm1_gain: bfloat16 [1024], P('dp'), may hold values from 0.5 to 1.5
- w_query: bfloat16 [1024, 1024], P('dp', 'tensor'), may hold values from -0.1875 to 0.1875
- key_projection: bfloat16 [1024, 512], P('dp', 'tensor'), may hold values from -0.1875 to 0.1875
- value_projection: bfloat16 [1024, 512], P('dp', 'tensor'), may hold values from -0.1875 to 0.1875
- w_out: bfloat16 [1024, 1024], P('tensor', 'dp'), may hold values from -0.75 to 0.75
- norm2_gain: bfloat16 [1024], P('dp'), may hold values from 0.5 to 1.5
- w_router: bfloat16 [1024, 32], P('dp'), may hold values from -0.09375 to 0.09375
- w_gate: bfloat16 [32, 1024, 512], P('tensor', 'dp'), may hold values from -0.1875 to 0.1875
- w_up: bfloat16 [32, 1024, 512], P('tensor', 'dp'), may hold values from -0.1875 to 0.1875
- w_down: bfloat16 [32, 512, 1024], P('tensor', 'dp'), may hold values from -1 to 1
- cotangent: bfloat16 [32768, 1024], P(('dp', 'tensor')), may hold values from -6 to 6
Outputs:
- output: bfloat16 [32768, 1024], P(('dp', 'tensor'))
- grad_tokens: bfloat16 [32768, 1024], P(('dp', 'tensor'))
- grad_norm1: float32 [1024], P('dp')
- grad_query: float32 [1024, 1024], P('dp', 'tensor')
- grad_key: float32 [1024, 512], P('dp', 'tensor')
- grad_value: float32 [1024, 512], P('dp', 'tensor')
- grad_out: float32 [1024, 1024], P('tensor', 'dp')
- grad_norm2: float32 [1024], P('dp')
- grad_router: float32 [1024, 32], P('dp')
- grad_gate: float32 [32, 1024, 512], P('tensor', 'dp')
- grad_up: float32 [32, 1024, 512], P('tensor', 'dp')
- grad_down: float32 [32, 512, 1024], P('tensor', 'dp')
Inputs may be any that keep to these rules, and one draw needn't show every extreme that they name: `routes`: in each group of 2048 rows no expert is named by more than 768 rows, a bound that some block reaches; a row names 8 different experts. `lengths`: each row sums to 2048; its largest entry is exactly 1024.
All inputs are finite; a program needn't handle non-finite values.
Results may differ from a plain program's by a relative error of at most 0.023.
Values may be sent and summed in bfloat16 or wider, within the bound.
No kernel may reach another device: no remote copies, remote signals or barrier semaphores. Data moves between devices by JAX's collectives and lax.ppermute only.
A program may use at most 448 MiB of HBM per device.

v0:
```python
import jax
import jax.numpy as jnp
from jax import lax
from jax.sharding import PartitionSpec as P

QUERY_HEADS = 16
KEY_VALUE_HEADS = 8
HEAD_SIZE = 64
EXPERTS = 32
MAXLEN = 1024
QUERY_BLOCK_ROWS = 512
CAP = 768


exact_mode = lax.Precision.HIGHEST
masked_score = -1000000000.0


def rms_norm(values, gain):
    inverse = lax.rsqrt(jnp.mean(values * values, axis=-1, keepdims=True) + 1e-06)
    return (values * inverse * gain, inverse)


def rms_back(grad_rows, values, inverse, gain):
    scaled = grad_rows * gain
    gain_grad = jnp.sum(grad_rows * values * inverse, axis=0)
    inner = jnp.mean(scaled * values, axis=-1, keepdims=True)
    return (inverse * scaled - values * inverse * inverse * inverse * inner, gain_grad)


def seq_layout(seq_lengths, overall_rows):
    ends = jnp.cumsum(seq_lengths)
    row_index = jnp.arange(overall_rows, dtype=jnp.int32)
    segment = jnp.sum((row_index[:, None] >= ends[None, :]).astype(jnp.int32), axis=1)
    starts = ends - seq_lengths
    which = segment[:, None] == jnp.arange(seq_lengths.shape[0], dtype=jnp.int32)[None, :]
    first_row = jnp.sum(jnp.where(which, starts[None, :], 0), axis=1)
    return (segment, row_index - first_row)


def rope_tables(position):
    half_width = HEAD_SIZE // 2
    frequency = 10000.0 ** (-2.0 * jnp.arange(half_width, dtype=jnp.float32) / HEAD_SIZE)
    angles = position.astype(jnp.float32)[:, None] * frequency[None, :]
    return (jnp.cos(angles)[:, None, :], jnp.sin(angles)[:, None, :])


def apply_rotary(values, cosine_table, sine_table):
    half_width = values.shape[-1] // 2
    first_half = values[..., :half_width]
    second_half = values[..., half_width:]
    return jnp.concatenate(
        [
            first_half * cosine_table - second_half * sine_table,
            second_half * cosine_table + first_half * sine_table,
        ],
        axis=-1,
    )


def block_scores(query_tile, key_block, query_first_row, key_start, segment):
    block_rows = query_tile.shape[0]
    key_window = key_block.shape[0]
    scores = jnp.einsum(
        "qhgd,khd->hgqk", query_tile, key_block, preferred_element_type=jnp.float32
    ) * HEAD_SIZE ** (-0.5)
    query_seg = lax.dynamic_slice_in_dim(segment, query_first_row, block_rows, 0)
    key_seg = lax.dynamic_slice_in_dim(segment, key_start, key_window, 0)
    query_index = query_first_row + jnp.arange(block_rows, dtype=jnp.int32)
    key_index = key_start + jnp.arange(key_window, dtype=jnp.int32)
    allowed = (query_seg[:, None] == key_seg[None, :]) & (
        key_index[None, :] <= query_index[:, None]
    )
    return jnp.where(allowed, scores, masked_score)


def shards(
    tokens,
    lengths,
    routes,
    norm1_gain,
    w_query,
    key_projection,
    value_projection,
    w_out,
    norm2_gain,
    w_router,
    w_gate,
    w_up,
    w_down,
    cotangent,
):
    tensor_parallel_count = lax.axis_size("tensor")
    tensor_rank = lax.axis_index("tensor")
    local_rows = tokens.shape[0]
    group_rows = local_rows * tensor_parallel_count
    query_heads = QUERY_HEADS // tensor_parallel_count
    key_value_heads = KEY_VALUE_HEADS // tensor_parallel_count
    ratio_heads = query_heads // key_value_heads
    key_window = QUERY_BLOCK_ROWS + MAXLEN
    block_count = group_rows // QUERY_BLOCK_ROWS
    score_scale = HEAD_SIZE ** (-0.5)
    query_weight, key_matrix, value_matrix, out_weight, router_weight, gain_one, gain_two = (
        lax.all_gather(w_query, "dp", axis=0, tiled=True),
        lax.all_gather(key_projection, "dp", axis=0, tiled=True),
        lax.all_gather(value_projection, "dp", axis=0, tiled=True),
        lax.all_gather(w_out, "dp", axis=1, tiled=True),
        lax.all_gather(w_router, "dp", axis=0, tiled=True),
        lax.all_gather(norm1_gain, "dp", axis=0, tiled=True),
        lax.all_gather(norm2_gain, "dp", axis=0, tiled=True),
    )
    gain_one = gain_one.astype(jnp.float32)
    gain_two = gain_two.astype(jnp.float32)
    segment, position = seq_layout(lengths[0], group_rows)
    cosine_table, sine_table = rope_tables(position)
    inputs_f = tokens.astype(jnp.float32)
    normed_one, inverse_one = rms_norm(inputs_f, gain_one)
    first_hidden = lax.all_gather(normed_one.astype(jnp.bfloat16), "tensor", axis=0, tiled=True)
    query_lin = jnp.dot(first_hidden, query_weight, preferred_element_type=jnp.float32).reshape(
        group_rows, query_heads, HEAD_SIZE
    )
    key_lin = jnp.dot(first_hidden, key_matrix, preferred_element_type=jnp.float32).reshape(
        group_rows, key_value_heads, HEAD_SIZE
    )
    query_matrix = apply_rotary(query_lin, cosine_table, sine_table).astype(jnp.bfloat16)
    rotated_keys = apply_rotary(key_lin, cosine_table, sine_table).astype(jnp.bfloat16)
    value_vectors = (
        jnp.dot(first_hidden, value_matrix, preferred_element_type=jnp.float32)
        .astype(jnp.bfloat16)
        .reshape(group_rows, key_value_heads, HEAD_SIZE)
    )

    def block_inputs(block_id):
        query_first_row = block_id * QUERY_BLOCK_ROWS
        key_start = jnp.clip(query_first_row - MAXLEN, 0, group_rows - key_window).astype(jnp.int32)
        query_tile = lax.dynamic_slice_in_dim(
            query_matrix, query_first_row, QUERY_BLOCK_ROWS, 0
        ).reshape(QUERY_BLOCK_ROWS, key_value_heads, ratio_heads, HEAD_SIZE)
        key_block = lax.dynamic_slice_in_dim(rotated_keys, key_start, key_window, 0)
        value_block = lax.dynamic_slice_in_dim(value_vectors, key_start, key_window, 0)
        scores = block_scores(query_tile, key_block, query_first_row, key_start, segment)
        return (query_first_row, key_start, query_tile, key_block, value_block, scores)

    def attend_block(block_id):
        query_first_row, key_start, query_tile, key_block, value_block, scores = block_inputs(
            block_id
        )
        peak = jnp.max(scores, axis=-1, keepdims=True)
        weights_raw = jnp.exp(scores - peak)
        weight_total = jnp.sum(weights_raw, axis=-1, keepdims=True)
        probs = (weights_raw / weight_total).astype(jnp.bfloat16)
        mixed = jnp.einsum("hgqk,khd->qhgd", probs, value_block, preferred_element_type=jnp.float32)
        return (
            mixed.reshape(QUERY_BLOCK_ROWS, query_heads * HEAD_SIZE).astype(jnp.bfloat16),
            (peak + jnp.log(weight_total))[..., 0],
        )

    attended, log_total = lax.map(attend_block, jnp.arange(block_count, dtype=jnp.int32))
    attended = attended.reshape(group_rows, query_heads * HEAD_SIZE)
    residual_two = inputs_f + lax.psum_scatter(
        jnp.dot(attended, out_weight, preferred_element_type=jnp.float32).astype(jnp.bfloat16),
        "tensor",
        scatter_dimension=0,
        tiled=True,
    ).astype(jnp.float32)
    normed_two, inverse_two = rms_norm(residual_two, gain_two)
    hidden_rows = normed_two.astype(jnp.bfloat16)
    logits = jnp.dot(hidden_rows, router_weight, preferred_element_type=jnp.float32)
    local_routes = lax.dynamic_slice_in_dim(routes, tensor_rank * local_rows, local_rows, 0)
    pick_table = (
        local_routes[:, :, None] == jnp.arange(EXPERTS, dtype=jnp.int32)[None, None, :]
    ).astype(jnp.float32)
    chosen = jnp.sum(pick_table * logits[:, None, :], axis=-1)
    gates_f = jax.nn.softmax(chosen, axis=-1)
    hidden_two, gates_all, grad_all = (
        lax.all_gather(hidden_rows, "tensor", axis=0, tiled=True),
        lax.all_gather(gates_f.astype(jnp.bfloat16), "tensor", axis=0, tiled=True),
        lax.all_gather(cotangent, "tensor", axis=0, tiled=True),
    )
    gate_weight, up_weight, down_weight = (
        lax.all_gather(w_gate, "dp", axis=1, tiled=True),
        lax.all_gather(w_up, "dp", axis=1, tiled=True),
        lax.all_gather(w_down, "dp", axis=1, tiled=True),
    )
    expert_local = gate_weight.shape[0]
    expert_names = tensor_rank * expert_local + jnp.arange(expert_local, dtype=jnp.int32)
    match = routes[:, :, None] == expert_names[None, None, :]
    member = jnp.any(match, axis=1)
    share = jnp.sum(jnp.where(match, gates_all.astype(jnp.float32)[:, :, None], 0.0), axis=1)
    slot = jnp.cumsum(member.astype(jnp.int32), axis=0) - 1
    slot = jnp.where(member, slot, CAP)
    row_index = jnp.broadcast_to(
        jnp.arange(group_rows, dtype=jnp.int32)[:, None], (group_rows, expert_local)
    )
    expert_index = jnp.broadcast_to(
        jnp.arange(expert_local, dtype=jnp.int32)[None, :], (group_rows, expert_local)
    )
    table = (
        jnp.zeros((expert_local, CAP), jnp.int32).at[expert_index, slot].set(row_index, mode="drop")
    )
    filled = jnp.sum(member.astype(jnp.int32), axis=0)
    valid = jnp.arange(CAP, dtype=jnp.int32)[None, :] < filled[:, None]
    slot_gate = jnp.where(valid, jnp.take_along_axis(share.T, table, axis=1), 0.0)
    flat_table = table.reshape(-1)
    picked = hidden_two[table]
    gate_lin = jnp.einsum("ecd,edf->ecf", picked, gate_weight, preferred_element_type=jnp.float32)
    up_lin = jnp.einsum("ecd,edf->ecf", picked, up_weight, preferred_element_type=jnp.float32)
    silu_gate = jax.nn.silu(gate_lin)
    hidden = (silu_gate * up_lin).astype(jnp.bfloat16)
    expert_out = jnp.einsum("ecf,efd->ecd", hidden, down_weight, preferred_element_type=jnp.float32)
    weighted = (slot_gate[:, :, None] * expert_out).reshape(-1, expert_out.shape[2])
    moe_part = (
        jnp.zeros((group_rows, expert_out.shape[2]), jnp.float32).at[flat_table].add(weighted)
    )
    moe_rows = lax.psum_scatter(
        moe_part.astype(jnp.bfloat16), "tensor", scatter_dimension=0, tiled=True
    ).astype(jnp.float32)
    output = (residual_two + moe_rows).astype(jnp.bfloat16)
    grad_slots = grad_all[table].astype(jnp.float32)
    d_expert = (slot_gate[:, :, None] * grad_slots).astype(jnp.bfloat16)
    d_slot_gate = jnp.where(valid, jnp.sum(expert_out * grad_slots, axis=-1), 0.0)
    grad_down = jnp.einsum("ecf,ecd->efd", hidden, d_expert, preferred_element_type=jnp.float32)
    d_hidden = jnp.einsum("ecd,efd->ecf", d_expert, down_weight, preferred_element_type=jnp.float32)
    sigmoid_gate = jax.nn.sigmoid(gate_lin)
    d_gate_lin = (
        d_hidden * up_lin * sigmoid_gate * (1.0 + gate_lin * (1.0 - sigmoid_gate))
    ).astype(jnp.bfloat16)
    d_up_lin = (d_hidden * silu_gate).astype(jnp.bfloat16)
    grad_gate = jnp.einsum("ecd,ecf->edf", picked, d_gate_lin, preferred_element_type=jnp.float32)
    grad_up = jnp.einsum("ecd,ecf->edf", picked, d_up_lin, preferred_element_type=jnp.float32)
    d_picked = jnp.einsum(
        "ecf,edf->ecd", d_gate_lin, gate_weight, preferred_element_type=jnp.float32
    )
    d_picked = d_picked + jnp.einsum(
        "ecf,edf->ecd", d_up_lin, up_weight, preferred_element_type=jnp.float32
    )
    d_hidden_two = (
        jnp.zeros((group_rows, d_picked.shape[2]), jnp.float32)
        .at[flat_table]
        .add(d_picked.reshape(-1, d_picked.shape[2]))
    )
    d_share = (
        jnp.zeros((group_rows, expert_local), jnp.float32)
        .at[table, jnp.arange(expert_local, dtype=jnp.int32)[:, None]]
        .add(d_slot_gate)
    )
    d_gates_part = jnp.sum(jnp.where(match, d_share[:, None, :], 0.0), axis=-1)
    d_hidden_rows, d_gates = (
        lax.psum_scatter(
            d_hidden_two.astype(jnp.bfloat16), "tensor", scatter_dimension=0, tiled=True
        ).astype(jnp.float32),
        lax.psum_scatter(
            d_gates_part.astype(jnp.bfloat16), "tensor", scatter_dimension=0, tiled=True
        ).astype(jnp.float32),
    )
    d_chosen = gates_f * (d_gates - jnp.sum(d_gates * gates_f, axis=-1, keepdims=True))
    d_logits = jnp.sum(pick_table * d_chosen[:, :, None], axis=1)
    router_grad = jnp.dot(hidden_rows.astype(jnp.float32).T, d_logits, precision=exact_mode)
    d_hidden_rows = d_hidden_rows + jnp.dot(
        d_logits, router_weight.astype(jnp.float32).T, precision=exact_mode
    )
    d_norm_two, gain_two_grad = rms_back(d_hidden_rows, residual_two, inverse_two, gain_two)
    d_residual = cotangent.astype(jnp.float32) + d_norm_two
    d_attn_out = lax.all_gather(d_residual.astype(jnp.bfloat16), "tensor", axis=0, tiled=True)
    grad_out = jnp.einsum("gi,gd->id", attended, d_attn_out, preferred_element_type=jnp.float32)
    d_attended = jnp.einsum(
        "gd,id->gi", d_attn_out, out_weight, preferred_element_type=jnp.float32
    ).astype(jnp.bfloat16)
    d_attended = d_attended.reshape(group_rows, key_value_heads, ratio_heads, HEAD_SIZE)

    def back_block(block_id, carry):
        d_query, d_key, d_value = carry
        query_first_row, key_start, query_tile, key_block, value_block, scores = block_inputs(
            block_id
        )
        probs_f = jnp.exp(scores - log_total[block_id][..., None])
        probs = probs_f.astype(jnp.bfloat16)
        grad_block = lax.dynamic_slice_in_dim(d_attended, query_first_row, QUERY_BLOCK_ROWS, 0)
        d_probs = jnp.einsum(
            "qhgd,khd->hgqk", grad_block, value_block, preferred_element_type=jnp.float32
        )
        inner = jnp.sum(probs_f * d_probs, axis=-1, keepdims=True)
        d_scores = (probs_f * (d_probs - inner)).astype(jnp.bfloat16)
        query_part = (
            jnp.einsum("hgqk,khd->qhgd", d_scores, key_block, preferred_element_type=jnp.float32)
            * score_scale
        )
        key_part = (
            jnp.einsum("hgqk,qhgd->khd", d_scores, query_tile, preferred_element_type=jnp.float32)
            * score_scale
        )
        value_part = jnp.einsum(
            "hgqk,qhgd->khd", probs, grad_block, preferred_element_type=jnp.float32
        )
        d_query = lax.dynamic_update_slice_in_dim(
            d_query,
            query_part.reshape(QUERY_BLOCK_ROWS, query_heads, HEAD_SIZE),
            query_first_row,
            0,
        )
        d_key = lax.dynamic_update_slice_in_dim(
            d_key,
            lax.dynamic_slice_in_dim(d_key, key_start, key_window, 0) + key_part,
            key_start,
            0,
        )
        d_value = lax.dynamic_update_slice_in_dim(
            d_value,
            lax.dynamic_slice_in_dim(d_value, key_start, key_window, 0) + value_part,
            key_start,
            0,
        )
        return (d_query, d_key, d_value)

    start_carry = (
        jnp.zeros((group_rows, query_heads, HEAD_SIZE), jnp.float32),
        jnp.zeros((group_rows, key_value_heads, HEAD_SIZE), jnp.float32),
        jnp.zeros((group_rows, key_value_heads, HEAD_SIZE), jnp.float32),
    )
    d_query, d_key, d_value = lax.fori_loop(0, block_count, back_block, start_carry)
    d_query_lin = (
        apply_rotary(d_query, cosine_table, -sine_table)
        .astype(jnp.bfloat16)
        .reshape(group_rows, query_heads * HEAD_SIZE)
    )
    d_key_lin = (
        apply_rotary(d_key, cosine_table, -sine_table)
        .astype(jnp.bfloat16)
        .reshape(group_rows, key_value_heads * HEAD_SIZE)
    )
    d_value_lin = d_value.astype(jnp.bfloat16).reshape(group_rows, key_value_heads * HEAD_SIZE)
    grad_query = jnp.einsum(
        "gd,gi->di", first_hidden, d_query_lin, preferred_element_type=jnp.float32
    )
    grad_key = jnp.einsum("gd,gi->di", first_hidden, d_key_lin, preferred_element_type=jnp.float32)
    grad_value = jnp.einsum(
        "gd,gi->di", first_hidden, d_value_lin, preferred_element_type=jnp.float32
    )
    total_term = jnp.einsum(
        "gi,di->gd", d_query_lin, query_weight, preferred_element_type=jnp.float32
    )
    total_term = total_term + jnp.einsum(
        "gi,di->gd", d_key_lin, key_matrix, preferred_element_type=jnp.float32
    )
    d_hidden_one = lax.psum_scatter(
        (
            total_term
            + jnp.einsum("gi,di->gd", d_value_lin, value_matrix, preferred_element_type=jnp.float32)
        ).astype(jnp.bfloat16),
        "tensor",
        scatter_dimension=0,
        tiled=True,
    ).astype(jnp.float32)
    d_norm_one, gain_one_grad = rms_back(d_hidden_one, inputs_f, inverse_one, gain_one)
    grad_tokens = (d_residual + d_norm_one).astype(jnp.bfloat16)
    grad_query, grad_key, grad_value, grad_out, grad_gate, grad_up, grad_down = (
        lax.psum_scatter(
            grad_query.astype(jnp.bfloat16), "dp", scatter_dimension=0, tiled=True
        ).astype(jnp.float32),
        lax.psum_scatter(
            grad_key.astype(jnp.bfloat16), "dp", scatter_dimension=0, tiled=True
        ).astype(jnp.float32),
        lax.psum_scatter(
            grad_value.astype(jnp.bfloat16), "dp", scatter_dimension=0, tiled=True
        ).astype(jnp.float32),
        lax.psum_scatter(
            grad_out.astype(jnp.bfloat16), "dp", scatter_dimension=1, tiled=True
        ).astype(jnp.float32),
        lax.psum_scatter(
            grad_gate.astype(jnp.bfloat16), "dp", scatter_dimension=1, tiled=True
        ).astype(jnp.float32),
        lax.psum_scatter(
            grad_up.astype(jnp.bfloat16), "dp", scatter_dimension=1, tiled=True
        ).astype(jnp.float32),
        lax.psum_scatter(
            grad_down.astype(jnp.bfloat16), "dp", scatter_dimension=1, tiled=True
        ).astype(jnp.float32),
    )
    norm_one_sum, norm_two_sum, router_sum = lax.psum(
        (gain_one_grad, gain_two_grad, router_grad), ("dp", "tensor")
    )
    shard_rows = norm1_gain.shape[0]
    offset = lax.axis_index("dp") * shard_rows
    grad_norm1 = lax.dynamic_slice_in_dim(norm_one_sum, offset, shard_rows, 0)
    grad_norm2 = lax.dynamic_slice_in_dim(norm_two_sum, offset, shard_rows, 0)
    grad_router = lax.dynamic_slice_in_dim(router_sum, offset, shard_rows, 0)
    return (
        output,
        grad_tokens,
        grad_norm1,
        grad_query,
        grad_key,
        grad_value,
        grad_out,
        grad_norm2,
        grad_router,
        grad_gate,
        grad_up,
        grad_down,
    )


def solution(mesh):
    return jax.shard_map(
        shards,
        mesh=mesh,
        in_specs=(
            P(("dp", "tensor"), None),
            P("dp", None),
            P("dp", None),
            P("dp"),
            P("dp", "tensor"),
            P("dp", "tensor"),
            P("dp", "tensor"),
            P("tensor", "dp"),
            P("dp"),
            P("dp", None),
            P("tensor", "dp", None),
            P("tensor", "dp", None),
            P("tensor", "dp", None),
            P(("dp", "tensor"), None),
        ),
        out_specs=(
            P(("dp", "tensor"), None),
            P(("dp", "tensor"), None),
            P("dp"),
            P("dp", "tensor"),
            P("dp", "tensor"),
            P("dp", "tensor"),
            P("tensor", "dp"),
            P("dp"),
            P("dp", None),
            P("tensor", "dp", None),
            P("tensor", "dp", None),
            P("tensor", "dp", None),
        ),
        check_vma=False,
    )
```

profile of v0, /device:TPU:0, one launch (start us, length us, event | category | flops | bytes accessed | tf_op | source)
XLA Modules:
  0.0 2712.9 jit_solution(16780217127686965952)
XLA Ops:
  11.6 35.7 %all-reduce.3 = (bf16[1024]{0:T(1024)(128)(2,1)S(1)}, bf16[1024]{0:T(1024)(128)(2,1)}) all-reduce(bf16[1024]{0:T(1024)(128)(2,1)S(1)} %dynamic-update-slice, bf16[1024]{0:T(1024)(128)(2,1)S(1)} %dynamic-update-slice.1), channel_id=1, replica_groups=mesh['dp'=16,'tensor'=2] {'dp'}, use_global_device_ids=true, to_apply=%add | all-reduce | flops 2048 | bytes 8192
  54.8 18.7 all_gather.48
  73.5 21.0 all_gather.47
  122.5 169.3 %while.33 = (s32[]{:T(128)}, bf16[4,512,512]{2,1,0:T(8,128)(2,1)}, f32[4,4,2,512]{3,2,1,0:T(2,128)}, s32[4]{0:T(128)S(1)}, bf16[2048,4,64]{0,2,1:T(8,128)(2,1)},...) while((s32[]{:T(128)}, bf16[4,512,512]{2,1,0:T(8,128)(2,1)}, ...), condition=%wide.region_7.8_spmd, body=%wide.region_4.7_spmd.sunk | while | flops 1663563776 | bytes 83010808 | solution.py:158
  137.4 13.3 fusion.165
  177.0 13.3 fusion.165
  216.4 13.3 fusion.165
  256.0 13.3 fusion.165
  299.3 53.8 %reduce-scatter.13.cloned.1.call-done = bf16[1024,1024]{1,0:T(8,128)(2,1)} async-done(((bf16[2048,1024]{1,0:T(8,128)(2,1)}), bf16[1024,1024]{1,0:T(8,128)(2,1)}) %reduce-scatter.13.cloned.1.call-update) | async-done | bytes 2097168 | tf_op jit(solution)/shard_map/reduce_scatter | solution.py:160
  360.6 21.7 all-gather
  390.0 120.1 %scatter_custom_fusion.2 = s32[12288]{0:T(1024)S(1)} fusion(s32[32768]{0:T(1024)S(1)} %reshape.423, s32[32768]{0:T(1024)S(1)} %reshape.425, s32[]{:T(128)} %constant.217.clone.1), kind=kCustom, calls=%fused_computation.173 | custom fusion | bytes 49156
  512.4 63.5 %gather_fusion.1 = bf16[12288,1024]{1,0:T(8,128)(2,1)} fusion(bf16[2048,1024]{1,0:T(8,128)(2,1)} %all-gather.25.cloned.1.call-done, s32[12288]{0:T(1024)S(1)} %broadcast_clamp_fusion), kind=kCustom, calls=%fused_computation.1 | custom fusion | bytes 50380800 | tf_op jit(solution)/shard_map/gather | solution.py:219
  583.1 63.6 %gather_fusion = bf16[12288,1024]{1,0:T(8,128)(2,1)} fusion(bf16[2048,1024]{1,0:T(8,128)(2,1)} %all-gather.17.cloned.1.call-done, s32[12288]{0:T(1024)S(1)} %broadcast_clamp_fusion), kind=kCustom, calls=%fused_computation | custom fusion | bytes 50380800 | tf_op jit(solution)/shard_map/gather | solution.py:205
  646.7 31.3 %fusion.87 = f32[16,768,512]{2,1,0:T(8,128)} fusion(bf16[16,768,1024]{2,1,0:T(8,128)(2,1)} %bitcast.234, bf16[16,1024,512]{2,1,0:T(8,128)(2,1)} %all-gather.19.cloned.1.call-done), kind=kOutput, calls=%fused_computation.194 | convolution fusion | flops 12884901888 | bytes 67108864 | tf_op jit(solution)/shard_map/ecd,edf->ecf/dot_general | solution.py:206
  678.0 49.0 %all-gather.21.cloned.1.call-done = bf16[16,1024,512]{2,1,0:T(8,128)(2,1)} async-done(((bf16[16,64,512]{2,1,0:T(8,128)(2,1)}), bf16[16,1024,512]{2,1,0:T(8,128)(2,1)}) %all-gather.21.cloned.1.call-update) | async-done | bytes 16777232 | tf_op jit(solution)/shard_map/all_gather | solution.py:182
  727.0 35.4 %multiply_convert_fusion.2 = (bf16[16,768,512]{2,1,0:T(8,128)(2,1)}, f32[16,768,512]{2,1,0:T(8,128)}) fusion(f32[16,768,512]{2,1,0:T(8,128)} %fusion.87, bf16[16,768,1024]{2,1,0:T(8,128)(2,1)} %bitcast.235, bf16[16,1024,512]{2,1,0:T(8,128)(2,1)} %all-gather.21.cloned.1.call-done), kind=kOutput, calls=%fused_computation.67 | convolution fusion | flops 12922650624 | bytes 104857600 | tf_op jit(solution)/shard_map/ecd,edf->ecf/dot_general | solution.py:207
  762.4 92.1 %all-gather.23.cloned.1.call-done = bf16[16,512,1024]{2,1,0:T(8,128)(2,1)} async-done(((bf16[16,32,1024]{2,1,0:T(8,128)(2,1)}), bf16[16,512,1024]{2,1,0:T(8,128)(2,1)}) %all-gather.23.cloned.1.call-update) | async-done | bytes 16777232 | tf_op jit(solution)/shard_map/all_gather | solution.py:183
  854.6 33.8 %fusion.39 = (f32[16,768]{1,0:T(8,128)S(1)}, f32[16,768,1024]{2,1,0:T(8,128)}) fusion(bf16[16,768,1024]{2,1,0:T(8,128)(2,1)} %bitcast.229, bf16[16,768,512]{2,1,0:T(8,128)(2,1)} %get-tuple-element.432, bf16[16,512,1024]{2,1,0:T(8,128)(2,1)} %all-gather.23.cloned.1.call-done), kind=kOutput, calls=%fused_computation.64 | convolution fusion | flops 12922638336 | bytes 104906752 | tf_op jit(solution)/shard_map/ecf,efd->ecd/dot_general | solution.py:210
  888.5 85.4 %scatter_custom_fusion.3 = f32[32768]{0:T(1024)S(1)} fusion(s32[12288]{0:T(1024)} %reshape.429, f32[12288]{0:T(1024)S(1)} %reshape.431, f32[]{:T(128)} %constant.219.clone.1), kind=kCustom, calls=%fused_computation.158 | custom fusion | flops 12288 | bytes 131584
  975.2 81.9 %gather_fusion.2 = f32[12288]{0:T(1024)S(1)} fusion(f32[16,2048]{0,1:T(8,128)S(1)} %bitcast.225, s32[12288]{0:T(1024)S(1)} %copy-done), kind=kCustom, calls=%fused_computation.2 | custom fusion | bytes 196608 | tf_op jit(solution)/shard_map/jit(take_along_axis)/gather | solution.py:203
  1057.3 42.3 %multiply_convert_fusion = (bf16[16,768,512]{2,1,0:T(8,128)(2,1)}, bf16[16,768,512]{2,1,0:T(8,128)(2,1)}) fusion(f32[16,768,512]{2,1,0:T(8,128)} %fusion.87, f32[16,768,512]{2,1,0:T(8,128)} %get-tuple-element.433, bf16[16,512,1024]{2,1,0:T(8,128)(2,1)} %all-gather.23.cloned.1.call-done, bf16[16,768,1024]{2,1,0:T(8,128)(2,1)} %bitcast.230, ...), kind=kOutput, calls=%fused_computation.65 | convolution fusion | flops 13004439552 | bytes 117489664 | tf_op jit(solution)/shard_map/ecd,efd->ecf/dot_general | solution.py:223
  1099.6 30.6 %fusion.88 = f32[16,768,1024]{2,1,0:T(8,128)} fusion(bf16[16,768,512]{2,1,0:T(8,128)(2,1)} %get-tuple-element.414, bf16[16,1024,512]{2,1,0:T(8,128)(2,1)} %all-gather.19.cloned.1.call-done), kind=kOutput, calls=%fused_computation.195 | convolution fusion | flops 12884901888 | bytes 79691776 | tf_op jit(solution)/shard_map/ecf,edf->ecd/dot_general | solution.py:231
  1130.2 48.6 %convolution_add_fusion = f32[16,768,1024]{2,1,0:T(8,128)} fusion(f32[16,768,1024]{2,1,0:T(8,128)} %fusion.88, bf16[16,768,512]{2,1,0:T(8,128)(2,1)} %get-tuple-element.413, bf16[16,1024,512]{2,1,0:T(8,128)(2,1)} %all-gather.21.cloned.1.call-done), kind=kOutput, calls=%fused_computation.73 | convolution fusion | flops 12897484800 | bytes 130023424 | tf_op jit(solution)/shard_map/ecf,edf->ecd/dot_general | solution.py:234
  1178.8 109.7 %scatter_custom_fusion.1 = f32[2048,1024]{1,0:T(8,128)} fusion(s32[12288]{0:T(1024)} %bitcast.252, f32[12288,1024]{1,0:T(8,128)} %bitcast.233, f32[]{:T(128)} %constant.219.clone.1), kind=kCustom, calls=%fused_computation.104 | custom fusion | flops 12582912 | bytes 8389120 | tf_op jit(solution)/shard_map/scatter-add | solution.py:240
  1296.9 50.3 %reduce-scatter.17.cloned.1.call-done = bf16[1024,1024]{1,0:T(8,128)(2,1)} async-done(((bf16[2048,1024]{1,0:T(8,128)(2,1)}), bf16[1024,1024]{1,0:T(8,128)(2,1)}) %reduce-scatter.17.cloned.1.call-update) | async-done | bytes 2097168 | tf_op jit(solution)/shard_map/reduce_scatter | solution.py:249
  1362.1 53.3 %all-gather.27.cloned.1.call-done = bf16[2048,1024]{1,0:T(8,128)(2,1)} async-done(((bf16[1024,1024]{1,0:T(8,128)(2,1)}), bf16[2048,1024]{1,0:T(8,128)(2,1)}) %all-gather.27.cloned.1.call-update) | async-done | bytes 4194320 | tf_op jit(solution)/shard_map/all_gather | solution.py:264
  1427.0 375.6 %while.34 = (s32[]{:T(128)}, f32[2048,8,64]{0,2,1:T(8,128)}, f32[2048,4,64]{0,2,1:T(8,128)}, f32[2048,4,64]{0,2,1:T(8,128)}, bf16[2048,4,64]{0,2,1:T(8,128)(2,1)...) while((s32[]{:T(128)}, f32[2048,8,64]{0,2,1:T(8,128)}, ...), condition=%wide.region_32.33_spmd, body=%wide.region_30.32_spmd.sunk | while | flops 4086953984 | bytes 213770544 | solution.py:320
  1428.4 13.2 fusion.177
  1443.5 18.8 fusion.178
  1462.4 16.9 fusion.179
  1537.7 18.7 fusion.178
  1556.5 16.8 fusion.179
  1631.8 18.7 fusion.178
  1650.5 16.8 fusion.179
  1710.8 13.2 fusion.177
  1725.9 18.7 fusion.178
  1744.6 16.8 fusion.179
  1836.0 32.8 %broadcast_multiply_fusion = f32[16,768,1024]{2,1,0:T(8,128)} fusion(f32[16,768,1024]{2,1,0:T(8,128)} %get-tuple-element.435, f32[16,768]{1,0:T(8,128)S(1)} %copy-done.38), kind=kLoop, calls=%fused_computation.70 | loop fusion | flops 12582912 | bytes 100712448 | tf_op jit(solution)/shard_map/mul | solution.py:211
  1868.8 109.3 %scatter_custom_fusion = f32[2048,1024]{1,0:T(8,128)} fusion(s32[12288]{0:T(1024)} %bitcast.253, f32[12288,1024]{1,0:T(8,128)} %bitcast.232, f32[]{:T(128)} %constant.219.clone.1), kind=kCustom, calls=%fused_computation.106 | custom fusion | flops 12582912 | bytes 8389120 | tf_op jit(solution)/shard_map/scatter-add | solution.py:213
  1984.4 23.5 fusion.45
  2008.0 23.4 convolution_convert_fusion.1
  2031.7 23.3 convolution_convert_fusion
  2062.4 37.0 %reduce-scatter.21.cloned.1.call-done = bf16[1024,1024]{1,0:T(8,128)(2,1)} async-done(((bf16[2048,1024]{1,0:T(8,128)(2,1)}), bf16[1024,1024]{1,0:T(8,128)(2,1)}) %reduce-scatter.21.cloned.1.call-update) | async-done | bytes 2097168 | tf_op jit(solution)/shard_map/reduce_scatter | solution.py:345
  2102.7 40.0 %all-reduce.2 = (f32[1024]{0:T(1024)S(1)}, f32[1024]{0:T(1024)S(1)}) all-reduce(f32[1024]{0:T(1024)S(1)} %get-tuple-element.365, f32[1024]{0:T(1024)S(1)} %copy-done.59), channel_id=1, replica_groups=mesh['dp'=16,'tensor'=2] {'dp','tensor'}, use_global_device_ids=true, to_apply=%region_36.37 | all-reduce | flops 2048 | bytes 16384 | tf_op jit(solution)/shard_map/psum | solution.py:379
  2143.8 13.5 reduce-scatter.15.cloned.1.call-done
  2165.4 174.3 %reduce-scatter.35.cloned.1.call-done = bf16[16,32,1024]{2,1,0:T(8,128)(2,1)} async-done(((bf16[16,512,1024]{2,1,0:T(8,128)(2,1)}), bf16[16,32,1024]{2,1,0:T(8,128)(2,1)}) %reduce-scatter.35.cloned.1.call-update) | async-done | bytes 1048592 | tf_op jit(solution)/shard_map/reduce_scatter | solution.py:375
  2342.5 178.9 %reduce-scatter.31.cloned.1.call-done = bf16[16,64,512]{2,1,0:T(8,128)(2,1)} async-done(((bf16[16,1024,512]{2,1,0:T(8,128)(2,1)}), bf16[16,64,512]{2,1,0:T(8,128)(2,1)}) %reduce-scatter.31.cloned.1.call-update) | async-done | bytes 1048592 | tf_op jit(solution)/shard_map/reduce_scatter | solution.py:369
  2524.2 178.8 %reduce-scatter.33.cloned.1.call-done = bf16[16,64,512]{2,1,0:T(8,128)(2,1)} async-done(((bf16[16,1024,512]{2,1,0:T(8,128)(2,1)}), bf16[16,64,512]{2,1,0:T(8,128)(2,1)}) %reduce-scatter.33.cloned.1.call-update) | async-done | bytes 1048592 | tf_op jit(solution)/shard_map/reduce_scatter | solution.py:372
  (429 shorter events, 483.5 us)
Async XLA Ops:
  7.2 89.1 %all-gather.13.cloned.1.call-start = ((), (), s32[]{:S(2)}) async-start(), calls=%async_computation.13 | async-start | bytes 1114112 | tf_op jit(solution)/shard_map/all_gather | solution.py:104
  7.9 100.8 %all-gather.11.cloned.1.call-start = ((), (), s32[]{:S(2)}) async-start(), calls=%async_computation.12 | async-start | bytes 6291456 | tf_op jit(solution)/shard_map/all_gather | solution.py:118
  53.5 238.3 %all-gather.15.cloned.1.call-start = ((), (), s32[]{:S(2)}) async-start(), calls=%async_computation.14 | async-start | bytes 1114112 | tf_op jit(solution)/shard_map/all_gather | solution.py:107
  54.2 298.8 %reduce-scatter.13.cloned.1.call-start = ((), (), s32[]{:S(2)}) async-start(), calls=%async_computation.15 | async-start | bytes 6291456 | tf_op jit(solution)/shard_map/reduce_scatter | solution.py:160
  298.6 54.4 %copy-start.2 = (bf16[1024,1024]{1,0:T(8,128)(2,1)S(1)}, bf16[1024,1024]{1,0:T(8,128)(2,1)}, u32[]{:S(2)}) copy-start(bf16[1024,1024]{1,0:T(8,128)(2,1)} %param.18) | copy-start | bytes 6291460
  298.6 213.8 %all-gather.25.cloned.1.call-start = ((), (), s32[]{:S(2)}) async-start(), calls=%async_computation.21 | async-start | bytes 6291456 | tf_op jit(solution)/shard_map/all_gather | solution.py:178
  299.2 283.9 %all-gather.17.cloned.1.call-start = ((), (), s32[]{:S(2)}) async-start(), calls=%async_computation.16 | async-start | bytes 6291456 | tf_op jit(solution)/shard_map/all_gather | solution.py:176
  299.3 58.9 %copy-start.41 = (f32[1024]{0:T(1024)}, f32[1024]{0:T(1024)S(1)}, u32[]{:S(2)}) copy-start(f32[1024]{0:T(1024)S(1)} %convert_element_type.217) | copy-start | bytes 12292
  358.3 288.4 %all-gather.19.cloned.1.call-start = ((), (), s32[]{:S(2)}) async-start(), calls=%async_computation.17 | async-start | bytes 17825792 | tf_op jit(solution)/shard_map/all_gather | solution.py:181
  359.0 368.0 %all-gather.21.cloned.1.call-start = ((), (), s32[]{:S(2)}) async-start(), calls=%async_computation.18 | async-start | bytes 17825792 | tf_op jit(solution)/shard_map/all_gather | solution.py:182
  359.8 494.8 %all-gather.23.cloned.1.call-start = ((), (), s32[]{:S(2)}) async-start(), calls=%async_computation.19 | async-start | bytes 17825792 | tf_op jit(solution)/shard_map/all_gather | solution.py:183
  360.5 149.7 %copy-start.64 = (s32[2]{0:T(128)S(1)}, s32[2]{0:T(128)}, u32[]{:S(2)}) copy-start(s32[2]{0:T(128)} %constant.244) | copy-start | bytes 28
  360.5 934.1 %reduce-scatter.19.cloned.1.call-start = ((), (), s32[]{:S(2)}) async-start(), calls=%async_computation.23 | async-start | bytes 49152 | tf_op jit(solution)/shard_map/reduce_scatter | solution.py:252
  360.6 149.7 %copy-start.63 = (s32[2]{0:T(128)S(1)}, s32[2]{0:T(128)}, u32[]{:S(2)}) copy-start(s32[2]{0:T(128)} %constant.247) | copy-start | bytes 28
  382.5 193.5 %copy-start.34 = (bf16[1024,32]{0,1:T(8,128)(2,1)}, bf16[1024,32]{0,1:T(8,128)(2,1)S(1)}, u32[]{:S(2)}) copy-start(bf16[1024,32]{0,1:T(8,128)(2,1)S(1)} %reshape.447) | copy-start | bytes 196612
  511.7 65.0 %copy-start.32 = (s32[1024,8]{0,1:T(8,128)}, s32[1024,8]{0,1:T(8,128)S(1)}, u32[]{:S(2)}) copy-start(s32[1024,8]{0,1:T(8,128)S(1)} %constant_dynamic-slice_fusion.3) | copy-start | bytes 98308
  512.4 63.5 %copy-start.8 = (bf16[1024,1024]{1,0:T(8,128)(2,1)S(1)}, bf16[1024,1024]{1,0:T(8,128)(2,1)}, u32[]{:S(2)}) copy-start(bf16[1024,1024]{1,0:T(8,128)(2,1)} %multiply_convert_fusion.3) | copy-start | bytes 6291460
  576.8 69.9 %copy-start.26 = (f32[1024,8]{0,1:T(8,128)}, f32[1024,8]{0,1:T(8,128)S(1)}, u32[]{:S(2)}) copy-start(f32[1024,8]{0,1:T(8,128)S(1)} %select_reduce_fusion.1) | copy-start | bytes 98308
  854.5 119.3 %copy-start.31 = (s32[2048,8]{0,1:T(8,128)S(1)}, s32[2048,8]{0,1:T(8,128)}, u32[]{:S(2)}) copy-start(s32[2048,8]{0,1:T(8,128)} %param.20) | copy-start | bytes 196612
  854.5 119.3 %copy-start.36 = (f32[2048,8]{0,1:T(8,128)S(1)}, f32[2048,8]{0,1:T(8,128)}, u32[]{:S(2)}) copy-start(f32[2048,8]{0,1:T(8,128)} %convert_element_type.220) | copy-start | bytes 196612
  854.6 119.3 %copy-start.61 = (s32[16]{0:T(128)S(1)}, s32[16]{0:T(128)}, u32[]{:S(2)}) copy-start(s32[16]{0:T(128)} %copy-done.60) | copy-start | bytes 196
  888.4 86.8 %copy-start = (s32[12288]{0:T(1024)S(1)}, s32[12288]{0:T(1024)}, u32[]{:S(2)}) copy-start(s32[12288]{0:T(1024)} %reshape.401) | copy-start | bytes 147460
  975.2 81.9 %copy-start.29 = (s32[16,768]{1,0:T(8,128)S(1)}, s32[16,768]{1,0:T(8,128)}, u32[]{:S(2)}) copy-start(s32[16,768]{1,0:T(8,128)} %copy-done.28) | copy-start | bytes 147460
  1057.3 289.9 %reduce-scatter.17.cloned.1.call-start = ((), (), s32[]{:S(2)}) async-start(), calls=%async_computation.22 | async-start | bytes 6291456 | tf_op jit(solution)/shard_map/reduce_scatter | solution.py:249
  1294.5 52.7 %copy-start.3 = (bf16[1024,1024]{1,0:T(8,128)(2,1)S(1)}, bf16[1024,1024]{1,0:T(8,128)(2,1)}, u32[]{:S(2)}) copy-start(bf16[1024,1024]{1,0:T(8,128)(2,1)} %param.18) | copy-start | bytes 6291460
  1294.5 52.7 %copy-start.35 = (bf16[1024,32]{0,1:T(8,128)(2,1)S(1)}, bf16[1024,32]{0,1:T(8,128)(2,1)}, u32[]{:S(2)}) copy-start(bf16[1024,32]{0,1:T(8,128)(2,1)} %copy-done.34) | copy-start | bytes 196612
  1294.5 52.6 %copy-start.42 = (f32[1024]{0:T(1024)S(1)}, f32[1024]{0:T(1024)}, u32[]{:S(2)}) copy-start(f32[1024]{0:T(1024)} %copy-done.41) | copy-start | bytes 12292
  1294.5 52.6 %copy-start.45 = (f32[1024]{0:T(1024)S(1)}, f32[1024]{0:T(1024)}, u32[]{:S(2)}) copy-start(f32[1024]{0:T(1024)} %copy-done.44) | copy-start | bytes 12292
  1294.6 120.9 %all-gather.27.cloned.1.call-start = ((), (), s32[]{:S(2)}) async-start(), calls=%async_computation.24 | async-start | bytes 6291456 | tf_op jit(solution)/shard_map/all_gather | solution.py:264
  1358.5 56.9 %copy-start.73 = (bf16[512,1024]{0,1:T(8,128)(2,1)S(1)}, bf16[512,1024]{0,1:T(8,128)(2,1)}, u32[]{:S(2)}) copy-start(bf16[512,1024]{0,1:T(8,128)(2,1)} %all-gather.15.cloned.1.call-done) | copy-start | bytes 3145732
  1358.5 696.5 %all-reduce.6.cloned.1.call-start = ((), (), s32[]{:S(2)}) async-start(), calls=%async_computation.30 | async-start | bytes 262144 | tf_op jit(solution)/shard_map/psum | solution.py:379
  1362.1 694.6 %reduce-scatter.25.cloned.1.call-start = ((), (), s32[]{:S(2)}) async-start(), calls=%async_computation.27 | async-start | bytes 557056 | tf_op jit(solution)/shard_map/reduce_scatter | solution.py:360
  1426.9 375.6 %copy-start.12 = (f32[2048,32]{0,1:T(8,128)S(1)}, f32[2048,32]{0,1:T(8,128)}, u32[]{:S(2)}) copy-start(f32[2048,32]{0,1:T(8,128)} %copy-done.11) | copy-start | bytes 786436
  1807.9 250.2 %reduce-scatter.27.cloned.1.call-start = ((), (), s32[]{:S(2)}) async-start(), calls=%async_computation.28 | async-start | bytes 557056 | tf_op jit(solution)/shard_map/reduce_scatter | solution.py:363
  1813.5 245.9 %reduce-scatter.29.cloned.1.call-start = ((), (), s32[]{:S(2)}) async-start(), calls=%async_computation.29 | async-start | bytes 1114112 | tf_op jit(solution)/shard_map/reduce_scatter | solution.py:366
  1819.2 241.7 %reduce-scatter.23.cloned.1.call-start = ((), (), s32[]{:S(2)}) async-start(), calls=%async_computation.26 | async-start | bytes 1114112 | tf_op jit(solution)/shard_map/reduce_scatter | solution.py:357
  1827.3 272.1 %reduce-scatter.21.cloned.1.call-start = ((), (), s32[]{:S(2)}) async-start(), calls=%async_computation.25 | async-start | bytes 6291456 | tf_op jit(solution)/shard_map/reduce_scatter | solution.py:345
  1835.3 322.1 %reduce-scatter.15.cloned.1.call-start = ((), (), s32[]{:S(2)}) async-start(), calls=%async_computation.20 | async-start | bytes 6291456 | tf_op jit(solution)/shard_map/reduce_scatter | solution.py:215
  1984.2 355.5 %reduce-scatter.35.cloned.1.call-start = ((), (), s32[]{:S(2)}) async-start(), calls=%async_computation.33 | async-start | bytes 17825792 | tf_op jit(solution)/shard_map/reduce_scatter | solution.py:375
  2007.9 513.5 %reduce-scatter.31.cloned.1.call-start = ((), (), s32[]{:S(2)}) async-start(), calls=%async_computation.31 | async-start | bytes 17825792 | tf_op jit(solution)/shard_map/reduce_scatter | solution.py:369
  2031.4 671.6 %reduce-scatter.33.cloned.1.call-start = ((), (), s32[]{:S(2)}) async-start(), calls=%async_computation.32 | async-start | bytes 17825792 | tf_op jit(solution)/shard_map/reduce_scatter | solution.py:372
  2055.0 44.4 %copy-start.4 = (bf16[1024,1024]{1,0:T(8,128)(2,1)S(1)}, bf16[1024,1024]{1,0:T(8,128)(2,1)}, u32[]{:S(2)}) copy-start(bf16[1024,1024]{1,0:T(8,128)(2,1)} %param.18) | copy-start | bytes 6291460
  2055.0 44.4 %copy-start.50 = (f32[1024]{0:T(1024)S(1)}, f32[1024]{0:T(1024)}, u32[]{:S(2)}) copy-start(f32[1024]{0:T(1024)} %copy-done.49) | copy-start | bytes 12292
  2055.0 44.4 %copy-start.52 = (f32[1024]{0:T(1024)S(1)}, f32[1024]{0:T(1024)}, u32[]{:S(2)}) copy-start(f32[1024]{0:T(1024)} %copy-done.51) | copy-start | bytes 12292
  2055.0 47.7 %copy-start.59 = (f32[1024]{0:T(1024)S(1)}, f32[1024]{0:T(1024)}, u32[]{:S(2)}) copy-start(f32[1024]{0:T(1024)} %get-tuple-element.363) | copy-start | bytes 12292
  2055.0 102.3 %copy-start.43 = (f32[1024]{0:T(1024)S(1)}, f32[1024]{0:T(1024)}, u32[]{:S(2)}) copy-start(f32[1024]{0:T(1024)} %copy-done.41) | copy-start | bytes 12292
  2055.0 102.3 %copy-start.46 = (f32[1024]{0:T(1024)S(1)}, f32[1024]{0:T(1024)}, u32[]{:S(2)}) copy-start(f32[1024]{0:T(1024)} %copy-done.44) | copy-start | bytes 12292
  2055.0 102.3 %copy-start.54 = (f32[1024]{0:T(1024)S(1)}, f32[1024]{0:T(1024)}, u32[]{:S(2)}) copy-start(f32[1024]{0:T(1024)} %copy-done.53) | copy-start | bytes 12292
  (51 other events, 463.5 us)
Sparse Core Ops, SparseCore 0:
  10.2 40.7 all-gather.12
  53.6 55.1 all-gather.10
  110.9 37.9 all-gather.14
  298.7 54.2 reduce-scatter.12
  354.5 56.7 all-gather.24
  413.3 56.7 all-gather.16
  472.5 126.8 all-gather.18
  601.9 125.0 all-gather.20
  729.4 125.0 all-gather.22
  1057.4 7.9 reduce-scatter.18
  1294.7 52.4 reduce-scatter.16
  1358.7 56.7 all-gather.26
  1421.5 122.4 all-reduce.5
  1808.0 55.7 reduce-scatter.24
  1867.6 54.8 reduce-scatter.26
  1926.6 56.3 reduce-scatter.28
  1987.5 56.3 reduce-scatter.22
  2046.1 53.3 reduce-scatter.20
  2101.8 55.5 reduce-scatter.14
  2161.3 178.3 reduce-scatter.34
  2343.9 177.4 reduce-scatter.30
  2525.5 177.5 reduce-scatter.32
where the time goes:
time: 2730 us; the launch traced here: 2710 us
  waiting for transfers between devices  898 us (33%)
  matrix products  657 us (24%)
  other arithmetic  529 us (19%)
  local copies, waits for them, and re-layouts  455 us (17%)
  blocking collectives  141 us (5%)
    reduce_scatter x1, waiting for transfers between devices, shards(): lax.psum_scatter(grad_gate.astype(jnp.bfloat16), 'dp', scatter_dimension=...  179 us
    reduce_scatter x1, waiting for transfers between devices, shards(): lax.psum_scatter(grad_up.astype(jnp.bfloat16), 'dp', scatter_dimension=1,...  179 us
    reduce_scatter x1, waiting for transfers between devices, shards(): lax.psum_scatter(grad_down.astype(jnp.bfloat16), 'dp', scatter_dimension=...  174 us
    unnamed x158, local copies, waits for them, and re-layouts  136 us
    dot_general x8, matrix products, block_scores(): jnp.einsum('qhgd,khd->hgqk', query_tile, key_block, preferred_element_typ...  128 us
    scatter-add x1, other arithmetic, shards(): d_hidden_two = jnp.zeros((group_rows, d_picked.shape[2]), jnp.float32).at...  110 us
    scatter-add x1, other arithmetic, shards(): jnp.zeros((group_rows, expert_out.shape[2]), jnp.float32).at[flat_table]  109 us
    all_gather x1, waiting for transfers between devices, shards(): lax.all_gather(w_down, 'dp', axis=1, tiled=True)  92.1 us
  transfers between devices with their start and end apart: 22, of which 11 were waited for; matrix products, arithmetic and copies ran while one was open for 52% of the time, Pallas kernels for 0%

commit v1 on v0

v1 whole, which is shorter than its diff:
```python
import functools

import jax
import jax.numpy as jnp
from jax import lax
from jax.experimental import pallas as pl
from jax.experimental.pallas import tpu as pltpu
from jax.sharding import PartitionSpec as P

QUERY_HEADS = 16
KEY_VALUE_HEADS = 8
HEAD_SIZE = 64
HALF = HEAD_SIZE // 2
EXPERTS = 32
CAP = 768
TILE = 256
BLOCK = 256
STEP = 16
EXPERT_CALLS = 4
KERNEL_COST = pl.CostEstimate(flops=1, bytes_accessed=150 * 10**6, transcendentals=0)

exact_mode = lax.Precision.HIGHEST
F32 = jnp.float32
BF16 = jnp.bfloat16
NEG = -1e30


def dot(a, b, ca, cb):
    return lax.dot_general(a, b, (((ca,), (cb,)), ((), ())), preferred_element_type=F32)


def z_core_shape(dp):
    return (4, 2, 2) if dp == 16 else None


def gather_rows(x, axis="tensor"):
    n = lax.axis_size(axis)
    if n != 2:
        return lax.all_gather(x, axis, axis=0, tiled=True)
    rank = lax.axis_index(axis)
    other = lax.ppermute(x, axis, [(0, 1), (1, 0)])
    first = rank == 0
    return jnp.concatenate([jnp.where(first, x, other), jnp.where(first, other, x)], axis=0)


def scatter_rows(x, axis="tensor"):
    n = lax.axis_size(axis)
    rows = x.shape[0] // n
    if n != 2:
        return lax.psum_scatter(x, axis, scatter_dimension=0, tiled=True).astype(F32)
    rank = lax.axis_index(axis)
    sent = lax.ppermute(
        lax.dynamic_slice_in_dim(x, (1 - rank) * rows, rows, 0), axis, [(0, 1), (1, 0)]
    )
    own = lax.dynamic_slice_in_dim(x, rank * rows, rows, 0)
    return own.astype(F32) + sent.astype(F32)


def dp_pairs(move):
    pairs = []
    for z in range(4):
        for y in range(2):
            for c in range(2):
                tz, ty, tc = move(z, y, c)
                pairs.append((z * 4 + y * 2 + c, tz * 4 + ty * 2 + tc))
    return pairs


CORE_PAIRS = dp_pairs(lambda z, y, c: (z, y, 1 - c))
Y_PAIRS = dp_pairs(lambda z, y, c: (z, 1 - y, c))
Z_PAIRS = {k: dp_pairs(lambda z, y, c, k=k: ((z + k) % 4, y, c)) for k in (1, 2, 3)}


def place(own, index, parts):
    buf = jnp.zeros((len(parts) + 1,) + own.shape, own.dtype)
    for i, a in [(index, own)] + parts:
        buf = lax.dynamic_update_index_in_dim(buf, a, i, 0)
    return buf


def gather_dp(x):
    n = lax.axis_size("dp")
    if z_core_shape(n) is None:
        return lax.all_gather(x, "dp", axis=0, tiled=False)
    me = lax.axis_index("dp")
    z, y, c = me // 4, (me // 2) % 2, me % 2
    parts = [((z - k) % 4, lax.ppermute(x, "dp", Z_PAIRS[k])) for k in (1, 3, 2)]
    buf = place(x, z, parts)
    buf = place(buf, y, [(1 - y, lax.ppermute(buf, "dp", Y_PAIRS))])
    buf = place(buf, c, [(1 - c, lax.ppermute(buf, "dp", CORE_PAIRS))])
    return jnp.transpose(buf, (2, 1, 0) + tuple(range(3, buf.ndim))).reshape((n,) + x.shape)


def at(a, i, axis):
    return lax.dynamic_index_in_dim(a, i, axis, keepdims=False)


def line_place():
    me = lax.axis_index("dp")
    return me // 4, (me // 2) % 2


class Reduce:
    def __init__(self, keep, send):
        self.by_hand = z_core_shape(lax.axis_size("dp")) is not None
        self.keep, self.send = keep, send
        self.stage = 0

    def sends(self):
        if not self.by_hand:
            return []
        if self.stage == 0:
            return [self.send]
        z, y = line_place()
        if self.stage == 1:
            self.keep = self.keep.reshape((4, 2) + self.keep.shape[1:])
            self.core = self.core.reshape(self.keep.shape)
            return [
                (
                    at(self.keep, 1 - y, 1).astype(F32) + at(self.core, 1 - y, 1).astype(F32)
                ).astype(BF16)
            ]

        def line(i):
            return (
                at(at(self.keep, y, 1), i, 0).astype(F32)
                + at(at(self.core, y, 1), i, 0).astype(F32)
                + at(self.over, i, 0).astype(F32)
            )

        self.own = line(z)
        return [line((z + k) % 4).astype(BF16) for k in (2, 1, 3)]

    def move(self, sent):
        if not self.by_hand:
            return []
        pairs = ([CORE_PAIRS], [Y_PAIRS], [Z_PAIRS[k] for k in (2, 1, 3)])[self.stage]
        return [lax.ppermute(a, "dp", p) for a, p in zip(sent, pairs)]

    def take(self, got):
        if self.by_hand:
            if self.stage == 0:
                (self.core,) = got
            elif self.stage == 1:
                (self.over,) = got
            else:
                self.parts = got
        self.stage += 1

    def result(self):
        n = lax.axis_size("dp")
        if not self.by_hand:
            even = lax.axis_index("dp") % 2 == 0
            first = jnp.where(even, self.keep, self.send)
            second = jnp.where(even, self.send, self.keep)
            both = jnp.stack([first, second], axis=1).reshape((n,) + self.keep.shape[1:])
            return lax.psum_scatter(both, "dp", scatter_dimension=0, tiled=False).astype(F32)
        total = self.own
        for a in self.parts:
            total = total + a.astype(F32)
        return total


def phase(work, inputs, reduces):
    sends = [r.sends() for r in reduces]
    (inputs, sends) = lax.optimization_barrier((list(inputs), sends))
    results = work(*inputs)
    moved = [r.move(sent) for r, sent in zip(reduces, sends)]
    results, moved = lax.optimization_barrier((results, moved))
    for r, got in zip(reduces, moved):
        r.take(got)
    return results


def rms_norm(values, gain):
    inverse = lax.rsqrt(jnp.mean(values * values, axis=-1, keepdims=True) + 1e-06)
    return (values * inverse * gain, inverse)


def rms_back(grad_rows, values, inverse, gain):
    scaled = grad_rows * gain
    gain_grad = jnp.sum(grad_rows * values * inverse, axis=0)
    inner = jnp.mean(scaled * values, axis=-1, keepdims=True)
    return (inverse * scaled - values * inverse * inverse * inverse * inner, gain_grad)


def rope_t(values, cosine, sine):
    rows = values.shape[1]
    v = values.reshape(-1, 2, HALF, rows)
    one, two = v[:, 0], v[:, 1]
    return jnp.stack(
        [one * cosine - two * sine, two * cosine + one * sine], axis=1
    ).reshape(values.shape)


def mask_of(start, j, i, bq):
    key = j * BLOCK + lax.broadcasted_iota(jnp.int32, (BLOCK, 2 * bq), 0)
    query = lax.broadcasted_iota(jnp.int32, (BLOCK, 2 * bq), 1)
    query = i * bq + jnp.where(query >= bq, query - bq, query)
    return (key >= start) & (key <= query)


def attend_kernel(low, q_ref, k_ref, v_ref, start_ref, o_ref, lse_ref):
    i = pl.program_id(1)
    bq = BLOCK
    q = q_ref[...]
    qs = jnp.concatenate([q[:HEAD_SIZE], q[HEAD_SIZE:]], axis=1)
    start = start_ref[...]
    start = jnp.concatenate([start, start], axis=1)

    def step(j, carry):
        peak, total, acc = carry
        at_key = pl.ds(pl.multiple_of(j * BLOCK, BLOCK), BLOCK)
        s = dot(k_ref[0, at_key, :], qs, 1, 0)
        s = jnp.where(mask_of(start, j, i, bq), s, NEG)
        new = jnp.maximum(peak, jnp.max(s, axis=0, keepdims=True))
        p = jnp.exp(s - new)
        scale = jnp.exp(peak - new)
        total = total * scale + jnp.sum(p, axis=0, keepdims=True)
        acc = acc * scale + dot(v_ref[:, at_key], p.astype(BF16), 1, 0)
        return new, total, acc

    peak, total, acc = lax.fori_loop(
        low[i],
        i + 1,
        step,
        (
            jnp.full((1, 2 * bq), NEG, F32),
            jnp.zeros((1, 2 * bq), F32),
            jnp.zeros((HEAD_SIZE, 2 * bq), F32),
        ),
    )
    out = (acc / total).astype(BF16)
    o_ref[...] = jnp.concatenate([out[:, :bq], out[:, bq:]], axis=0)
    lse = peak + jnp.log(total)
    lse_ref[0] = jnp.concatenate([lse[:, :bq], lse[:, bq:]], axis=0)


def attend(q_t, k, v_t, start, low):
    rows = q_t.shape[1]
    heads = k.shape[0]
    blocks = rows // BLOCK
    return pl.pallas_call(
        attend_kernel,
        grid_spec=pltpu.PrefetchScalarGridSpec(
            num_scalar_prefetch=1,
            grid=(heads, blocks),
            in_specs=[
                pl.BlockSpec((2 * HEAD_SIZE, BLOCK), lambda h, i, low: (h, i)),
                pl.BlockSpec((1, rows, HEAD_SIZE), lambda h, i, low: (h, 0, 0)),
                pl.BlockSpec((HEAD_SIZE, rows), lambda h, i, low: (h, 0)),
                pl.BlockSpec((1, BLOCK), lambda h, i, low: (0, i)),
            ],
            out_specs=[
                pl.BlockSpec((2 * HEAD_SIZE, BLOCK), lambda h, i, low: (h, i)),
                pl.BlockSpec((1, 2, BLOCK), lambda h, i, low: (h, 0, i)),
            ],
        ),
        out_shape=[
            jax.ShapeDtypeStruct(q_t.shape, BF16),
            jax.ShapeDtypeStruct((heads, 2, rows), F32),
        ],
        cost_estimate=KERNEL_COST,
        name="attend",
    )(low, q_t, k, v_t, start)


def attend_back_kernel(
    low, q_ref, do_ref, o_ref, lse_ref, k_ref, v_ref, kt_ref, start_ref, cos_ref, sin_ref,
    dq_ref, dk_ref, dv_ref,
):
    i = pl.program_id(1)
    bq = BLOCK

    @pl.when(i == 0)
    def _():
        dk_ref[...] = jnp.zeros_like(dk_ref)
        dv_ref[...] = jnp.zeros_like(dv_ref)

    def side(a):
        return jnp.concatenate([a[:HEAD_SIZE], a[HEAD_SIZE:]], axis=1)

    qs = side(q_ref[...])
    dos = side(do_ref[...])
    inner = jnp.sum(dos.astype(F32) * side(o_ref[...]).astype(F32), axis=0, keepdims=True)
    lse = lse_ref[0]
    lse = jnp.concatenate([lse[0:1], lse[1:2]], axis=1)
    start = start_ref[...]
    start = jnp.concatenate([start, start], axis=1)

    def step(j, dq):
        at_key = pl.ds(pl.multiple_of(j * BLOCK, BLOCK), BLOCK)
        s = dot(k_ref[0, at_key, :], qs, 1, 0)
        p = jnp.where(mask_of(start, j, i, bq), jnp.exp(s - lse), 0.0)
        dp = dot(v_ref[0, at_key, :], dos, 1, 0)
        ds = (p * (dp - inner)).astype(BF16)
        dv_ref[0, at_key, :] += dot(p.astype(BF16), dos, 1, 1)
        dk_ref[0, at_key, :] += dot(ds, qs, 1, 1)
        return dq + dot(kt_ref[:, at_key], ds, 1, 0)

    dq = lax.fori_loop(low[i], i + 1, step, jnp.zeros((HEAD_SIZE, 2 * bq), F32))
    dq = dq * HEAD_SIZE ** (-0.5)
    cosine, sine = cos_ref[...], sin_ref[...]
    for h in range(2):
        one = dq[:HALF, h * bq : (h + 1) * bq]
        two = dq[HALF:, h * bq : (h + 1) * bq]
        dq_ref[h * HEAD_SIZE : h * HEAD_SIZE + HALF, :] = (one * cosine + two * sine).astype(BF16)
        dq_ref[h * HEAD_SIZE + HALF : (h + 1) * HEAD_SIZE, :] = (
            two * cosine - one * sine
        ).astype(BF16)


def attend_back(first, heads, q_t, do_t, o_t, lse, k, v, k_t, start, cosine, sine, low):
    rows = q_t.shape[1]
    blocks = rows // BLOCK
    pair = pl.BlockSpec((2 * HEAD_SIZE, BLOCK), lambda h, i, low: (h + first, i))
    whole = pl.BlockSpec((1, rows, HEAD_SIZE), lambda h, i, low: (h + first, 0, 0))
    table = pl.BlockSpec((HALF, BLOCK), lambda h, i, low: (0, i))
    grad = pl.BlockSpec((1, rows, HEAD_SIZE), lambda h, i, low: (h, 0, 0))
    return pl.pallas_call(
        attend_back_kernel,
        grid_spec=pltpu.PrefetchScalarGridSpec(
            num_scalar_prefetch=1,
            grid=(heads, blocks),
            in_specs=[
                pair,
                pair,
                pair,
                pl.BlockSpec((1, 2, BLOCK), lambda h, i, low: (h + first, 0, i)),
                whole,
                whole,
                pl.BlockSpec((HEAD_SIZE, rows), lambda h, i, low: (h + first, 0)),
                pl.BlockSpec((1, BLOCK), lambda h, i, low: (0, i)),
                table,
                table,
            ],
            out_specs=[
                pl.BlockSpec((2 * HEAD_SIZE, BLOCK), lambda h, i, low: (h, i)), grad, grad,
            ],
        ),
        out_shape=[
            jax.ShapeDtypeStruct((heads * 2 * HEAD_SIZE, rows), BF16),
            jax.ShapeDtypeStruct((heads, rows, HEAD_SIZE), F32),
            jax.ShapeDtypeStruct((heads, rows, HEAD_SIZE), F32),
        ],
        cost_estimate=KERNEL_COST,
        name="attend_back",
    )(low, q_t, do_t, o_t, lse, k, v, k_t, start, cosine, sine)


def pieces_of(rows, most):
    return [(r, min(most, rows - r)) for r in range(0, rows, most)]


def expert_kernel(
    table, count, parity, x_hbm, c_hbm, gate_ref, w_ref, keep_ref, send_ref, out_hbm, dx_hbm,
    dg_ref, mark_ref, xs, cs, oacc, dacc, xg, cg, xb, cb, dab, hgb, sems,
):
    e = pl.program_id(0)
    last = pl.num_programs(0) - 1
    rows, width = x_hbm.shape
    lanes = width // 128
    dp, rs, ff = w_ref.shape[0], w_ref.shape[3], w_ref.shape[4]
    stages = (xb, cb, dab)

    @pl.when(e == 0)
    def _():
        jobs = [
            (source.at[pl.ds(r, n), :], target, r, n)
            for source, target in ((x_hbm, xs), (c_hbm, cs))
            for r, n in pieces_of(rows, CAP)
        ]
        copies = [
            pltpu.make_async_copy(
                source, stages[i % 3].at[pl.ds(0, n), :], sems.at[i % 3]
            )
            for i, (source, _, _, n) in enumerate(jobs)
        ]
        for op in copies[:3]:
            op.start()
        oacc[...] = jnp.zeros_like(oacc)
        dacc[...] = jnp.zeros_like(dacc)
        xg[...] = jnp.zeros_like(xg)
        cg[...] = jnp.zeros_like(cg)
        for i, (_, target, r, n) in enumerate(jobs):
            copies[i].wait()
            for j in range(lanes):
                target[pl.ds(r * lanes + j, n, stride=lanes), :] = stages[i % 3][
                    :n, j * 128 : (j + 1) * 128
                ].astype(F32)
            if i + 3 < len(jobs):
                copies[i + 3].start()
        for target in (xs, cs):
            target[rows * lanes :, :] = jnp.zeros((8 * lanes, 128), F32)

    named = count[e]
    w_gate = w_ref[:, 0, 0].reshape(dp * rs, ff)
    w_up = w_ref[:, 0, 1].reshape(dp * rs, ff)
    w_low = w_ref[:, 0, 2, : rs // 2].reshape(dp * rs // 2, ff)
    w_high = w_ref[:, 0, 2, rs // 2 :].reshape(dp * rs // 2, ff)

    for t in range(CAP // TILE):
        here = slice(t * TILE, (t + 1) * TILE)

        @pl.when(named > t * TILE)
        def _(t=t, here=here):
            groups = (jnp.minimum(named - t * TILE, TILE) + STEP - 1) // STEP
            first = e * CAP + t * TILE

            def places(b):
                return [
                    pl.ds(pl.multiple_of(table[first + b * STEP + k], 8), lanes)
                    for k in range(STEP)
                ]

            def own(b):
                return [
                    pl.ds(pl.multiple_of(b * (STEP * lanes) + k * lanes, 8), lanes)
                    for k in range(STEP)
                ]

            def pick(b, carry):
                there, here_ = places(b), own(b)
                xrows = [xs[p, :] for p in there]
                crows = [cs[p, :] for p in there]
                for p, v, w in zip(here_, xrows, crows):
                    xg[p, :] = v
                    cg[p, :] = w
                return carry

            lax.fori_loop(0, groups, pick, 0)
            for j in range(lanes):
                one = slice(j * 128, (j + 1) * 128)
                xb[here, one] = xg[pl.ds(j, TILE, stride=lanes), :].astype(BF16)
                cb[here, one] = cg[pl.ds(j, TILE, stride=lanes), :].astype(BF16)
            gate = gate_ref[0, here, :]
            x = xb[here, :]
            c = cb[here, :]
            a = dot(x, w_gate, 1, 0)
            b = dot(x, w_up, 1, 0)
            sig = jax.nn.sigmoid(a)
            silu = a * sig
            hid = silu * b
            hg = (hid * gate).astype(BF16)
            hgb[here, :] = hg
            u = dot(c[:, :ff], w_low, 1, 1) + dot(c[:, ff:], w_high, 1, 1)
            dg_ref[0, here, :] = jnp.sum(hid * u, axis=1, keepdims=True)
            du = gate * u
            da = (du * b * sig * (1.0 + a * (1.0 - sig))).astype(BF16)
            db = (du * silu).astype(BF16)
            dab[here, :ff] = da
            dab[here, ff:] = db
            for half, w in enumerate((w_low, w_high)):
                y = dot(hg, w, 1, 0)
                for j in range(ff // 128):
                    xg[pl.ds(half * (ff // 128) + j, TILE, stride=lanes), :] = y[
                        :, j * 128 : (j + 1) * 128
                    ]
            dx = dot(da, w_gate, 1, 1) + dot(db, w_up, 1, 1)
            for j in range(lanes):
                cg[pl.ds(j, TILE, stride=lanes), :] = dx[:, j * 128 : (j + 1) * 128]

            def add(b, carry):
                there, here_ = places(b), own(b)
                outs = [oacc[p, :] + xg[q, :] for p, q in zip(there, here_)]
                backs = [dacc[p, :] + cg[q, :] for p, q in zip(there, here_)]
                for p, v, w in zip(there, outs, backs):
                    oacc[p, :] = v
                    dacc[p, :] = w
                return carry

            lax.fori_loop(0, groups, add, 0)

    even = parity[0] == 0

    def split(value, slot, low, high):
        v = value.reshape(dp // 2, 2, high - low, ff)
        first, second = v[:, 0], v[:, 1]
        keep_ref[:, 0, slot, low:high, :] = jnp.where(even, first, second)
        send_ref[:, 0, slot, low:high, :] = jnp.where(even, second, first)

    def grads(depth):
        x = xb[:depth, :]
        d = dab[:depth, :]
        split(dot(x, d[:, :ff], 0, 0).astype(BF16), 0, 0, rs)
        split(dot(x, d[:, ff:], 0, 0).astype(BF16), 1, 0, rs)
        h = hgb[:depth, :]
        c = cb[:depth, :]
        split(dot(h, c[:, :ff], 0, 0).astype(BF16), 2, 0, rs // 2)
        split(dot(h, c[:, ff:], 0, 0).astype(BF16), 2, rs // 2, rs)

    @pl.when(named == 0)
    def _():
        keep_ref[...] = jnp.zeros_like(keep_ref)
        send_ref[...] = jnp.zeros_like(send_ref)

    for t in range(CAP // TILE):

        @pl.when((named > t * TILE) & (named <= (t + 1) * TILE))
        def _(t=t):
            grads((t + 1) * TILE)

    @pl.when(e == last)
    def _():
        mark_ref[...] = jnp.zeros_like(mark_ref)
        jobs = [
            (source, target.at[pl.ds(r, n), :], r, n)
            for source, target in ((oacc, out_hbm), (dacc, dx_hbm))
            for r, n in pieces_of(rows, CAP)
        ]
        copies = [
            pltpu.make_async_copy(
                stages[i % 3].at[pl.ds(0, n), :], target, sems.at[i % 3]
            )
            for i, (_, target, _, n) in enumerate(jobs)
        ]
        for i, (source, _, r, n) in enumerate(jobs):
            if i >= 3:
                copies[i - 3].wait()
            for j in range(lanes):
                stages[i % 3][:n, j * 128 : (j + 1) * 128] = source[
                    pl.ds(r * lanes + j, n, stride=lanes), :
                ].astype(BF16)
            copies[i].start()
        for op in copies[-3:]:
            op.wait()


def expert_call(table, count, parity, x, c, gates, weights, first_expert, expert_count):
    rows, width = x.shape
    dp, _, _, rs, ff = weights.shape
    lanes = width // 128
    grads = pl.BlockSpec((dp // 2, 1, 3, rs, ff), lambda e, *_: (0, e, 0, 0, 0))
    hbm = pl.BlockSpec(memory_space=pl.ANY)
    return pl.pallas_call(
        expert_kernel,
        grid_spec=pltpu.PrefetchScalarGridSpec(
            num_scalar_prefetch=3,
            grid=(expert_count,),
            in_specs=[
                hbm,
                hbm,
                pl.BlockSpec((1, CAP, 1), lambda e, *_: (e + first_expert, 0, 0)),
                pl.BlockSpec(
                    (dp, 1, 3, rs, ff), lambda e, *_: (0, e + first_expert, 0, 0, 0)
                ),
            ],
            out_specs=[
                grads, grads, hbm, hbm, pl.BlockSpec((1, CAP, 1), lambda e, *_: (e, 0, 0)),
                pl.BlockSpec((8, 128), lambda e, *_: (0, 0)),
            ],
            scratch_shapes=[
                pltpu.VMEM(((rows + 8) * lanes, 128), F32),
                pltpu.VMEM(((rows + 8) * lanes, 128), F32),
                pltpu.VMEM(((rows + 8) * lanes, 128), F32),
                pltpu.VMEM(((rows + 8) * lanes, 128), F32),
                pltpu.VMEM((TILE * lanes, 128), F32),
                pltpu.VMEM((TILE * lanes, 128), F32),
                pltpu.VMEM((CAP, width), BF16),
                pltpu.VMEM((CAP, width), BF16),
                pltpu.VMEM((CAP, 2 * ff), BF16),
                pltpu.VMEM((CAP, ff), BF16),
                pltpu.SemaphoreType.DMA((3,)),
            ],
        ),
        out_shape=[
            jax.ShapeDtypeStruct((dp // 2, expert_count, 3, rs, ff), BF16),
            jax.ShapeDtypeStruct((dp // 2, expert_count, 3, rs, ff), BF16),
            jax.ShapeDtypeStruct((rows, width), BF16),
            jax.ShapeDtypeStruct((rows, width), BF16),
            jax.ShapeDtypeStruct((expert_count, CAP, 1), F32),
            jax.ShapeDtypeStruct((8, 128), F32),
        ],
        compiler_params=pltpu.CompilerParams(vmem_limit_bytes=63 * 2**20),
        cost_estimate=KERNEL_COST,
        name="experts",
    )(table, count, parity, x, c, gates, weights)


def shards(
    tokens, lengths, routes, norm1_gain, w_query, key_projection, value_projection, w_out,
    norm2_gain, w_router, w_gate, w_up, w_down, cotangent,
):
    tensor = lax.axis_size("tensor")
    rank = lax.axis_index("tensor")
    dp = lax.axis_size("dp")
    me = lax.axis_index("dp")
    local_rows, width = tokens.shape
    rows = local_rows * tensor
    heads = QUERY_HEADS // tensor
    kv_heads = KEY_VALUE_HEADS // tensor
    expert_local = w_gate.shape[0]
    shard_rows = norm1_gain.shape[0]
    own_row = rank * local_rows

    pack = jnp.concatenate(
        [
            w_query, key_projection, value_projection, w_out.T, w_router,
            norm1_gain[:, None], norm2_gain[:, None],
        ],
        axis=1,
    )
    used = pack.shape[1]
    pack = jnp.pad(pack, ((0, 0), (0, -used % 128)))
    small = gather_dp(pack).reshape(dp * shard_rows, pack.shape[1])
    d_qkv = w_query.shape[1] + 2 * key_projection.shape[1]
    d_q, d_k = w_query.shape[1], key_projection.shape[1]
    d_o = w_out.shape[0]
    qkv_weight = small[:, :d_qkv]
    out_weight_t = small[:, d_qkv : d_qkv + d_o]
    router_weight = small[:, d_qkv + d_o : d_qkv + d_o + EXPERTS]
    gains = small[:, used - 2 : used].astype(F32).T
    gain_one, gain_two = gains[0], gains[1]

    ff = w_gate.shape[2]
    down = jnp.concatenate([w_down[:, :, :ff], w_down[:, :, ff:]], axis=1)
    big_shard = jnp.stack([w_gate, w_up, down], axis=1)
    big = lax.all_gather(big_shard.reshape(-1, ff), "dp", axis=0, tiled=True)
    big = big.reshape((dp,) + big_shard.shape)

    inputs_all = gather_rows(tokens)
    grad_all = gather_rows(cotangent)

    seq = lengths[0]
    order = jnp.arange(seq.shape[0], dtype=jnp.int32)
    ends = jnp.sum(jnp.where(order[:, None] <= order[None, :], seq[:, None], 0), axis=0)
    row_index = jnp.arange(rows, dtype=jnp.int32)
    passed = row_index[None, :] >= ends[:, None]
    first_row = jnp.max(jnp.where(passed, ends[:, None], 0), axis=0)
    position = row_index - first_row
    frequency = 10000.0 ** (-2.0 * jnp.arange(HALF, dtype=F32) / HEAD_SIZE)
    angles = frequency[:, None] * position.astype(F32)[None, :]
    cosine, sine = jnp.cos(angles), jnp.sin(angles)
    low = first_row[::BLOCK] // BLOCK
    start = first_row[None, :]

    names = rank * expert_local + jnp.arange(expert_local, dtype=jnp.int32)
    member_all = jnp.any(
        routes[:, :, None] == jnp.arange(EXPERTS, dtype=jnp.int32)[None, None, :], axis=1
    )
    member = jnp.any(routes.T[None, :, :] == names[:, None, None], axis=1)
    count = jnp.sum(member.astype(jnp.int32), axis=1)
    table = jnp.sort(jnp.where(member, row_index[None, :], rows), axis=1)[:, :CAP]
    filled = jnp.arange(CAP, dtype=jnp.int32)[None, :] < count[:, None]

    normed_all, inverse_all = rms_norm(inputs_all.astype(F32), gain_one)
    hidden_one = normed_all.astype(BF16)
    qkv = dot(qkv_weight, hidden_one, 0, 1)
    q_t = (rope_t(qkv[:d_q], cosine, sine).astype(BF16).astype(F32) * HEAD_SIZE ** (-0.5)).astype(
        BF16
    )
    k_t = rope_t(qkv[d_q : d_q + d_k], cosine, sine).astype(BF16)
    v_t = qkv[d_q + d_k :].astype(BF16)
    k = jnp.transpose(k_t.reshape(kv_heads, HEAD_SIZE, rows), (0, 2, 1))
    v = jnp.transpose(v_t.reshape(kv_heads, HEAD_SIZE, rows), (0, 2, 1))
    o_t, lse = attend(q_t, k, v_t, start, low)
    inputs_f = tokens.astype(F32)
    residual_two = inputs_f + scatter_rows(dot(o_t, out_weight_t, 0, 1).astype(BF16))

    normed_two, inverse_two = rms_norm(residual_two, gain_two)
    hidden_rows = normed_two.astype(BF16)
    hidden_two = gather_rows(hidden_rows)
    logits = jnp.where(member_all, dot(hidden_two, router_weight, 1, 0), NEG)
    gates_f = jax.nn.softmax(logits, axis=-1)
    share = lax.dynamic_slice_in_dim(gates_f, rank * expert_local, expert_local, 1)
    share_t = share.astype(BF16).astype(F32).T
    slot_gate = jnp.sum(
        jnp.where(table[:, :, None] == row_index[None, None, :], share_t[:, None, :], 0.0), axis=2
    )[:, :, None]

    calls = EXPERT_CALLS
    each = expert_local // calls
    parity = (me % 2).astype(jnp.int32).reshape(1)
    slots = table * (width // 128)
    out_part, dx_part = 0.0, 0.0
    dg, sums = [], []
    for call in range(calls):
        picked = slice(call * each, (call + 1) * each)
        made = []

        def work(counted, picked=picked, call=call, made=made):
            *outs, mark = expert_call(
                slots[picked].reshape(-1), counted, parity, hidden_two, grad_all, slot_gate,
                big, call * each, each,
            )
            made.extend(outs)
            return [mark]

        phase(work, [count[picked]], sums)
        keep, send, out_p, dx_p, dg_p = made
        sums.append(Reduce(keep, send))
        out_part = out_part + out_p.astype(F32)
        dx_part = dx_part + dx_p.astype(F32)
        dg.append(dg_p[:, :, 0])

    dg = jnp.where(filled, jnp.concatenate(dg, axis=0), 0.0)

    def over_x(sent, sent_out, dg):
        dg = jnp.sum(
            jnp.where(table[:, None, :] == row_index[None, :, None], dg[:, None, :], 0.0), axis=2
        )
        d_dense = lax.dynamic_update_slice_in_dim(
            jnp.zeros((rows, EXPERTS), F32), dg.T, rank * expert_local, 1
        )
        return [scatter_rows(sent), scatter_rows(d_dense), sent_out]

    d_rows, d_gates, out_part = phase(
        over_x, [dx_part.astype(BF16), out_part.astype(BF16), dg], sums[1:]
    )
    gates_own = lax.dynamic_slice_in_dim(gates_f, own_row, local_rows, 0)
    d_logits = gates_own * (d_gates - jnp.sum(d_gates * gates_own, axis=-1, keepdims=True))
    router_grad = jnp.dot(hidden_rows.astype(F32).T, d_logits, precision=exact_mode)
    d_rows = d_rows + jnp.dot(d_logits, router_weight.astype(F32).T, precision=exact_mode)
    d_norm_two, gain_two_grad = rms_back(d_rows, residual_two, inverse_two, gain_two)
    d_residual = cotangent.astype(F32) + d_norm_two
    (d_all,) = phase(
        lambda sent: [gather_rows(sent)], [d_residual.astype(BF16)], sums[2:]
    )

    do_t = dot(out_weight_t, d_all, 0, 1).astype(BF16)

    def back(do_t, out_part):
        parts = attend_back(
            0, kv_heads, q_t, do_t, o_t, lse, k, v, k_t, start, cosine, sine, low
        )
        return list(parts) + [scatter_rows(out_part)]

    dq_t, dk, dv, moe_rows = phase(back, [do_t, out_part], sums[3:])
    output = (residual_two + moe_rows).astype(BF16)
    dk_t = rope_t(jnp.transpose(dk, (0, 2, 1)).reshape(d_k, rows), cosine, -sine).astype(BF16)
    dv_t = jnp.transpose(dv, (0, 2, 1)).reshape(d_k, rows).astype(BF16)
    d_qkv_t = jnp.concatenate([dq_t, dk_t, dv_t], axis=0)
    grad_out_t = dot(d_all, o_t, 0, 1).astype(BF16)
    grad_qkv = dot(hidden_one, d_qkv_t, 0, 1).astype(BF16)
    d_hidden_part = dot(d_qkv_t, qkv_weight, 0, 1)
    gain_one_grad = jnp.sum(d_hidden_part * inputs_all.astype(F32) * inverse_all, axis=0)
    misc = jnp.concatenate(
        [router_grad, gain_one_grad[:, None], gain_two_grad[:, None]], axis=1
    ).astype(BF16)
    misc = jnp.pad(misc, ((0, 0), (0, -misc.shape[1] % 128)))
    small_grad = jnp.concatenate([grad_qkv, grad_out_t, misc], axis=1)
    small_grad = small_grad.reshape(dp // 2, 2, shard_rows, small_grad.shape[1])
    even = parity[0] == 0
    first, second = small_grad[:, 0], small_grad[:, 1]
    small = Reduce(jnp.where(even, first, second), jnp.where(even, second, first))
    d_hidden_one = scatter_rows(d_hidden_part.astype(BF16))
    for _ in range(3):
        small.take(small.move(small.sends()))
    small_sum = small.result()
    d_norm_one, _ = rms_back(
        d_hidden_one, inputs_f, lax.dynamic_slice_in_dim(inverse_all, own_row, local_rows, 0),
        gain_one,
    )
    grad_tokens = (d_residual + d_norm_one).astype(BF16)

    total = jnp.concatenate([r.result() for r in sums], axis=0)
    grad_gate, grad_up = total[:, 0], total[:, 1]
    half = shard_rows // 2
    grad_down = jnp.concatenate([total[:, 2, :half], total[:, 2, half:]], axis=2)
    over_tensor = small_sum[:, d_qkv + d_o : used]
    if tensor == 2:
        over_tensor = over_tensor + lax.ppermute(over_tensor, "tensor", [(0, 1), (1, 0)])
    else:
        over_tensor = lax.psum(over_tensor, "tensor")
    return (
        output,
        grad_tokens,
        over_tensor[:, EXPERTS],
        small_sum[:, :d_q],
        small_sum[:, d_q : d_q + d_k],
        small_sum[:, d_q + d_k : d_qkv],
        small_sum[:, d_qkv : d_qkv + d_o].T,
        over_tensor[:, EXPERTS + 1],
        over_tensor[:, :EXPERTS],
        grad_gate,
        grad_up,
        grad_down,
    )


def solution(mesh):
    return jax.shard_map(
        shards,
        mesh=mesh,
        in_specs=(
            P(("dp", "tensor"), None),
            P("dp", None),
            P("dp", None),
            P("dp"),
            P("dp", "tensor"),
            P("dp", "tensor"),
            P("dp", "tensor"),
            P("tensor", "dp"),
            P("dp"),
            P("dp", None),
            P("tensor", "dp", None),
            P("tensor", "dp", None),
            P("tensor", "dp", None),
            P(("dp", "tensor"), None),
        ),
        out_specs=(
            P(("dp", "tensor"), None),
            P(("dp", "tensor"), None),
            P("dp"),
            P("dp", "tensor"),
            P("dp", "tensor"),
            P("dp", "tensor"),
            P("tensor", "dp"),
            P("dp"),
            P("dp", None),
            P("tensor", "dp", None),
            P("tensor", "dp", None),
            P("tensor", "dp", None),
        ),
        check_vma=False,
    )
```

time: 2730 us -> 1070 us (0.39)
  matrix products: 657 us -> 43.5 us
  waiting for transfers between devices: 898 us -> 324 us
  local copies, waits for them, and re-layouts: 455 us -> 74.6 us
  other arithmetic: 529 us -> 161 us
  Pallas kernels: 0 us -> 363 us
  blocking collectives: 141 us -> 0 us
  starting transfers between devices: 1.68 us -> 71.4 us
    reduce_scatter x12 -> x0, waiting for transfers between devices: 687 us -> none  [the longest x1 179 us: shards(): lax.psum_scatter(grad_gate.astype(jnp.bfloat16), 'dp', scatter_dimension=...]
    dot_general x52 -> x9, matrix products: 657 us -> 43.5 us  [the longest x7 38 us: dot(): lax.dot_general(a, b, (((ca,), (cb,)), ((), ())), preferred_element_type=...]
    pallas_call x0 -> x6, Pallas kernels: none -> 363 us  [the longest x4 269 us: expert_call(): pl.pallas_call(expert_kernel, grid_spec=pltpu.PrefetchScalarGridSpec(num_...]
    ppermute x0 -> x40, waiting for transfers between devices: none -> 324 us  [the longest x5 103 us: scatter_rows(): lax.ppermute(lax.dynamic_slice_in_dim(x, (1 - rank) * rows, rows, 0), axi...]
    scatter-add x2 -> x0, other arithmetic: 219 us -> none  [the longest x1 110 us: shards(): d_hidden_two = jnp.zeros((group_rows, d_picked.shape[2]), jnp.float32).at...]
    gather x5 -> x0, local copies, waits for them, and re-layouts: 210 us -> none  [the longest x3 82.5 us: shards(): jnp.take_along_axis(share.T, table, axis=1)]
    all_gather x9 -> x1, waiting for transfers between devices: 207 us -> 0.01 us  [shards(): big = lax.all_gather(big_shard.reshape(-1, ff), 'dp', axis=0, tiled=True)]
    unnamed x158 -> x195, local copies, waits for them, and re-layouts: 136 us -> 13 us
  transfers between devices with their start and end apart: 22 -> 41, of which waited for: 11 -> 18; matrix products, arithmetic and copies ran while one was open for 52% -> 16% of each run, Pallas kernels for 0% -> 27%
where the time goes in v1:
time: 1070 us; the launch traced here: 1060 us
  Pallas kernels  363 us (34%)
  waiting for transfers between devices  324 us (30%)
  other arithmetic  161 us (15%)
  local copies, waits for them, and re-layouts  74.6 us (7%)
  starting transfers between devices  71.4 us (7%)
  matrix products  43.5 us (4%)
  between operations  17.6 us (2%)
    pallas_call x4, Pallas kernels, expert_call(): pl.pallas_call(expert_kernel, grid_spec=pltpu.PrefetchScalarGridSpec(num_...  269 us
    ppermute x5, waiting for transfers between devices, scatter_rows(): lax.ppermute(lax.dynamic_slice_in_dim(x, (1 - rank) * rows, rows, 0), axi...  103 us
    ppermute x4, waiting for transfers between devices, gather_rows(): other = lax.ppermute(x, axis, [(0, 1), (1, 0)])  97.8 us
    ppermute x25, waiting for transfers between devices, move(): return [lax.ppermute(a, 'dp', p) for a, p in zip(sent, pairs)]  62.7 us
    pallas_call x1, Pallas kernels, attend_back(): pl.pallas_call(attend_back_kernel, grid_spec=pltpu.PrefetchScalarGridSpec...  50.5 us
    pallas_call x1, Pallas kernels, attend(): pl.pallas_call(attend_kernel, grid_spec=pltpu.PrefetchScalarGridSpec(num_...  44.3 us
    ppermute x25, starting transfers between devices, move(): return [lax.ppermute(a, 'dp', p) for a, p in zip(sent, pairs)]  40.4 us
    dot_general x7, matrix products, dot(): lax.dot_general(a, b, (((ca,), (cb,)), ((), ())), preferred_element_type=...  38 us
  transfers between devices with their start and end apart: 41, of which 18 were waited for; matrix products, arithmetic and copies ran while one was open for 16% of the time, Pallas kernels for 27%

profile of v1, /device:TPU:0, one launch (start us, length us, event | category | flops | bytes accessed | tf_op | source)
XLA Modules:
  0.0 1055.5 jit_solution(946635207283545943)
XLA Ops:
  26.2 7.4 collective-permute-done.1
  33.6 13.6 %collective-permute-done.2 = bf16[64,1664]{1,0:T(8,128)(2,1)S(1)} collective-permute-done((bf16[64,1664]{1,0:T(8,128)(2,1)S(1)}, bf16[64,1664]{1,0:T(8,128)(2,1)S(1)}, u32[]{:S(2)}, u32[]{:S(2)}) %collective-permute-start.2) | collective-permute-done | bytes 213024 | tf_op jit(solution)/shard_map/ppermute | solution.py:87
  50.7 36.2 %collective-permute-done.3 = bf16[4,64,1664]{2,1,0:T(8,128)(2,1)S(1)} collective-permute-done((bf16[4,64,1664]{2,1,0:T(8,128)(2,1)S(1)}, bf16[4,64,1664]{2,1,0:T(8,128)(2,1)S(1)}, u32[]{:S(2)}, u32[]{:S(2)}) %collective-permute-start.3) | collective-permute-done | bytes 852000 | tf_op jit(solution)/shard_map/ppermute | solution.py:89
  87.8 24.8 %collective-permute-done.8 = bf16[1024,1024]{1,0:T(8,128)(2,1)} collective-permute-done((bf16[1024,1024]{1,0:T(8,128)(2,1)}, bf16[1024,1024]{1,0:T(8,128)(2,1)}, u32[]{:S(2)}, u32[]{:S(2)}) %collective-permute-start.8) | collective-permute-done | bytes 2097184 | tf_op jit(solution)/shard_map/ppermute | solution.py:41
  112.6 3.9 broadcast_select_fusion.3
  118.5 5.0 fusion.19
  134.0 44.3 %attend.1 = (bf16[512,2048]{1,0:T(8,128)(2,1)}, f32[4,2,2048]{2,1,0:T(2,128)}) custom-call(s32[8]{0:T(128)} %and_select_fusion.low, bf16[512,2048]{1,0:T(8,128)(2,1)} %bitcast.206, bf16[4,2048,64]{2,1,0:T(8,128)(2,1)} %bitcast.204, bf16[256,2048]{1,0:T(8,128)(2,1)} %slice.236.v_ref, s32[1,2048]{1,0:T(1,128)} %bitcast.250), custom_call_target="tpu_custom_call" | custom-call | flops 1 | bytes 150000000 | tf_op jit(solution)/shard_map/attend/pallas_call | solution.py:243
  178.3 4.5 convolution_convert_fusion
  187.8 44.7 %collective-permute-done.6 = bf16[1024,1024]{1,0:T(8,128)(2,1)} collective-permute-done((bf16[1024,1024]{1,0:T(8,128)(2,1)}, bf16[1024,1024]{1,0:T(8,128)(2,1)}, u32[]{:S(2)}, u32[]{:S(2)}) %collective-permute-start.6) | collective-permute-done | bytes 2097184 | tf_op jit(solution)/shard_map/ppermute | solution.py:52
  241.7 4.9 pad_maximum_fusion.3.c_hbm
  246.6 36.3 %collective-permute-done.7 = bf16[1024,1024]{1,0:T(8,128)(2,1)} collective-permute-done((bf16[1024,1024]{1,0:T(8,128)(2,1)S(1)}, bf16[1024,1024]{1,0:T(8,128)(2,1)}, u32[]{:S(2)}, u32[]{:S(2)}) %collective-permute-start.7) | collective-permute-done | bytes 2097184 | tf_op jit(solution)/shard_map/ppermute | solution.py:41
  288.8 16.1 %select_reduce_fusion.1 = f32[16,768]{1,0:T(8,128)S(1)} fusion(f32[16,2048]{1,0:T(8,128)S(1)} %convert_bitcast_fusion.2, s32[16,768]{1,0:T(8,128)S(1)} %get-tuple-element.319), kind=kLoop, calls=%fused_computation.2 | loop fusion | flops 75485184 | bytes 229376 | tf_op jit(solution)/shard_map/reduce_sum | solution.py:667
  304.9 4.0 copy.270.gate_ref
  308.9 4.0 pad_maximum_fusion.2.x_hbm
  312.9 75.8 %experts.4 = (bf16[8,4,3,64,512]{4,3,2,1,0:T(8,128)(2,1)}, bf16[8,4,3,64,512]{4,3,2,1,0:T(8,128)(2,1)}, bf16[2048,1024]{1,0:T(8,128)(2,1)}, bf16[2048,1024]{1,0:...) custom-call(s32[3072]{0:T(1024)} %reshape.457.table, s32[4]{0:T(128)} %get-tuple-element.333.count, ...), custom_call_target="tpu_custom_call" | custom-call | flops 1 | bytes 150000000 | tf_op jit(solution)/shard_map/experts/pallas_call | solution.py:535
  389.4 72.7 %experts.5 = (bf16[8,4,3,64,512]{4,3,2,1,0:T(8,128)(2,1)}, bf16[8,4,3,64,512]{4,3,2,1,0:T(8,128)(2,1)}, bf16[2048,1024]{1,0:T(8,128)(2,1)}, bf16[2048,1024]{1,0:...) custom-call(s32[3072]{0:T(1024)} %reshape.461.table, s32[4]{0:T(128)} %get-tuple-element.96.count, ...), custom_call_target="tpu_custom_call" | custom-call | flops 1 | bytes 150000000 | tf_op jit(solution)/shard_map/experts/pallas_call | solution.py:535
  462.2 5.9 fusion.12
  472.0 62.2 %experts.6 = (bf16[8,4,3,64,512]{4,3,2,1,0:T(8,128)(2,1)}, bf16[8,4,3,64,512]{4,3,2,1,0:T(8,128)(2,1)}, bf16[2048,1024]{1,0:T(8,128)(2,1)}, bf16[2048,1024]{1,0:...) custom-call(s32[3072]{0:T(1024)} %reshape.462.table, s32[4]{0:T(128)} %get-tuple-element.101.count, ...), custom_call_target="tpu_custom_call" | custom-call | flops 1 | bytes 150000000 | tf_op jit(solution)/shard_map/experts/pallas_call | solution.py:535
  538.9 5.9 fusion.13
  544.8 4.1 fusion.42
  564.7 57.8 %experts.7 = (bf16[8,4,3,64,512]{4,3,2,1,0:T(8,128)(2,1)}, bf16[8,4,3,64,512]{4,3,2,1,0:T(8,128)(2,1)}, bf16[2048,1024]{1,0:T(8,128)(2,1)}, bf16[2048,1024]{1,0:...) custom-call(s32[3072]{0:T(1024)} %reshape.465.table, s32[4]{0:T(128)} %get-tuple-element.109.count, ...), custom_call_target="tpu_custom_call" | custom-call | flops 1 | bytes 150000000 | tf_op jit(solution)/shard_map/experts/pallas_call | solution.py:535
  628.2 7.3 add_convert_fusion
  639.2 4.1 add_convert_fusion.1
  643.4 5.0 fusion.14
  648.5 4.0 fusion.39
  652.7 11.4 %collective-permute-start.17 = (bf16[1024,1024]{1,0:T(8,128)(2,1)S(1)}, bf16[1024,1024]{1,0:T(8,128)(2,1)S(1)}, u32[]{:S(2)}, u32[]{:S(2)}) collective-permute-start(bf16[1024,1024]{1,0:T(8,128)(2,1)S(1)} %constant_dynamic-slice_fusion.25), channel_id=1, source_target_pairs={{0,1},{1,0},{2,3},{3,2},{4,5},{5,4},{6,7},{7,6},{8,9},{9,8},{10,11... | collective-permute-start | bytes 6291464 | tf_op jit(solution)/shard_map/ppermute | solution.py:52
  664.1 15.3 %select_reduce_fusion = f32[16,2048]{1,0:T(8,128)S(1)} fusion(f32[16,768]{1,0:T(8,128)S(1)} %maximum_select_fusion, s32[16,768]{1,0:T(8,128)S(1)} %copy-done.82), kind=kLoop, calls=%fused_computation | loop fusion | flops 75464704 | bytes 229376 | tf_op jit(solution)/shard_map/reduce_sum | solution.py:699
  685.4 27.8 %collective-permute-done.18 = f32[1024,32]{0,1:T(8,128)S(1)} collective-permute-done((f32[1024,32]{0,1:T(8,128)S(1)}, f32[1024,32]{0,1:T(8,128)S(1)}, u32[]{:S(2)}, u32[]{:S(2)}) %collective-permute-start.18) | collective-permute-done | bytes 131104 | tf_op jit(solution)/shard_map/ppermute | solution.py:52
  713.2 4.0 collective-permute-start.21
  721.8 14.8 %collective-permute-done.19 = bf16[4,3,64,512]{3,2,0,1:T(8,128)(2,1)S(1)} collective-permute-done((bf16[4,3,64,512]{3,2,0,1:T(8,128)(2,1)}, bf16[4,3,64,512]{3,2,0,1:T(8,128)(2,1)S(1)}, u32[]{:S(2)}, u32[]{:S(2)}) %collective-permute-start.19) | collective-permute-done | bytes 786464 | tf_op jit(solution)/shard_map/ppermute | solution.py:138
  736.6 16.7 %collective-permute-done.21 = bf16[4,3,64,512]{3,2,0,1:T(8,128)(2,1)S(1)} collective-permute-done((bf16[4,3,64,512]{3,2,0,1:T(8,128)(2,1)}, bf16[4,3,64,512]{3,2,0,1:T(8,128)(2,1)S(1)}, u32[]{:S(2)}, u32[]{:S(2)}) %collective-permute-start.21) | collective-permute-done | bytes 786464 | tf_op jit(solution)/shard_map/ppermute | solution.py:138
  753.4 4.4 multiply_reduce_fusion
  764.0 5.1 fusion.36
  780.8 36.7 %collective-permute-done.24 = bf16[1024,1024]{1,0:T(8,128)(2,1)S(1)} collective-permute-done((bf16[1024,1024]{1,0:T(8,128)(2,1)S(1)}, bf16[1024,1024]{1,0:T(8,128)(2,1)S(1)}, u32[]{:S(2)}, u32[]{:S(2)}) %collective-permute-start.24) | collective-permute-done | bytes 2097184 | tf_op jit(solution)/shard_map/ppermute | solution.py:41
  818.6 9.1 collective-permute-done.25
  829.0 10.5 collective-permute-done.28
  839.5 4.9 convolution_convert_fusion.1.do_ref
  844.5 4.0 fusion.33
  858.8 5.9 collective-permute-start.30
  864.7 4.1 collective-permute-start.32
  868.8 50.5 %attend_back.1 = (bf16[512,2048]{1,0:T(8,128)(2,1)}, f32[4,2048,64]{2,1,0:T(8,128)}, f32[4,2048,64]{2,1,0:T(8,128)}) custom-call(s32[8]{0:T(128)} %and_select_fusion.low, bf16[512,2048]{1,0:T(8,128)(2,1)} %bitcast.207, bf16[512,2048]{1,0:T(8,128)(2,1)} %convolution_convert_fusion.1.do_ref, bf16[512,2048]{1,0:T(8,128)(2,1)} %get-tuple-element.93.o_ref, ...), custom_call_target="tpu_custom_call" | custom-call | flops 1 | bytes 150000000 | tf_op jit(solution)/shard_map/attend_back/pallas_call | solution.py:320
  919.3 6.3 convolution_convert_fusion.3
  925.6 4.5 convert_add_fusion.1
  943.6 6.4 convolution_convert_fusion.2
  950.0 8.4 fusion.4
  960.4 5.8 copy.309
  989.3 30.5 %collective-permute-done.33 = bf16[1024,1024]{1,0:T(8,128)(2,1)S(1)} collective-permute-done((bf16[1024,1024]{1,0:T(8,128)(2,1)}, bf16[1024,1024]{1,0:T(8,128)(2,1)S(1)}, u32[]{:S(2)}, u32[]{:S(2)}) %collective-permute-start.33) | collective-permute-done | bytes 2097184 | tf_op jit(solution)/shard_map/ppermute | solution.py:52
  1031.9 8.6 collective-permute-done.36
  (382 shorter events, 187.8 us)
Async XLA Ops:
  8.0 232.3 %sort.10.cloned.1.call-start = ((), (), s32[]{:S(2)}) async-start(), calls=%async_computation.1 | async-start | bytes 393248 | tf_op jit(solution)/shard_map/jit(sort)/sort | solution.py:643
  10.3 302.6 %all-gather.2.cloned.1.call-start = ((), (), s32[]{:S(2)}) async-start(), calls=%async_computation | async-start | bytes 53477376 | tf_op jit(solution)/shard_map/all_gather | solution.py:618
  14.9 11.2 %collective-permute-start = (bf16[64,1664]{1,0:T(8,128)(2,1)S(1)}, bf16[64,1664]{1,0:T(8,128)(2,1)S(1)}, u32[]{:S(2)}, u32[]{:S(2)}) collective-permute-start(bf16[64,1664]{1,0:T(8,128)(2,1)S(1)} %pad.8), channel_id=1, source_target_pairs={{0,8},{2,10},{4,12},{6,14},{8,16},{10,18},{12,20},{14,22},{16,24},... | collective-permute-start | bytes 638984 | tf_op jit(solution)/shard_map/ppermute | solution.py:87
  18.0 15.6 %collective-permute-start.1 = (bf16[64,1664]{1,0:T(8,128)(2,1)S(1)}, bf16[64,1664]{1,0:T(8,128)(2,1)S(1)}, u32[]{:S(2)}, u32[]{:S(2)}) collective-permute-start(bf16[64,1664]{1,0:T(8,128)(2,1)S(1)} %pad.8), channel_id=1, source_target_pairs={{0,24},{2,26},{4,28},{6,30},{8,0},{10,2},{12,4},{14,6},{16,8},{18,... | collective-permute-start | bytes 638984 | tf_op jit(solution)/shard_map/ppermute | solution.py:87
  20.1 27.1 %collective-permute-start.2 = (bf16[64,1664]{1,0:T(8,128)(2,1)S(1)}, bf16[64,1664]{1,0:T(8,128)(2,1)S(1)}, u32[]{:S(2)}, u32[]{:S(2)}) collective-permute-start(bf16[64,1664]{1,0:T(8,128)(2,1)S(1)} %pad.8), channel_id=1, source_target_pairs={{0,16},{2,18},{4,20},{6,22},{8,24},{10,26},{12,28},{14,30},{16,0},... | collective-permute-start | bytes 638984 | tf_op jit(solution)/shard_map/ppermute | solution.py:87
  21.0 66.8 %collective-permute-start.5 = (bf16[1024,1024]{1,0:T(8,128)(2,1)S(1)}, bf16[1024,1024]{1,0:T(8,128)(2,1)}, u32[]{:S(2)}, u32[]{:S(2)}) collective-permute-start(bf16[1024,1024]{1,0:T(8,128)(2,1)S(1)} %copy-done.4), channel_id=1, source_target_pairs={{0,1},{1,0},{2,3},{3,2},{4,5},{5,4},{6,7},{7,6},{8,9},{9,8},{10,11... | collective-permute-start | bytes 6291464 | tf_op jit(solution)/shard_map/ppermute | solution.py:41
  22.5 90.1 %collective-permute-start.8 = (bf16[1024,1024]{1,0:T(8,128)(2,1)}, bf16[1024,1024]{1,0:T(8,128)(2,1)}, u32[]{:S(2)}, u32[]{:S(2)}) collective-permute-start(bf16[1024,1024]{1,0:T(8,128)(2,1)} %param.27), channel_id=1, source_target_pairs={{0,1},{1,0},{2,3},{3,2},{4,5},{5,4},{6,7},{7,6},{8,9},{9,8},{10,11... | collective-permute-start | bytes 6291464 | tf_op jit(solution)/shard_map/ppermute | solution.py:41
  47.2 39.7 %collective-permute-start.3 = (bf16[4,64,1664]{2,1,0:T(8,128)(2,1)S(1)}, bf16[4,64,1664]{2,1,0:T(8,128)(2,1)S(1)}, u32[]{:S(2)}, u32[]{:S(2)}) collective-permute-start(bf16[4,64,1664]{2,1,0:T(8,128)(2,1)S(1)} %bitcast_dynamic-update-slice_fusion.4), channel_id=1, source_target_pairs={{0,4},{2,6},{4,0},{6,2},{8,12},{10,14},{12,8},{14,10},{16,20},{18,... | collective-permute-start | bytes 2555912 | tf_op jit(solution)/shard_map/ppermute | solution.py:89
  50.5 76.7 %copy-start.33 = (f32[32,2048]{1,0:T(8,128)}, f32[32,2048]{1,0:T(8,128)S(1)}, u32[]{:S(2)}) copy-start(f32[32,2048]{1,0:T(8,128)S(1)} %get-tuple-element.328.sin_ref) | copy-start | bytes 786436
  50.5 78.9 %copy-start.22 = (f32[32,2048]{1,0:T(8,128)}, f32[32,2048]{1,0:T(8,128)S(1)}, u32[]{:S(2)}) copy-start(f32[32,2048]{1,0:T(8,128)S(1)} %get-tuple-element.329.cos_ref) | copy-start | bytes 786436
  87.1 30.4 %collective-permute-start.4 = (bf16[2,4,64,1664]{3,2,0,1:T(8,128)(2,1)S(1)}, bf16[2,4,64,1664]{3,2,0,1:T(8,128)(2,1)S(1)}, u32[]{:S(2)}, u32[]{:S(2)}) collective-permute-start(bf16[2,4,64,1664]{3,2,0,1:T(8,128)(2,1)S(1)} %bitcast_dynamic-update-slice_fusion.3), channel_id=1, source_target_pairs={{0,2},{2,0},{4,6},{6,4},{8,10},{10,8},{12,14},{14,12},{16,18},{18,... | collective-permute-start | bytes 5111816 | tf_op jit(solution)/shard_map/ppermute | solution.py:90
  186.3 46.2 %collective-permute-start.6 = (bf16[1024,1024]{1,0:T(8,128)(2,1)}, bf16[1024,1024]{1,0:T(8,128)(2,1)}, u32[]{:S(2)}, u32[]{:S(2)}) collective-permute-start(bf16[1024,1024]{1,0:T(8,128)(2,1)} %constant_dynamic-slice_fusion.44), channel_id=1, source_target_pairs={{0,1},{1,0},{2,3},{3,2},{4,5},{5,4},{6,7},{7,6},{8,9},{9,8},{10,11... | collective-permute-start | bytes 6291464 | tf_op jit(solution)/shard_map/ppermute | solution.py:52
  237.8 45.1 %collective-permute-start.7 = (bf16[1024,1024]{1,0:T(8,128)(2,1)S(1)}, bf16[1024,1024]{1,0:T(8,128)(2,1)}, u32[]{:S(2)}, u32[]{:S(2)}) collective-permute-start(bf16[1024,1024]{1,0:T(8,128)(2,1)S(1)} %multiply_convert_fusion), channel_id=1, source_target_pairs={{0,1},{1,0},{2,3},{3,2},{4,5},{5,4},{6,7},{7,6},{8,9},{9,8},{10,11... | collective-permute-start | bytes 6291464 | tf_op jit(solution)/shard_map/ppermute | solution.py:41
  241.1 47.7 %copy-start.81 = (s32[16,768]{1,0:T(8,128)}, s32[16,768]{1,0:T(8,128)S(1)}, u32[]{:S(2)}) copy-start(s32[16,768]{1,0:T(8,128)S(1)} %get-tuple-element.319) | copy-start | bytes 147460
  241.7 41.2 %copy-start.1 = (f32[1024,1024]{1,0:T(8,128)S(1)}, f32[1024,1024]{1,0:T(8,128)}, u32[]{:S(2)}) copy-start(f32[1024,1024]{1,0:T(8,128)} %copy-done) | copy-start | bytes 12582916
  388.7 73.4 %collective-permute-start.9 = (bf16[8,4,3,64,512]{4,3,2,1,0:T(8,128)(2,1)}, bf16[8,4,3,64,512]{4,3,2,1,0:T(8,128)(2,1)}, u32[]{:S(2)}, u32[]{:S(2)}) collective-permute-start(bf16[8,4,3,64,512]{4,3,2,1,0:T(8,128)(2,1)} %get-tuple-element.99), channel_id=1, source_target_pairs={{0,2},{2,0},{4,6},{6,4},{8,10},{10,8},{12,14},{14,12},{16,18},{18,... | collective-permute-start | bytes 18874376 | tf_op jit(solution)/shard_map/ppermute | solution.py:138
  468.1 70.8 %collective-permute-start.11 = (bf16[8,4,3,64,512]{4,3,2,1,0:T(8,128)(2,1)}, bf16[8,4,3,64,512]{4,3,2,1,0:T(8,128)(2,1)}, u32[]{:S(2)}, u32[]{:S(2)}) collective-permute-start(bf16[8,4,3,64,512]{4,3,2,1,0:T(8,128)(2,1)} %get-tuple-element.104), channel_id=1, source_target_pairs={{0,2},{2,0},{4,6},{6,4},{8,10},{10,8},{12,14},{14,12},{16,18},{18,... | collective-permute-start | bytes 18874376 | tf_op jit(solution)/shard_map/ppermute | solution.py:138
  468.1 70.8 %collective-permute-start.10 = (bf16[4,4,3,64,512]{4,3,1,2,0:T(8,128)(2,1)}, bf16[4,4,3,64,512]{4,3,1,2,0:T(8,128)(2,1)}, u32[]{:S(2)}, u32[]{:S(2)}) collective-permute-start(bf16[4,4,3,64,512]{4,3,1,2,0:T(8,128)(2,1)} %fusion.12), channel_id=1, source_target_pairs={{0,4},{2,6},{4,0},{6,2},{8,12},{10,14},{12,8},{14,10},{16,20},{18,... | collective-permute-start | bytes 9437192 | tf_op jit(solution)/shard_map/ppermute | solution.py:138
  549.0 94.4 %collective-permute-start.16 = (bf16[8,4,3,64,512]{4,3,2,1,0:T(8,128)(2,1)}, bf16[8,4,3,64,512]{4,3,2,1,0:T(8,128)(2,1)}, u32[]{:S(2)}, u32[]{:S(2)}) collective-permute-start(bf16[8,4,3,64,512]{4,3,2,1,0:T(8,128)(2,1)} %get-tuple-element.123), channel_id=1, source_target_pairs={{0,2},{2,0},{4,6},{6,4},{8,10},{10,8},{12,14},{14,12},{16,18},{18,... | collective-permute-start | bytes 18874376 | tf_op jit(solution)/shard_map/ppermute | solution.py:138
  551.8 91.6 %collective-permute-start.15 = (bf16[4,4,3,64,512]{4,3,1,2,0:T(8,128)(2,1)}, bf16[4,4,3,64,512]{4,3,1,2,0:T(8,128)(2,1)}, u32[]{:S(2)}, u32[]{:S(2)}) collective-permute-start(bf16[4,4,3,64,512]{4,3,1,2,0:T(8,128)(2,1)} %fusion.13), channel_id=1, source_target_pairs={{0,4},{2,6},{4,0},{6,2},{8,12},{10,14},{12,8},{14,10},{16,20},{18,... | collective-permute-start | bytes 9437192 | tf_op jit(solution)/shard_map/ppermute | solution.py:138
  558.9 84.4 %collective-permute-start.12 = (bf16[4,3,64,512]{3,2,0,1:T(8,128)(2,1)}, bf16[4,3,64,512]{3,2,0,1:T(8,128)(2,1)}, u32[]{:S(2)}, u32[]{:S(2)}) collective-permute-start(bf16[4,3,64,512]{3,2,0,1:T(8,128)(2,1)} %get-tuple-element.119), channel_id=1, source_target_pairs={{0,16},{2,18},{4,20},{6,22},{8,24},{10,26},{12,28},{14,30},{16,0},... | collective-permute-start | bytes 2359304 | tf_op jit(solution)/shard_map/ppermute | solution.py:138
  560.8 82.5 %collective-permute-start.13 = (bf16[4,3,64,512]{3,2,0,1:T(8,128)(2,1)}, bf16[4,3,64,512]{3,2,0,1:T(8,128)(2,1)}, u32[]{:S(2)}, u32[]{:S(2)}) collective-permute-start(bf16[4,3,64,512]{3,2,0,1:T(8,128)(2,1)} %get-tuple-element.120), channel_id=1, source_target_pairs={{0,8},{2,10},{4,12},{6,14},{8,16},{10,18},{12,20},{14,22},{16,24},... | collective-permute-start | bytes 2359304 | tf_op jit(solution)/shard_map/ppermute | solution.py:138
  560.8 82.5 %collective-permute-start.14 = (bf16[4,3,64,512]{3,2,0,1:T(8,128)(2,1)}, bf16[4,3,64,512]{3,2,0,1:T(8,128)(2,1)}, u32[]{:S(2)}, u32[]{:S(2)}) collective-permute-start(bf16[4,3,64,512]{3,2,0,1:T(8,128)(2,1)} %get-tuple-element.121), channel_id=1, source_target_pairs={{0,24},{2,26},{4,28},{6,30},{8,0},{10,2},{12,4},{14,6},{16,8},{18,... | collective-permute-start | bytes 2359304 | tf_op jit(solution)/shard_map/ppermute | solution.py:138
  635.5 212.9 %copy-start.6 = (bf16[2048,1024]{1,0:T(8,128)(2,1)}, bf16[2048,1024]{1,0:T(8,128)(2,1)S(1)}, u32[]{:S(2)}) copy-start(bf16[2048,1024]{1,0:T(8,128)(2,1)S(1)} %add_convert_fusion) | copy-start | bytes 12582916
  652.5 100.8 %collective-permute-start.23 = (bf16[8,4,3,64,512]{4,3,2,1,0:T(8,128)(2,1)}, bf16[8,4,3,64,512]{4,3,2,1,0:T(8,128)(2,1)S(1)}, u32[]{:S(2)}, u32[]{:S(2)}) collective-permute-start(bf16[8,4,3,64,512]{4,3,2,1,0:T(8,128)(2,1)} %get-tuple-element.135), channel_id=1, source_target_pairs={{0,2},{2,0},{4,6},{6,4},{8,10},{10,8},{12,14},{14,12},{16,18},{18,... | collective-permute-start | bytes 18874376 | tf_op jit(solution)/shard_map/ppermute | solution.py:138
  652.7 60.5 %collective-permute-start.17 = (bf16[1024,1024]{1,0:T(8,128)(2,1)S(1)}, bf16[1024,1024]{1,0:T(8,128)(2,1)S(1)}, u32[]{:S(2)}, u32[]{:S(2)}) collective-permute-start(bf16[1024,1024]{1,0:T(8,128)(2,1)S(1)} %constant_dynamic-slice_fusion.25), channel_id=1, source_target_pairs={{0,1},{1,0},{2,3},{3,2},{4,5},{5,4},{6,7},{7,6},{8,9},{9,8},{10,11... | collective-permute-start | bytes 6291464 | tf_op jit(solution)/shard_map/ppermute | solution.py:52
  664.1 89.2 %collective-permute-start.22 = (bf16[4,4,3,64,512]{4,3,1,2,0:T(8,128)(2,1)}, bf16[4,4,3,64,512]{4,3,1,2,0:T(8,128)(2,1)}, u32[]{:S(2)}, u32[]{:S(2)}) collective-permute-start(bf16[4,4,3,64,512]{4,3,1,2,0:T(8,128)(2,1)} %fusion.14), channel_id=1, source_target_pairs={{0,4},{2,6},{4,0},{6,2},{8,12},{10,14},{12,8},{14,10},{16,20},{18,... | collective-permute-start | bytes 9437192 | tf_op jit(solution)/shard_map/ppermute | solution.py:138
  679.5 33.7 %collective-permute-start.18 = (f32[1024,32]{0,1:T(8,128)S(1)}, f32[1024,32]{0,1:T(8,128)S(1)}, u32[]{:S(2)}, u32[]{:S(2)}) collective-permute-start(f32[1024,32]{0,1:T(8,128)S(1)} %constant_dynamic-slice_fusion.24), channel_id=1, source_target_pairs={{0,1},{1,0},{2,3},{3,2},{4,5},{5,4},{6,7},{7,6},{8,9},{9,8},{10,11... | collective-permute-start | bytes 393224 | tf_op jit(solution)/shard_map/ppermute | solution.py:52
  681.8 54.7 %collective-permute-start.19 = (bf16[4,3,64,512]{3,2,0,1:T(8,128)(2,1)}, bf16[4,3,64,512]{3,2,0,1:T(8,128)(2,1)S(1)}, u32[]{:S(2)}, u32[]{:S(2)}) collective-permute-start(bf16[4,3,64,512]{3,2,0,1:T(8,128)(2,1)} %get-tuple-element.131), channel_id=1, source_target_pairs={{0,16},{2,18},{4,20},{6,22},{8,24},{10,26},{12,28},{14,30},{16,0},... | collective-permute-start | bytes 2359304 | tf_op jit(solution)/shard_map/ppermute | solution.py:138
  713.2 23.4 %collective-permute-start.20 = (bf16[4,3,64,512]{3,2,0,1:T(8,128)(2,1)}, bf16[4,3,64,512]{3,2,0,1:T(8,128)(2,1)S(1)}, u32[]{:S(2)}, u32[]{:S(2)}) collective-permute-start(bf16[4,3,64,512]{3,2,0,1:T(8,128)(2,1)} %get-tuple-element.132), channel_id=1, source_target_pairs={{0,8},{2,10},{4,12},{6,14},{8,16},{10,18},{12,20},{14,22},{16,24},... | collective-permute-start | bytes 2359304 | tf_op jit(solution)/shard_map/ppermute | solution.py:138
  713.2 40.1 %collective-permute-start.21 = (bf16[4,3,64,512]{3,2,0,1:T(8,128)(2,1)}, bf16[4,3,64,512]{3,2,0,1:T(8,128)(2,1)S(1)}, u32[]{:S(2)}, u32[]{:S(2)}) collective-permute-start(bf16[4,3,64,512]{3,2,0,1:T(8,128)(2,1)} %get-tuple-element.133), channel_id=1, source_target_pairs={{0,24},{2,26},{4,28},{6,30},{8,0},{10,2},{12,4},{14,6},{16,8},{18,... | collective-permute-start | bytes 2359304 | tf_op jit(solution)/shard_map/ppermute | solution.py:138
  769.1 70.3 %collective-permute-start.28 = (bf16[4,4,3,64,512]{4,3,1,2,0:T(8,128)(2,1)}, bf16[4,4,3,64,512]{4,3,1,2,0:T(8,128)(2,1)}, u32[]{:S(2)}, u32[]{:S(2)}) collective-permute-start(bf16[4,4,3,64,512]{4,3,1,2,0:T(8,128)(2,1)} %fusion.15), channel_id=1, source_target_pairs={{0,4},{2,6},{4,0},{6,2},{8,12},{10,14},{12,8},{14,10},{16,20},{18,... | collective-permute-start | bytes 9437192 | tf_op jit(solution)/shard_map/ppermute | solution.py:138
  770.3 47.3 %collective-permute-start.24 = (bf16[1024,1024]{1,0:T(8,128)(2,1)S(1)}, bf16[1024,1024]{1,0:T(8,128)(2,1)S(1)}, u32[]{:S(2)}, u32[]{:S(2)}) collective-permute-start(bf16[1024,1024]{1,0:T(8,128)(2,1)S(1)} %get-tuple-element.141), channel_id=1, source_target_pairs={{0,1},{1,0},{2,3},{3,2},{4,5},{5,4},{6,7},{7,6},{8,9},{9,8},{10,11... | collective-permute-start | bytes 6291464 | tf_op jit(solution)/shard_map/ppermute | solution.py:41
  773.4 54.2 %collective-permute-start.25 = (bf16[4,3,64,512]{3,2,0,1:T(8,128)(2,1)}, bf16[4,3,64,512]{3,2,0,1:T(8,128)(2,1)S(1)}, u32[]{:S(2)}, u32[]{:S(2)}) collective-permute-start(bf16[4,3,64,512]{3,2,0,1:T(8,128)(2,1)} %get-tuple-element.142), channel_id=1, source_target_pairs={{0,16},{2,18},{4,20},{6,22},{8,24},{10,26},{12,28},{14,30},{16,0},... | collective-permute-start | bytes 2359304 | tf_op jit(solution)/shard_map/ppermute | solution.py:138
  775.5 52.2 %collective-permute-start.26 = (bf16[4,3,64,512]{3,2,0,1:T(8,128)(2,1)}, bf16[4,3,64,512]{3,2,0,1:T(8,128)(2,1)S(1)}, u32[]{:S(2)}, u32[]{:S(2)}) collective-permute-start(bf16[4,3,64,512]{3,2,0,1:T(8,128)(2,1)} %get-tuple-element.143), channel_id=1, source_target_pairs={{0,8},{2,10},{4,12},{6,14},{8,16},{10,18},{12,20},{14,22},{16,24},... | collective-permute-start | bytes 2359304 | tf_op jit(solution)/shard_map/ppermute | solution.py:138
  776.9 52.1 %collective-permute-start.27 = (bf16[4,3,64,512]{3,2,0,1:T(8,128)(2,1)}, bf16[4,3,64,512]{3,2,0,1:T(8,128)(2,1)S(1)}, u32[]{:S(2)}, u32[]{:S(2)}) collective-permute-start(bf16[4,3,64,512]{3,2,0,1:T(8,128)(2,1)} %get-tuple-element.144), channel_id=1, source_target_pairs={{0,24},{2,26},{4,28},{6,30},{8,0},{10,2},{12,4},{14,6},{16,8},{18,... | collective-permute-start | bytes 2359304 | tf_op jit(solution)/shard_map/ppermute | solution.py:138
  849.9 75.6 %collective-permute-start.29 = (bf16[1024,1024]{1,0:T(8,128)(2,1)}, bf16[1024,1024]{1,0:T(8,128)(2,1)}, u32[]{:S(2)}, u32[]{:S(2)}) collective-permute-start(bf16[1024,1024]{1,0:T(8,128)(2,1)} %constant_dynamic-slice_fusion.9), channel_id=1, source_target_pairs={{0,1},{1,0},{2,3},{3,2},{4,5},{5,4},{6,7},{7,6},{8,9},{9,8},{10,11... | collective-permute-start | bytes 6291464 | tf_op jit(solution)/shard_map/ppermute | solution.py:52
  858.8 71.3 %collective-permute-start.30 = (bf16[4,3,64,512]{3,2,0,1:T(8,128)(2,1)}, bf16[4,3,64,512]{3,2,0,1:T(8,128)(2,1)}, u32[]{:S(2)}, u32[]{:S(2)}) collective-permute-start(bf16[4,3,64,512]{3,2,0,1:T(8,128)(2,1)} %get-tuple-element.155), channel_id=1, source_target_pairs={{0,16},{2,18},{4,20},{6,22},{8,24},{10,26},{12,28},{14,30},{16,0},... | collective-permute-start | bytes 2359304 | tf_op jit(solution)/shard_map/ppermute | solution.py:138
  864.7 65.4 %collective-permute-start.31 = (bf16[4,3,64,512]{3,2,0,1:T(8,128)(2,1)}, bf16[4,3,64,512]{3,2,0,1:T(8,128)(2,1)}, u32[]{:S(2)}, u32[]{:S(2)}) collective-permute-start(bf16[4,3,64,512]{3,2,0,1:T(8,128)(2,1)} %get-tuple-element.156), channel_id=1, source_target_pairs={{0,8},{2,10},{4,12},{6,14},{8,16},{10,18},{12,20},{14,22},{16,24},... | collective-permute-start | bytes 2359304 | tf_op jit(solution)/shard_map/ppermute | solution.py:138
  864.7 65.4 %collective-permute-start.32 = (bf16[4,3,64,512]{3,2,0,1:T(8,128)(2,1)}, bf16[4,3,64,512]{3,2,0,1:T(8,128)(2,1)}, u32[]{:S(2)}, u32[]{:S(2)}) collective-permute-start(bf16[4,3,64,512]{3,2,0,1:T(8,128)(2,1)} %get-tuple-element.157), channel_id=1, source_target_pairs={{0,24},{2,26},{4,28},{6,30},{8,0},{10,2},{12,4},{14,6},{16,8},{18,... | collective-permute-start | bytes 2359304 | tf_op jit(solution)/shard_map/ppermute | solution.py:138
  969.9 15.9 %collective-permute-start.34 = (bf16[8,64,1664]{2,1,0:T(8,128)(2,1)}, bf16[8,64,1664]{2,1,0:T(8,128)(2,1)}, u32[]{:S(2)}, u32[]{:S(2)}) collective-permute-start(bf16[8,64,1664]{2,1,0:T(8,128)(2,1)} %get-tuple-element.296), channel_id=1, source_target_pairs={{0,2},{2,0},{4,6},{6,4},{8,10},{10,8},{12,14},{14,12},{16,18},{18,... | collective-permute-start | bytes 5111816 | tf_op jit(solution)/shard_map/ppermute | solution.py:138
  971.5 48.2 %collective-permute-start.33 = (bf16[1024,1024]{1,0:T(8,128)(2,1)}, bf16[1024,1024]{1,0:T(8,128)(2,1)S(1)}, u32[]{:S(2)}, u32[]{:S(2)}) collective-permute-start(bf16[1024,1024]{1,0:T(8,128)(2,1)} %constant_dynamic-slice_fusion.8), channel_id=1, source_target_pairs={{0,1},{1,0},{2,3},{3,2},{4,5},{5,4},{6,7},{7,6},{8,9},{9,8},{10,11... | collective-permute-start | bytes 6291464 | tf_op jit(solution)/shard_map/ppermute | solution.py:52
  987.2 33.5 %collective-permute-start.35 = (bf16[4,64,1664]{2,1,0:T(8,128)(2,1)S(1)}, bf16[4,64,1664]{2,1,0:T(8,128)(2,1)S(1)}, u32[]{:S(2)}, u32[]{:S(2)}) collective-permute-start(bf16[4,64,1664]{2,1,0:T(8,128)(2,1)S(1)} %fusion.47), channel_id=1, source_target_pairs={{0,4},{2,6},{4,0},{6,2},{8,12},{10,14},{12,8},{14,10},{16,20},{18,... | collective-permute-start | bytes 2555912 | tf_op jit(solution)/shard_map/ppermute | solution.py:138
  989.3 39.6 %dynamic-slice-start = ((f32[2048]{0:T(1024)}, s32[]{:T(128)}), f32[1024]{0:T(1024)S(1)}, s32[]{:S(2)}) async-start(f32[2048]{0:T(1024)} %copy-done.79, s32[]{:T(128)} %select_n.389), calls=%async_computation.7 | async-start | bytes 8704 | tf_op jit(solution)/shard_map/dynamic-slice.80
  1022.2 18.2 %collective-permute-start.36 = (bf16[64,1664]{1,0:T(8,128)(2,1)S(1)}, bf16[64,1664]{1,0:T(8,128)(2,1)S(1)}, u32[]{:S(2)}, u32[]{:S(2)}) collective-permute-start(bf16[64,1664]{1,0:T(8,128)(2,1)S(1)} %get-tuple-element.284), channel_id=1, source_target_pairs={{0,16},{2,18},{4,20},{6,22},{8,24},{10,26},{12,28},{14,30},{16,0},... | collective-permute-start | bytes 638984 | tf_op jit(solution)/shard_map/ppermute | solution.py:138
  1025.0 15.4 %collective-permute-start.37 = (bf16[64,1664]{1,0:T(8,128)(2,1)S(1)}, bf16[64,1664]{1,0:T(8,128)(2,1)S(1)}, u32[]{:S(2)}, u32[]{:S(2)}) collective-permute-start(bf16[64,1664]{1,0:T(8,128)(2,1)S(1)} %get-tuple-element.286), channel_id=1, source_target_pairs={{0,8},{2,10},{4,12},{6,14},{8,16},{10,18},{12,20},{14,22},{16,24},... | collective-permute-start | bytes 638984 | tf_op jit(solution)/shard_map/ppermute | solution.py:138
  1025.9 14.6 %collective-permute-start.38 = (bf16[64,1664]{1,0:T(8,128)(2,1)S(1)}, bf16[64,1664]{1,0:T(8,128)(2,1)S(1)}, u32[]{:S(2)}, u32[]{:S(2)}) collective-permute-start(bf16[64,1664]{1,0:T(8,128)(2,1)S(1)} %get-tuple-element.285), channel_id=1, source_target_pairs={{0,24},{2,26},{4,28},{6,30},{8,0},{10,2},{12,4},{14,6},{16,8},{18,... | collective-permute-start | bytes 638984 | tf_op jit(solution)/shard_map/ppermute | solution.py:138
  1042.3 3.9 collective-permute-start.39
  (91 other events, 742.9 us)
Sparse Core Ops, SparseCore 0:
  11.9 4.6 sort.12.cloned.1.call-done
  (1 shorter events, 0.0 us)
Sparse Core Ops, SparseCore 1:
  13.9 267.4 all-gather.1

commit v2 on v1

--- a/solution.py
+++ b/solution.py
@@ -43,6 +43,19 @@
     return jnp.concatenate([jnp.where(first, x, other), jnp.where(first, other, x)], axis=0)
 
 
+def swap_rows(x):
+    if lax.axis_size("tensor") != 2:
+        return lax.all_gather(x, "tensor", axis=0, tiled=True)
+    return lax.ppermute(x, "tensor", [(0, 1), (1, 0)])
+
+
+def join_rows(x, swapped):
+    if lax.axis_size("tensor") != 2:
+        return swapped
+    first = lax.axis_index("tensor") == 0
+    return jnp.concatenate([jnp.where(first, x, swapped), jnp.where(first, swapped, x)], axis=0)
+
+
 def scatter_rows(x, axis="tensor"):
     n = lax.axis_size(axis)
     rows = x.shape[0] // n
@@ -105,6 +118,17 @@
         self.by_hand = z_core_shape(lax.axis_size("dp")) is not None
         self.keep, self.send = keep, send
         self.stage = 0
+
+    def split(self, *sizes):
+        if not self.by_hand or sum(sizes) != self.keep.shape[1]:
+            return [self] + [None] * (len(sizes) - 1)
+        parts = []
+        for i, size in enumerate(sizes):
+            run = slice(sum(sizes[:i]), sum(sizes[:i]) + size)
+            part = Reduce(self.keep[:, run], None)
+            part.core, part.stage = self.core[:, run], 1
+            parts.append(part)
+        return parts
 
     def sends(self):
         if not self.by_hand:
@@ -162,6 +186,7 @@
 
 
 def phase(work, inputs, reduces):
+    reduces = [r for r in reduces if r is not None]
     sends = [r.sends() for r in reduces]
     (inputs, sends) = lax.optimization_barrier((list(inputs), sends))
     results = work(*inputs)
@@ -267,15 +292,15 @@
 
 def attend_back_kernel(
     low, q_ref, do_ref, o_ref, lse_ref, k_ref, v_ref, kt_ref, start_ref, cos_ref, sin_ref,
-    dq_ref, dk_ref, dv_ref,
+    dq_ref, dk_ref, dv_ref, dk_sum, dv_sum,
 ):
     i = pl.program_id(1)
     bq = BLOCK
 
     @pl.when(i == 0)
     def _():
-        dk_ref[...] = jnp.zeros_like(dk_ref)
-        dv_ref[...] = jnp.zeros_like(dv_ref)
+        dk_sum[...] = jnp.zeros_like(dk_sum)
+        dv_sum[...] = jnp.zeros_like(dv_sum)
 
     def side(a):
         return jnp.concatenate([a[:HEAD_SIZE], a[HEAD_SIZE:]], axis=1)
@@ -294,20 +319,29 @@
         p = jnp.where(mask_of(start, j, i, bq), jnp.exp(s - lse), 0.0)
         dp = dot(v_ref[0, at_key, :], dos, 1, 0)
         ds = (p * (dp - inner)).astype(BF16)
-        dv_ref[0, at_key, :] += dot(p.astype(BF16), dos, 1, 1)
-        dk_ref[0, at_key, :] += dot(ds, qs, 1, 1)
+        dv_sum[:, at_key] += dot(dos, p.astype(BF16), 1, 1)
+        dk_sum[:, at_key] += dot(qs, ds, 1, 1)
         return dq + dot(kt_ref[:, at_key], ds, 1, 0)
 
     dq = lax.fori_loop(low[i], i + 1, step, jnp.zeros((HEAD_SIZE, 2 * bq), F32))
     dq = dq * HEAD_SIZE ** (-0.5)
-    cosine, sine = cos_ref[...], sin_ref[...]
+    here = pl.ds(pl.multiple_of(i * bq, bq), bq)
+
+    def turn_back(v, cosine, sine):
+        one, two = v[:HALF], v[HALF:]
+        return jnp.concatenate(
+            [one * cosine + two * sine, two * cosine - one * sine], axis=0
+        ).astype(BF16)
+
     for h in range(2):
-        one = dq[:HALF, h * bq : (h + 1) * bq]
-        two = dq[HALF:, h * bq : (h + 1) * bq]
-        dq_ref[h * HEAD_SIZE : h * HEAD_SIZE + HALF, :] = (one * cosine + two * sine).astype(BF16)
-        dq_ref[h * HEAD_SIZE + HALF : (h + 1) * HEAD_SIZE, :] = (
-            two * cosine - one * sine
-        ).astype(BF16)
+        dq_ref[h * HEAD_SIZE : (h + 1) * HEAD_SIZE, :] = turn_back(
+            dq[:, h * bq : (h + 1) * bq], cos_ref[:, here], sin_ref[:, here]
+        )
+
+    @pl.when(i == pl.num_programs(1) - 1)
+    def _():
+        dk_ref[...] = turn_back(dk_sum[...], cos_ref[...], sin_ref[...])
+        dv_ref[...] = dv_sum[...].astype(BF16)
 
 
 def attend_back(first, heads, q_t, do_t, o_t, lse, k, v, k_t, start, cosine, sine, low):
@@ -315,8 +349,8 @@
     blocks = rows // BLOCK
     pair = pl.BlockSpec((2 * HEAD_SIZE, BLOCK), lambda h, i, low: (h + first, i))
     whole = pl.BlockSpec((1, rows, HEAD_SIZE), lambda h, i, low: (h + first, 0, 0))
-    table = pl.BlockSpec((HALF, BLOCK), lambda h, i, low: (0, i))
-    grad = pl.BlockSpec((1, rows, HEAD_SIZE), lambda h, i, low: (h, 0, 0))
+    table = pl.BlockSpec((HALF, rows), lambda h, i, low: (0, 0))
+    grad = pl.BlockSpec((HEAD_SIZE, rows), lambda h, i, low: (h, 0))
     return pl.pallas_call(
         attend_back_kernel,
         grid_spec=pltpu.PrefetchScalarGridSpec(
@@ -337,11 +371,14 @@
             out_specs=[
                 pl.BlockSpec((2 * HEAD_SIZE, BLOCK), lambda h, i, low: (h, i)), grad, grad,
             ],
+            scratch_shapes=[
+                pltpu.VMEM((HEAD_SIZE, rows), F32), pltpu.VMEM((HEAD_SIZE, rows), F32),
+            ],
         ),
         out_shape=[
             jax.ShapeDtypeStruct((heads * 2 * HEAD_SIZE, rows), BF16),
-            jax.ShapeDtypeStruct((heads, rows, HEAD_SIZE), F32),
-            jax.ShapeDtypeStruct((heads, rows, HEAD_SIZE), F32),
+            jax.ShapeDtypeStruct((heads * HEAD_SIZE, rows), BF16),
+            jax.ShapeDtypeStruct((heads * HEAD_SIZE, rows), BF16),
         ],
         cost_estimate=KERNEL_COST,
         name="attend_back",
@@ -619,7 +656,6 @@
     big = big.reshape((dp,) + big_shard.shape)
 
     inputs_all = gather_rows(tokens)
-    grad_all = gather_rows(cotangent)
 
     seq = lengths[0]
     order = jnp.arange(seq.shape[0], dtype=jnp.int32)
@@ -642,6 +678,10 @@
     count = jnp.sum(member.astype(jnp.int32), axis=1)
     table = jnp.sort(jnp.where(member, row_index[None, :], rows), axis=1)[:, :CAP]
     filled = jnp.arange(CAP, dtype=jnp.int32)[None, :] < count[:, None]
+    is_high = (
+        table[:, :, None] // 128 == jnp.arange(rows // 128, dtype=jnp.int32)[None, None, :]
+    ).astype(BF16)
+    is_low = table[:, :, None] % 128 == jnp.arange(128, dtype=jnp.int32)[None, None, :]
 
     normed_all, inverse_all = rms_norm(inputs_all.astype(F32), gain_one)
     hidden_one = normed_all.astype(BF16)
@@ -653,7 +693,11 @@
     v_t = qkv[d_q + d_k :].astype(BF16)
     k = jnp.transpose(k_t.reshape(kv_heads, HEAD_SIZE, rows), (0, 2, 1))
     v = jnp.transpose(v_t.reshape(kv_heads, HEAD_SIZE, rows), (0, 2, 1))
-    o_t, lse = attend(q_t, k, v_t, start, low)
+    o_t, lse, swapped = phase(
+        lambda q_t, sent: list(attend(q_t, k, v_t, start, low)) + [swap_rows(sent)],
+        [q_t, cotangent], [],
+    )
+    grad_all = join_rows(cotangent, swapped)
     inputs_f = tokens.astype(F32)
     residual_two = inputs_f + scatter_rows(dot(o_t, out_weight_t, 0, 1).astype(BF16))
 
@@ -663,12 +707,13 @@
     logits = jnp.where(member_all, dot(hidden_two, router_weight, 1, 0), NEG)
     gates_f = jax.nn.softmax(logits, axis=-1)
     share = lax.dynamic_slice_in_dim(gates_f, rank * expert_local, expert_local, 1)
-    share_t = share.astype(BF16).astype(F32).T
-    slot_gate = jnp.sum(
-        jnp.where(table[:, :, None] == row_index[None, None, :], share_t[:, None, :], 0.0), axis=2
-    )[:, :, None]
-
-    calls = EXPERT_CALLS
+    picked = jnp.einsum(
+        "esh,ehl->esl", is_high, share.astype(BF16).T.reshape(expert_local, rows // 128, 128),
+        preferred_element_type=F32,
+    )
+    slot_gate = jnp.sum(jnp.where(is_low, picked, 0.0), axis=2, keepdims=True)
+
+    calls = min(EXPERT_CALLS, expert_local)
     each = expert_local // calls
     parity = (me % 2).astype(jnp.int32).reshape(1)
     slots = table * (width // 128)
@@ -693,20 +738,24 @@
         dx_part = dx_part + dx_p.astype(F32)
         dg.append(dg_p[:, :, 0])
 
+    two_a, two_b = sums[2].split(3, 1)
+
     dg = jnp.where(filled, jnp.concatenate(dg, axis=0), 0.0)
 
     def over_x(sent, sent_out, dg):
-        dg = jnp.sum(
-            jnp.where(table[:, None, :] == row_index[None, :, None], dg[:, None, :], 0.0), axis=2
-        )
+        dg = jnp.where(is_low, dg[:, :, None], 0.0).astype(BF16)
+        dg = jnp.einsum("esh,esl->ehl", is_high, dg, preferred_element_type=F32)
+        dg = dg.reshape(expert_local, rows)
         d_dense = lax.dynamic_update_slice_in_dim(
             jnp.zeros((rows, EXPERTS), F32), dg.T, rank * expert_local, 1
         )
         return [scatter_rows(sent), scatter_rows(d_dense), sent_out]
 
     d_rows, d_gates, out_part = phase(
-        over_x, [dx_part.astype(BF16), out_part.astype(BF16), dg], sums[1:]
-    )
+        over_x, [dx_part.astype(BF16), out_part.astype(BF16), dg],
+        [sums[1], two_a, sums[3]],
+    )
+    three_a, three_b = sums[3].split(2, 2)
     gates_own = lax.dynamic_slice_in_dim(gates_f, own_row, local_rows, 0)
     d_logits = gates_own * (d_gates - jnp.sum(d_gates * gates_own, axis=-1, keepdims=True))
     router_grad = jnp.dot(hidden_rows.astype(F32).T, d_logits, precision=exact_mode)
@@ -714,7 +763,7 @@
     d_norm_two, gain_two_grad = rms_back(d_rows, residual_two, inverse_two, gain_two)
     d_residual = cotangent.astype(F32) + d_norm_two
     (d_all,) = phase(
-        lambda sent: [gather_rows(sent)], [d_residual.astype(BF16)], sums[2:]
+        lambda sent: [gather_rows(sent)], [d_residual.astype(BF16)], [two_a, two_b, three_a]
     )
 
     do_t = dot(out_weight_t, d_all, 0, 1).astype(BF16)
@@ -725,10 +774,10 @@
         )
         return list(parts) + [scatter_rows(out_part)]
 
-    dq_t, dk, dv, moe_rows = phase(back, [do_t, out_part], sums[3:])
+    dq_t, dk_t, dv_t, moe_rows = phase(
+        back, [do_t, out_part], [two_b, three_a, three_b]
+    )
     output = (residual_two + moe_rows).astype(BF16)
-    dk_t = rope_t(jnp.transpose(dk, (0, 2, 1)).reshape(d_k, rows), cosine, -sine).astype(BF16)
-    dv_t = jnp.transpose(dv, (0, 2, 1)).reshape(d_k, rows).astype(BF16)
     d_qkv_t = jnp.concatenate([dq_t, dk_t, dv_t], axis=0)
     grad_out_t = dot(d_all, o_t, 0, 1).astype(BF16)
     grad_qkv = dot(hidden_one, d_qkv_t, 0, 1).astype(BF16)
@@ -743,17 +792,21 @@
     even = parity[0] == 0
     first, second = small_grad[:, 0], small_grad[:, 1]
     small = Reduce(jnp.where(even, first, second), jnp.where(even, second, first))
-    d_hidden_one = scatter_rows(d_hidden_part.astype(BF16))
-    for _ in range(3):
-        small.take(small.move(small.sends()))
-    small_sum = small.result()
+
+    def end(sent):
+        for _ in range(3):
+            small.take(small.move(small.sends()))
+        return [scatter_rows(sent), small.result()]
+
+    d_hidden_one, small_sum = phase(end, [d_hidden_part.astype(BF16)], [three_b])
     d_norm_one, _ = rms_back(
         d_hidden_one, inputs_f, lax.dynamic_slice_in_dim(inverse_all, own_row, local_rows, 0),
         gain_one,
     )
     grad_tokens = (d_residual + d_norm_one).astype(BF16)
 
-    total = jnp.concatenate([r.result() for r in sums], axis=0)
+    ends = [sums[0], sums[1], two_a, two_b, three_a, three_b]
+    total = jnp.concatenate([r.result() for r in ends if r is not None], axis=0)
     grad_gate, grad_up = total[:, 0], total[:, 1]
     half = shard_rows // 2
     grad_down = jnp.concatenate([total[:, 2, :half], total[:, 2, half:]], axis=2)

time: 1070 us -> 1090 us (1.019)
  other arithmetic: 161 us -> 120 us
  starting transfers between devices: 71.4 us -> 97.7 us
  Pallas kernels: 363 us -> 382 us
  local copies, waits for them, and re-layouts: 74.6 us -> 93.2 us
    ppermute x25 -> x33, waiting for transfers between devices: 62.7 us -> 109 us  [move(): return [lax.ppermute(a, 'dp', p) for a, p in zip(sent, pairs)]]
    ppermute x25 -> x33, starting transfers between devices: 40.4 us -> 79.9 us  [move(): return [lax.ppermute(a, 'dp', p) for a, p in zip(sent, pairs)]]
    reduce_sum x2 -> x0, other arithmetic: 31.5 us -> none  [the longest x1 16.1 us: shards(): jnp.sum(jnp.where(table[:, :, None] == row_index[None, None, :], share_t[...]
    ppermute x4 -> x3, waiting for transfers between devices: 97.8 us -> 69.1 us  [gather_rows(): other = lax.ppermute(x, axis, [(0, 1), (1, 0)])]
    slice x0 -> x6, local copies, waits for them, and re-layouts: none -> 19.6 us  [the longest x3 9.92 us: split(): part = Reduce(self.keep[:, run], None)]
    ppermute x5, waiting for transfers between devices: 103 us -> 90.6 us  [scatter_rows(): lax.ppermute(lax.dynamic_slice_in_dim(x, (1 - rank) * rows, rows, 0), axi...]
    pallas_call x4, Pallas kernels: 269 us -> 280 us  [expert_call(): pl.pallas_call(expert_kernel, grid_spec=pltpu.PrefetchScalarGridSpec(num_...]
    ppermute x5, starting transfers between devices: 16.4 us -> 5.19 us  [scatter_rows(): lax.ppermute(lax.dynamic_slice_in_dim(x, (1 - rank) * rows, rows, 0), axi...]
  transfers between devices with their start and end apart: 41 -> 49, of which waited for: 18 -> 21; matrix products, arithmetic and copies ran while one was open for 16% -> 14% of each run, Pallas kernels for 27% -> 29%
where the time goes in v2:
time: 1090 us; the launch traced here: 1080 us
  Pallas kernels  382 us (35%)
  waiting for transfers between devices  331 us (30%)
  other arithmetic  120 us (11%)
  starting transfers between devices  97.7 us (9%)
  local copies, waits for them, and re-layouts  93.2 us (9%)
  matrix products  43.4 us (4%)
  between operations  18 us (2%)
    pallas_call x4, Pallas kernels, expert_call(): pl.pallas_call(expert_kernel, grid_spec=pltpu.PrefetchScalarGridSpec(num_...  280 us
    ppermute x33, waiting for transfers between devices, move(): return [lax.ppermute(a, 'dp', p) for a, p in zip(sent, pairs)]  109 us
    ppermute x5, waiting for transfers between devices, scatter_rows(): lax.ppermute(lax.dynamic_slice_in_dim(x, (1 - rank) * rows, rows, 0), axi...  90.6 us
    ppermute x33, starting transfers between devices, move(): return [lax.ppermute(a, 'dp', p) for a, p in zip(sent, pairs)]  79.9 us
    ppermute x3, waiting for transfers between devices, gather_rows(): other = lax.ppermute(x, axis, [(0, 1), (1, 0)])  69.1 us
    pallas_call x1, Pallas kernels, attend_back(): pl.pallas_call(attend_back_kernel, grid_spec=pltpu.PrefetchScalarGridSpec...  57.9 us
    pallas_call x1, Pallas kernels, attend(): pl.pallas_call(attend_kernel, grid_spec=pltpu.PrefetchScalarGridSpec(num_...  44.3 us
    ppermute x1, waiting for transfers between devices, gather_dp(): buf = place(buf, y, [(1 - y, lax.ppermute(buf, 'dp', Y_PAIRS))])  37 us
  transfers between devices with their start and end apart: 49, of which 21 were waited for; matrix products, arithmetic and copies ran while one was open for 14% of the time, Pallas kernels for 29%

profile of v2, /device:TPU:0, one launch (start us, length us, event | category | flops | bytes accessed | tf_op | source)
XLA Modules:
  0.0 1084.9 jit_solution(17749136958479441742)
XLA Ops:
  14.9 5.1 collective-permute-start.1
  22.7 14.6 %collective-permute-done = bf16[64,1664]{1,0:T(8,128)(2,1)} collective-permute-done((bf16[64,1664]{1,0:T(8,128)(2,1)S(1)}, bf16[64,1664]{1,0:T(8,128)(2,1)}, u32[]{:S(2)}, u32[]{:S(2)}) %collective-permute-start) | collective-permute-done | bytes 213024 | tf_op jit(solution)/shard_map/ppermute | solution.py:100
  39.2 6.1 collective-permute-done.2
  48.2 37.0 %collective-permute-done.3 = bf16[4,64,1664]{2,1,0:T(8,128)(2,1)} collective-permute-done((bf16[4,64,1664]{2,1,0:T(8,128)(2,1)S(1)}, bf16[4,64,1664]{2,1,0:T(8,128)(2,1)}, u32[]{:S(2)}, u32[]{:S(2)}) %collective-permute-start.3) | collective-permute-done | bytes 852000 | tf_op jit(solution)/shard_map/ppermute | solution.py:102
  92.1 5.0 fusion.22
  109.9 44.3 %attend.1 = (bf16[512,2048]{1,0:T(8,128)(2,1)}, f32[4,2,2048]{2,1,0:T(2,128)}) custom-call(s32[8]{0:T(128)} %and_select_fusion.low, bf16[512,2048]{1,0:T(8,128)(2,1)} %bitcast.284, bf16[4,2048,64]{2,1,0:T(8,128)(2,1)} %bitcast.286, bf16[256,2048]{1,0:T(8,128)(2,1)} %slice.268.v_ref, s32[1,2048]{1,0:T(1,128)} %bitcast.334), custom_call_target="tpu_custom_call" | custom-call | flops 1 | bytes 150000000 | tf_op jit(solution)/shard_map/attend/pallas_call | solution.py:268
  154.2 4.4 convolution_convert_fusion
  163.0 47.1 %collective-permute-done.7 = bf16[1024,1024]{1,0:T(8,128)(2,1)} collective-permute-done((bf16[1024,1024]{1,0:T(8,128)(2,1)}, bf16[1024,1024]{1,0:T(8,128)(2,1)}, u32[]{:S(2)}, u32[]{:S(2)}) %collective-permute-start.7) | collective-permute-done | bytes 2097184 | tf_op jit(solution)/shard_map/ppermute | solution.py:65
  224.5 37.7 %collective-permute-done.8 = bf16[1024,1024]{1,0:T(8,128)(2,1)} collective-permute-done((bf16[1024,1024]{1,0:T(8,128)(2,1)S(1)}, bf16[1024,1024]{1,0:T(8,128)(2,1)}, u32[]{:S(2)}, u32[]{:S(2)}) %collective-permute-start.8) | collective-permute-done | bytes 2097184 | tf_op jit(solution)/shard_map/ppermute | solution.py:41
  277.3 4.2 all-gather.2.cloned.1.call-done
  281.5 71.0 %experts.4 = (bf16[8,4,3,64,512]{4,3,2,1,0:T(8,128)(2,1)}, bf16[8,4,3,64,512]{4,3,2,1,0:T(8,128)(2,1)}, bf16[2048,1024]{1,0:T(8,128)(2,1)}, bf16[2048,1024]{1,0:...) custom-call(s32[3072]{0:T(1024)} %reshape.767.table, s32[4]{0:T(128)} %get-tuple-element.397.count, ...), custom_call_target="tpu_custom_call" | custom-call | flops 1 | bytes 150000000 | tf_op jit(solution)/shard_map/experts/pallas_call | solution.py:572
  357.2 75.6 %experts.5 = (bf16[8,4,3,64,512]{4,3,2,1,0:T(8,128)(2,1)}, bf16[8,4,3,64,512]{4,3,2,1,0:T(8,128)(2,1)}, bf16[2048,1024]{1,0:T(8,128)(2,1)}, bf16[2048,1024]{1,0:...) custom-call(s32[3072]{0:T(1024)} %reshape.772.table, s32[4]{0:T(128)} %get-tuple-element.125.count, ...), custom_call_target="tpu_custom_call" | custom-call | flops 1 | bytes 150000000 | tf_op jit(solution)/shard_map/experts/pallas_call | solution.py:572
  432.9 5.9 fusion.12
  439.3 8.2 collective-permute-start.10
  451.4 72.4 %experts.6 = (bf16[8,4,3,64,512]{4,3,2,1,0:T(8,128)(2,1)}, bf16[8,4,3,64,512]{4,3,2,1,0:T(8,128)(2,1)}, bf16[2048,1024]{1,0:T(8,128)(2,1)}, bf16[2048,1024]{1,0:...) custom-call(s32[3072]{0:T(1024)} %reshape.773.table, s32[4]{0:T(128)} %get-tuple-element.130.count, ...), custom_call_target="tpu_custom_call" | custom-call | flops 1 | bytes 150000000 | tf_op jit(solution)/shard_map/experts/pallas_call | solution.py:572
  527.0 6.0 fusion.13
  547.4 5.1 slice.167
  552.5 60.9 %experts.7 = (bf16[8,4,3,64,512]{4,3,2,1,0:T(8,128)(2,1)}, bf16[8,4,3,64,512]{4,3,2,1,0:T(8,128)(2,1)}, bf16[2048,1024]{1,0:T(8,128)(2,1)}, bf16[2048,1024]{1,0:...) custom-call(s32[3072]{0:T(1024)} %reshape.776.table, s32[4]{0:T(128)} %get-tuple-element.138.count, ...), custom_call_target="tpu_custom_call" | custom-call | flops 1 | bytes 150000000 | tf_op jit(solution)/shard_map/experts/pallas_call | solution.py:572
  622.4 7.1 add_convert_fusion
  629.6 7.8 add_convert_fusion.1
  637.4 22.3 %collective-permute-done.12 = bf16[4,3,64,512]{3,2,0,1:T(8,128)(2,1)S(1)} collective-permute-done((bf16[4,3,64,512]{3,2,0,1:T(8,128)(2,1)}, bf16[4,3,64,512]{3,2,0,1:T(8,128)(2,1)S(1)}, u32[]{:S(2)}, u32[]{:S(2)}) %collective-permute-start.12) | collective-permute-done | bytes 786464 | tf_op jit(solution)/shard_map/ppermute | solution.py:162
  659.7 10.1 collective-permute-done.14
  689.1 14.0 %collective-permute-start.19 = (bf16[4,3,64,512]{3,2,0,1:T(8,128)(2,1)}, bf16[4,3,64,512]{3,2,0,1:T(8,128)(2,1)S(1)}, u32[]{:S(2)}, u32[]{:S(2)}) collective-permute-start(bf16[4,3,64,512]{3,2,0,1:T(8,128)(2,1)} %get-tuple-element.160), channel_id=1, source_target_pairs={{0,16},{2,18},{4,20},{6,22},{8,24},{10,26},{12,28},{14,30},{16,0},... | collective-permute-start | bytes 2359304 | tf_op jit(solution)/shard_map/ppermute | solution.py:162
  703.1 28.5 %collective-permute-done.18 = f32[1024,32]{0,1:T(8,128)} collective-permute-done((f32[1024,32]{0,1:T(8,128)}, f32[1024,32]{0,1:T(8,128)}, u32[]{:S(2)}, u32[]{:S(2)}) %collective-permute-start.18) | collective-permute-done | bytes 131104 | tf_op jit(solution)/shard_map/ppermute | solution.py:65
  731.6 7.3 collective-permute-start.20
  747.8 7.7 collective-permute-done.19
  757.2 15.6 %collective-permute-done.21 = bf16[4,3,64,512]{3,2,0,1:T(8,128)(2,1)S(1)} collective-permute-done((bf16[4,3,64,512]{3,2,0,1:T(8,128)(2,1)}, bf16[4,3,64,512]{3,2,0,1:T(8,128)(2,1)S(1)}, u32[]{:S(2)}, u32[]{:S(2)}) %collective-permute-start.21) | collective-permute-done | bytes 786464 | tf_op jit(solution)/shard_map/ppermute | solution.py:162
  773.7 5.4 fusion.102
  779.2 4.4 multiply_reduce_fusion
  786.7 4.6 fusion.100
  795.4 6.3 collective-permute-start.29
  805.2 4.7 collective-permute-start.26
  809.9 31.4 %collective-permute-done.24 = bf16[1024,1024]{1,0:T(8,128)(2,1)S(1)} collective-permute-done((bf16[1024,1024]{1,0:T(8,128)(2,1)S(1)}, bf16[1024,1024]{1,0:T(8,128)(2,1)S(1)}, u32[]{:S(2)}, u32[]{:S(2)}) %collective-permute-start.24) | collective-permute-done | bytes 2097184 | tf_op jit(solution)/shard_map/ppermute | solution.py:41
  841.3 4.4 collective-permute-start.27
  846.9 10.9 %collective-permute-done.27 = bf16[3,3,64,512]{3,2,0,1:T(8,128)(2,1)S(1)} collective-permute-done((bf16[3,3,64,512]{3,2,0,1:T(8,128)(2,1)}, bf16[3,3,64,512]{3,2,0,1:T(8,128)(2,1)S(1)}, u32[]{:S(2)}, u32[]{:S(2)}) %collective-permute-start.27) | collective-permute-done | bytes 589856 | tf_op jit(solution)/shard_map/ppermute | solution.py:162
  859.7 5.0 convolution_convert_fusion.1.do_ref
  869.0 4.5 collective-permute-start.37
  881.9 16.5 %collective-permute-done.31 = bf16[1,3,64,512]{3,2,1,0:T(8,128)(2,1)S(1)} collective-permute-done((bf16[1,3,64,512]{3,2,1,0:T(8,128)(2,1)}, bf16[1,3,64,512]{3,2,1,0:T(8,128)(2,1)S(1)}, u32[]{:S(2)}, u32[]{:S(2)}) %collective-permute-start.31) | collective-permute-done | bytes 196640 | tf_op jit(solution)/shard_map/ppermute | solution.py:162
  902.9 5.1 convolution_convert_fusion.3
  908.0 57.9 %attend_back.1 = (bf16[512,2048]{1,0:T(8,128)(2,1)}, bf16[256,2048]{1,0:T(8,128)(2,1)}, bf16[256,2048]{1,0:T(8,128)(2,1)}) custom-call(s32[8]{0:T(128)} %and_select_fusion.low, bf16[512,2048]{1,0:T(8,128)(2,1)} %bitcast.285, bf16[512,2048]{1,0:T(8,128)(2,1)} %convolution_convert_fusion.1.do_ref, bf16[512,2048]{1,0:T(8,128)(2,1)} %get-tuple-element.121.o_ref, ...), custom_call_target="tpu_custom_call" | custom-call | flops 1 | bytes 150000000 | tf_op jit(solution)/shard_map/attend_back/pallas_call | solution.py:354
  966.3 5.3 convert_add_fusion.2
  975.7 8.1 fusion.4
  983.8 4.9 convolution_convert_fusion.2
  990.8 4.4 copy.404
  1017.2 13.7 %collective-permute-done.40 = bf16[4,64,1664]{2,1,0:T(8,128)(2,1)S(1)} collective-permute-done((bf16[4,64,1664]{2,1,0:T(8,128)(2,1)S(1)}, bf16[4,64,1664]{2,1,0:T(8,128)(2,1)S(1)}, u32[]{:S(2)}, u32[]{:S(2)}) %collective-permute-start.40) | collective-permute-done | bytes 852000 | tf_op jit(solution)/shard_map/ppermute | solution.py:162
  1034.1 15.1 %collective-permute-done.38 = bf16[1024,1024]{1,0:T(8,128)(2,1)S(1)} collective-permute-done((bf16[1024,1024]{1,0:T(8,128)(2,1)S(1)}, bf16[1024,1024]{1,0:T(8,128)(2,1)S(1)}, u32[]{:S(2)}, u32[]{:S(2)}) %collective-permute-start.38) | collective-permute-done | bytes 2097184 | tf_op jit(solution)/shard_map/ppermute | solution.py:65
  1053.9 5.2 collective-permute-done.42
  1059.3 4.6 collective-permute-done.46
  (462 shorter events, 213.5 us)
Async XLA Ops:
  10.3 271.2 %all-gather.2.cloned.1.call-start = ((), (), s32[]{:S(2)}) async-start(), calls=%async_computation | async-start | bytes 53477376 | tf_op jit(solution)/shard_map/all_gather | solution.py:655
  14.9 23.4 %collective-permute-start.1 = (bf16[64,1664]{1,0:T(8,128)(2,1)S(1)}, bf16[64,1664]{1,0:T(8,128)(2,1)}, u32[]{:S(2)}, u32[]{:S(2)}) collective-permute-start(bf16[64,1664]{1,0:T(8,128)(2,1)S(1)} %pad.8), channel_id=1, source_target_pairs={{0,24},{2,26},{4,28},{6,30},{8,0},{10,2},{12,4},{14,6},{16,8},{18,... | collective-permute-start | bytes 638984 | tf_op jit(solution)/shard_map/ppermute | solution.py:100
  20.0 17.3 %collective-permute-start = (bf16[64,1664]{1,0:T(8,128)(2,1)S(1)}, bf16[64,1664]{1,0:T(8,128)(2,1)}, u32[]{:S(2)}, u32[]{:S(2)}) collective-permute-start(bf16[64,1664]{1,0:T(8,128)(2,1)S(1)} %pad.8), channel_id=1, source_target_pairs={{0,8},{2,10},{4,12},{6,14},{8,16},{10,18},{12,20},{14,22},{16,24},... | collective-permute-start | bytes 638984 | tf_op jit(solution)/shard_map/ppermute | solution.py:100
  20.0 25.3 %collective-permute-start.2 = (bf16[64,1664]{1,0:T(8,128)(2,1)S(1)}, bf16[64,1664]{1,0:T(8,128)(2,1)}, u32[]{:S(2)}, u32[]{:S(2)}) collective-permute-start(bf16[64,1664]{1,0:T(8,128)(2,1)S(1)} %pad.8), channel_id=1, source_target_pairs={{0,16},{2,18},{4,20},{6,22},{8,24},{10,26},{12,28},{14,30},{16,0},... | collective-permute-start | bytes 638984 | tf_op jit(solution)/shard_map/ppermute | solution.py:100
  21.0 67.1 %collective-permute-start.5 = (bf16[1024,1024]{1,0:T(8,128)(2,1)S(1)}, bf16[1024,1024]{1,0:T(8,128)(2,1)}, u32[]{:S(2)}, u32[]{:S(2)}) collective-permute-start(bf16[1024,1024]{1,0:T(8,128)(2,1)S(1)} %copy-done.4), channel_id=1, source_target_pairs={{0,1},{1,0},{2,3},{3,2},{4,5},{5,4},{6,7},{7,6},{8,9},{9,8},{10,11... | collective-permute-start | bytes 6291464 | tf_op jit(solution)/shard_map/ppermute | solution.py:41
  46.3 38.8 %collective-permute-start.3 = (bf16[4,64,1664]{2,1,0:T(8,128)(2,1)S(1)}, bf16[4,64,1664]{2,1,0:T(8,128)(2,1)}, u32[]{:S(2)}, u32[]{:S(2)}) collective-permute-start(bf16[4,64,1664]{2,1,0:T(8,128)(2,1)S(1)} %bitcast_dynamic-update-slice_fusion.4), channel_id=1, source_target_pairs={{0,4},{2,6},{4,0},{6,2},{8,12},{10,14},{12,8},{14,10},{16,20},{18,... | collective-permute-start | bytes 2555912 | tf_op jit(solution)/shard_map/ppermute | solution.py:102
  102.8 51.4 %collective-permute-start.6 = (bf16[1024,1024]{1,0:T(8,128)(2,1)}, bf16[1024,1024]{1,0:T(8,128)(2,1)}, u32[]{:S(2)}, u32[]{:S(2)}) collective-permute-start(bf16[1024,1024]{1,0:T(8,128)(2,1)} %param.27), channel_id=1, source_target_pairs={{0,1},{1,0},{2,3},{3,2},{4,5},{5,4},{6,7},{7,6},{8,9},{9,8},{10,11... | collective-permute-start | bytes 6291464 | tf_op jit(solution)/shard_map/ppermute | solution.py:49
  162.1 48.0 %collective-permute-start.7 = (bf16[1024,1024]{1,0:T(8,128)(2,1)}, bf16[1024,1024]{1,0:T(8,128)(2,1)}, u32[]{:S(2)}, u32[]{:S(2)}) collective-permute-start(bf16[1024,1024]{1,0:T(8,128)(2,1)} %constant_dynamic-slice_fusion.54), channel_id=1, source_target_pairs={{0,1},{1,0},{2,3},{3,2},{4,5},{5,4},{6,7},{7,6},{8,9},{9,8},{10,11... | collective-permute-start | bytes 6291464 | tf_op jit(solution)/shard_map/ppermute | solution.py:65
  215.3 46.9 %collective-permute-start.8 = (bf16[1024,1024]{1,0:T(8,128)(2,1)S(1)}, bf16[1024,1024]{1,0:T(8,128)(2,1)}, u32[]{:S(2)}, u32[]{:S(2)}) collective-permute-start(bf16[1024,1024]{1,0:T(8,128)(2,1)S(1)} %multiply_convert_fusion), channel_id=1, source_target_pairs={{0,1},{1,0},{2,3},{3,2},{4,5},{5,4},{6,7},{7,6},{8,9},{9,8},{10,11... | collective-permute-start | bytes 6291464 | tf_op jit(solution)/shard_map/ppermute | solution.py:41
  352.5 80.4 %collective-permute-start.9 = (bf16[8,4,3,64,512]{4,3,2,1,0:T(8,128)(2,1)}, bf16[8,4,3,64,512]{4,3,2,1,0:T(8,128)(2,1)}, u32[]{:S(2)}, u32[]{:S(2)}) collective-permute-start(bf16[8,4,3,64,512]{4,3,2,1,0:T(8,128)(2,1)} %get-tuple-element.128), channel_id=1, source_target_pairs={{0,2},{2,0},{4,6},{6,4},{8,10},{10,8},{12,14},{14,12},{16,18},{18,... | collective-permute-start | bytes 18874376 | tf_op jit(solution)/shard_map/ppermute | solution.py:162
  438.8 88.3 %collective-permute-start.11 = (bf16[8,4,3,64,512]{4,3,2,1,0:T(8,128)(2,1)}, bf16[8,4,3,64,512]{4,3,2,1,0:T(8,128)(2,1)}, u32[]{:S(2)}, u32[]{:S(2)}) collective-permute-start(bf16[8,4,3,64,512]{4,3,2,1,0:T(8,128)(2,1)} %get-tuple-element.133), channel_id=1, source_target_pairs={{0,2},{2,0},{4,6},{6,4},{8,10},{10,8},{12,14},{14,12},{16,18},{18,... | collective-permute-start | bytes 18874376 | tf_op jit(solution)/shard_map/ppermute | solution.py:162
  439.3 87.7 %collective-permute-start.10 = (bf16[4,4,3,64,512]{4,3,1,2,0:T(8,128)(2,1)}, bf16[4,4,3,64,512]{4,3,1,2,0:T(8,128)(2,1)}, u32[]{:S(2)}, u32[]{:S(2)}) collective-permute-start(bf16[4,4,3,64,512]{4,3,1,2,0:T(8,128)(2,1)} %fusion.12), channel_id=1, source_target_pairs={{0,4},{2,6},{4,0},{6,2},{8,12},{10,14},{12,8},{14,10},{16,20},{18,... | collective-permute-start | bytes 9437192 | tf_op jit(solution)/shard_map/ppermute | solution.py:162
  537.2 132.7 %collective-permute-start.16 = (bf16[8,4,3,64,512]{4,3,2,1,0:T(8,128)(2,1)}, bf16[8,4,3,64,512]{4,3,2,1,0:T(8,128)(2,1)}, u32[]{:S(2)}, u32[]{:S(2)}) collective-permute-start(bf16[8,4,3,64,512]{4,3,2,1,0:T(8,128)(2,1)} %get-tuple-element.152), channel_id=1, source_target_pairs={{0,2},{2,0},{4,6},{6,4},{8,10},{10,8},{12,14},{14,12},{16,18},{18,... | collective-permute-start | bytes 18874376 | tf_op jit(solution)/shard_map/ppermute | solution.py:162
  537.2 132.7 %collective-permute-start.15 = (bf16[4,4,3,64,512]{4,3,1,2,0:T(8,128)(2,1)}, bf16[4,4,3,64,512]{4,3,1,2,0:T(8,128)(2,1)}, u32[]{:S(2)}, u32[]{:S(2)}) collective-permute-start(bf16[4,4,3,64,512]{4,3,1,2,0:T(8,128)(2,1)} %fusion.13), channel_id=1, source_target_pairs={{0,4},{2,6},{4,0},{6,2},{8,12},{10,14},{12,8},{14,10},{16,20},{18,... | collective-permute-start | bytes 9437192 | tf_op jit(solution)/shard_map/ppermute | solution.py:162
  615.3 44.4 %collective-permute-start.12 = (bf16[4,3,64,512]{3,2,0,1:T(8,128)(2,1)}, bf16[4,3,64,512]{3,2,0,1:T(8,128)(2,1)S(1)}, u32[]{:S(2)}, u32[]{:S(2)}) collective-permute-start(bf16[4,3,64,512]{3,2,0,1:T(8,128)(2,1)} %get-tuple-element.148), channel_id=1, source_target_pairs={{0,16},{2,18},{4,20},{6,22},{8,24},{10,26},{12,28},{14,30},{16,0},... | collective-permute-start | bytes 2359304 | tf_op jit(solution)/shard_map/ppermute | solution.py:162
  615.4 44.3 %collective-permute-start.13 = (bf16[4,3,64,512]{3,2,0,1:T(8,128)(2,1)}, bf16[4,3,64,512]{3,2,0,1:T(8,128)(2,1)S(1)}, u32[]{:S(2)}, u32[]{:S(2)}) collective-permute-start(bf16[4,3,64,512]{3,2,0,1:T(8,128)(2,1)} %get-tuple-element.149), channel_id=1, source_target_pairs={{0,8},{2,10},{4,12},{6,14},{8,16},{10,18},{12,20},{14,22},{16,24},... | collective-permute-start | bytes 2359304 | tf_op jit(solution)/shard_map/ppermute | solution.py:162
  615.4 54.4 %collective-permute-start.14 = (bf16[4,3,64,512]{3,2,0,1:T(8,128)(2,1)}, bf16[4,3,64,512]{3,2,0,1:T(8,128)(2,1)}, u32[]{:S(2)}, u32[]{:S(2)}) collective-permute-start(bf16[4,3,64,512]{3,2,0,1:T(8,128)(2,1)} %get-tuple-element.150), channel_id=1, source_target_pairs={{0,24},{2,26},{4,28},{6,30},{8,0},{10,2},{12,4},{14,6},{16,8},{18,... | collective-permute-start | bytes 2359304 | tf_op jit(solution)/shard_map/ppermute | solution.py:162
  679.0 94.7 %collective-permute-start.23 = (bf16[8,4,3,64,512]{4,3,2,1,0:T(8,128)(2,1)}, bf16[8,4,3,64,512]{4,3,2,1,0:T(8,128)(2,1)}, u32[]{:S(2)}, u32[]{:S(2)}) collective-permute-start(bf16[8,4,3,64,512]{4,3,2,1,0:T(8,128)(2,1)} %get-tuple-element.164), channel_id=1, source_target_pairs={{0,2},{2,0},{4,6},{6,4},{8,10},{10,8},{12,14},{14,12},{16,18},{18,... | collective-permute-start | bytes 18874376 | tf_op jit(solution)/shard_map/ppermute | solution.py:162
  680.4 58.5 %collective-permute-start.17 = (bf16[1024,1024]{1,0:T(8,128)(2,1)}, bf16[1024,1024]{1,0:T(8,128)(2,1)}, u32[]{:S(2)}, u32[]{:S(2)}) collective-permute-start(bf16[1024,1024]{1,0:T(8,128)(2,1)} %constant_dynamic-slice_fusion.35), channel_id=1, source_target_pairs={{0,1},{1,0},{2,3},{3,2},{4,5},{5,4},{6,7},{7,6},{8,9},{9,8},{10,11... | collective-permute-start | bytes 6291464 | tf_op jit(solution)/shard_map/ppermute | solution.py:65
  680.5 92.3 %collective-permute-start.22 = (bf16[4,3,3,64,512]{4,3,1,2,0:T(8,128)(2,1)}, bf16[4,3,3,64,512]{4,3,1,2,0:T(8,128)(2,1)}, u32[]{:S(2)}, u32[]{:S(2)}) collective-permute-start(bf16[4,3,3,64,512]{4,3,1,2,0:T(8,128)(2,1)} %fusion.18), channel_id=1, source_target_pairs={{0,4},{2,6},{4,0},{6,2},{8,12},{10,14},{12,8},{14,10},{16,20},{18,... | collective-permute-start | bytes 7077896 | tf_op jit(solution)/shard_map/ppermute | solution.py:162
  683.8 47.9 %collective-permute-start.18 = (f32[1024,32]{0,1:T(8,128)}, f32[1024,32]{0,1:T(8,128)}, u32[]{:S(2)}, u32[]{:S(2)}) collective-permute-start(f32[1024,32]{0,1:T(8,128)} %constant_dynamic-slice_fusion.34), channel_id=1, source_target_pairs={{0,1},{1,0},{2,3},{3,2},{4,5},{5,4},{6,7},{7,6},{8,9},{9,8},{10,11... | collective-permute-start | bytes 393224 | tf_op jit(solution)/shard_map/ppermute | solution.py:65
  689.1 66.4 %collective-permute-start.19 = (bf16[4,3,64,512]{3,2,0,1:T(8,128)(2,1)}, bf16[4,3,64,512]{3,2,0,1:T(8,128)(2,1)S(1)}, u32[]{:S(2)}, u32[]{:S(2)}) collective-permute-start(bf16[4,3,64,512]{3,2,0,1:T(8,128)(2,1)} %get-tuple-element.160), channel_id=1, source_target_pairs={{0,16},{2,18},{4,20},{6,22},{8,24},{10,26},{12,28},{14,30},{16,0},... | collective-permute-start | bytes 2359304 | tf_op jit(solution)/shard_map/ppermute | solution.py:162
  731.6 25.6 %collective-permute-start.20 = (bf16[4,3,64,512]{3,2,0,1:T(8,128)(2,1)}, bf16[4,3,64,512]{3,2,0,1:T(8,128)(2,1)S(1)}, u32[]{:S(2)}, u32[]{:S(2)}) collective-permute-start(bf16[4,3,64,512]{3,2,0,1:T(8,128)(2,1)} %get-tuple-element.161), channel_id=1, source_target_pairs={{0,8},{2,10},{4,12},{6,14},{8,16},{10,18},{12,20},{14,22},{16,24},... | collective-permute-start | bytes 2359304 | tf_op jit(solution)/shard_map/ppermute | solution.py:162
  738.9 33.9 %collective-permute-start.21 = (bf16[4,3,64,512]{3,2,0,1:T(8,128)(2,1)}, bf16[4,3,64,512]{3,2,0,1:T(8,128)(2,1)S(1)}, u32[]{:S(2)}, u32[]{:S(2)}) collective-permute-start(bf16[4,3,64,512]{3,2,0,1:T(8,128)(2,1)} %get-tuple-element.162), channel_id=1, source_target_pairs={{0,24},{2,26},{4,28},{6,30},{8,0},{10,2},{12,4},{14,6},{16,8},{18,... | collective-permute-start | bytes 2359304 | tf_op jit(solution)/shard_map/ppermute | solution.py:162
  794.9 46.4 %collective-permute-start.24 = (bf16[1024,1024]{1,0:T(8,128)(2,1)S(1)}, bf16[1024,1024]{1,0:T(8,128)(2,1)S(1)}, u32[]{:S(2)}, u32[]{:S(2)}) collective-permute-start(bf16[1024,1024]{1,0:T(8,128)(2,1)S(1)} %get-tuple-element.170), channel_id=1, source_target_pairs={{0,1},{1,0},{2,3},{3,2},{4,5},{5,4},{6,7},{7,6},{8,9},{9,8},{10,11... | collective-permute-start | bytes 6291464 | tf_op jit(solution)/shard_map/ppermute | solution.py:41
  795.4 62.5 %collective-permute-start.29 = (bf16[4,2,3,64,512]{4,3,1,2,0:T(8,128)(2,1)S(1)}, bf16[4,2,3,64,512]{4,3,1,2,0:T(8,128)(2,1)S(1)}, u32[]{:S(2)}, u32[]{:S(2)}) collective-permute-start(bf16[4,2,3,64,512]{4,3,1,2,0:T(8,128)(2,1)S(1)} %copy-done.58), channel_id=1, source_target_pairs={{0,4},{2,6},{4,0},{6,2},{8,12},{10,14},{12,8},{14,10},{16,20},{18,... | collective-permute-start | bytes 4718600 | tf_op jit(solution)/shard_map/ppermute | solution.py:162
  802.6 55.3 %collective-permute-start.28 = (bf16[4,1,3,64,512]{4,3,2,1,0:T(8,128)(2,1)S(1)}, bf16[4,1,3,64,512]{4,3,2,1,0:T(8,128)(2,1)S(1)}, u32[]{:S(2)}, u32[]{:S(2)}) collective-permute-start(bf16[4,1,3,64,512]{4,3,2,1,0:T(8,128)(2,1)S(1)} %copy-done.80), channel_id=1, source_target_pairs={{0,4},{2,6},{4,0},{6,2},{8,12},{10,14},{12,8},{14,10},{16,20},{18,... | collective-permute-start | bytes 2359304 | tf_op jit(solution)/shard_map/ppermute | solution.py:162
  805.2 41.7 %collective-permute-start.25 = (bf16[3,3,64,512]{3,2,0,1:T(8,128)(2,1)}, bf16[3,3,64,512]{3,2,0,1:T(8,128)(2,1)S(1)}, u32[]{:S(2)}, u32[]{:S(2)}) collective-permute-start(bf16[3,3,64,512]{3,2,0,1:T(8,128)(2,1)} %get-tuple-element.171), channel_id=1, source_target_pairs={{0,16},{2,18},{4,20},{6,22},{8,24},{10,26},{12,28},{14,30},{16,0},... | collective-permute-start | bytes 1769480 | tf_op jit(solution)/shard_map/ppermute | solution.py:162
  805.2 41.7 %collective-permute-start.26 = (bf16[3,3,64,512]{3,2,0,1:T(8,128)(2,1)}, bf16[3,3,64,512]{3,2,0,1:T(8,128)(2,1)S(1)}, u32[]{:S(2)}, u32[]{:S(2)}) collective-permute-start(bf16[3,3,64,512]{3,2,0,1:T(8,128)(2,1)} %get-tuple-element.172), channel_id=1, source_target_pairs={{0,8},{2,10},{4,12},{6,14},{8,16},{10,18},{12,20},{14,22},{16,24},... | collective-permute-start | bytes 1769480 | tf_op jit(solution)/shard_map/ppermute | solution.py:162
  841.3 16.6 %collective-permute-start.27 = (bf16[3,3,64,512]{3,2,0,1:T(8,128)(2,1)}, bf16[3,3,64,512]{3,2,0,1:T(8,128)(2,1)S(1)}, u32[]{:S(2)}, u32[]{:S(2)}) collective-permute-start(bf16[3,3,64,512]{3,2,0,1:T(8,128)(2,1)} %get-tuple-element.173), channel_id=1, source_target_pairs={{0,24},{2,26},{4,28},{6,30},{8,0},{10,2},{12,4},{14,6},{16,8},{18,... | collective-permute-start | bytes 1769480 | tf_op jit(solution)/shard_map/ppermute | solution.py:162
  867.7 98.3 %collective-permute-start.30 = (bf16[1024,1024]{1,0:T(8,128)(2,1)}, bf16[1024,1024]{1,0:T(8,128)(2,1)}, u32[]{:S(2)}, u32[]{:S(2)}) collective-permute-start(bf16[1024,1024]{1,0:T(8,128)(2,1)} %constant_dynamic-slice_fusion.12), channel_id=1, source_target_pairs={{0,1},{1,0},{2,3},{3,2},{4,5},{5,4},{6,7},{7,6},{8,9},{9,8},{10,11... | collective-permute-start | bytes 6291464 | tf_op jit(solution)/shard_map/ppermute | solution.py:65
  869.0 103.0 %collective-permute-start.37 = (bf16[4,2,3,64,512]{4,3,1,2,0:T(8,128)(2,1)}, bf16[4,2,3,64,512]{4,3,1,2,0:T(8,128)(2,1)}, u32[]{:S(2)}, u32[]{:S(2)}) collective-permute-start(bf16[4,2,3,64,512]{4,3,1,2,0:T(8,128)(2,1)} %fusion.25), channel_id=1, source_target_pairs={{0,4},{2,6},{4,0},{6,2},{8,12},{10,14},{12,8},{14,10},{16,20},{18,... | collective-permute-start | bytes 4718600 | tf_op jit(solution)/shard_map/ppermute | solution.py:162
  875.3 23.0 %collective-permute-start.31 = (bf16[1,3,64,512]{3,2,1,0:T(8,128)(2,1)}, bf16[1,3,64,512]{3,2,1,0:T(8,128)(2,1)S(1)}, u32[]{:S(2)}, u32[]{:S(2)}) collective-permute-start(bf16[1,3,64,512]{3,2,1,0:T(8,128)(2,1)} %get-tuple-element.186), channel_id=1, source_target_pairs={{0,16},{2,18},{4,20},{6,22},{8,24},{10,26},{12,28},{14,30},{16,0},... | collective-permute-start | bytes 589832 | tf_op jit(solution)/shard_map/ppermute | solution.py:162
  876.5 21.8 %collective-permute-start.32 = (bf16[1,3,64,512]{3,2,1,0:T(8,128)(2,1)}, bf16[1,3,64,512]{3,2,1,0:T(8,128)(2,1)S(1)}, u32[]{:S(2)}, u32[]{:S(2)}) collective-permute-start(bf16[1,3,64,512]{3,2,1,0:T(8,128)(2,1)} %get-tuple-element.187), channel_id=1, source_target_pairs={{0,8},{2,10},{4,12},{6,14},{8,16},{10,18},{12,20},{14,22},{16,24},... | collective-permute-start | bytes 589832 | tf_op jit(solution)/shard_map/ppermute | solution.py:162
  881.8 90.2 %collective-permute-start.34 = (bf16[2,3,64,512]{3,2,0,1:T(8,128)(2,1)}, bf16[2,3,64,512]{3,2,0,1:T(8,128)(2,1)S(1)}, u32[]{:S(2)}, u32[]{:S(2)}) collective-permute-start(bf16[2,3,64,512]{3,2,0,1:T(8,128)(2,1)} %get-tuple-element.189), channel_id=1, source_target_pairs={{0,16},{2,18},{4,20},{6,22},{8,24},{10,26},{12,28},{14,30},{16,0},... | collective-permute-start | bytes 1179656 | tf_op jit(solution)/shard_map/ppermute | solution.py:162
  898.4 73.6 %collective-permute-start.35 = (bf16[2,3,64,512]{3,2,0,1:T(8,128)(2,1)}, bf16[2,3,64,512]{3,2,0,1:T(8,128)(2,1)S(1)}, u32[]{:S(2)}, u32[]{:S(2)}) collective-permute-start(bf16[2,3,64,512]{3,2,0,1:T(8,128)(2,1)} %get-tuple-element.190), channel_id=1, source_target_pairs={{0,8},{2,10},{4,12},{6,14},{8,16},{10,18},{12,20},{14,22},{16,24},... | collective-permute-start | bytes 1179656 | tf_op jit(solution)/shard_map/ppermute | solution.py:162
  899.7 72.3 %collective-permute-start.36 = (bf16[2,3,64,512]{3,2,0,1:T(8,128)(2,1)}, bf16[2,3,64,512]{3,2,0,1:T(8,128)(2,1)S(1)}, u32[]{:S(2)}, u32[]{:S(2)}) collective-permute-start(bf16[2,3,64,512]{3,2,0,1:T(8,128)(2,1)} %get-tuple-element.191), channel_id=1, source_target_pairs={{0,24},{2,26},{4,28},{6,30},{8,0},{10,2},{12,4},{14,6},{16,8},{18,... | collective-permute-start | bytes 1179656 | tf_op jit(solution)/shard_map/ppermute | solution.py:162
  966.0 6.0 collective-permute-start.33
  995.5 16.5 %collective-permute-start.39 = (bf16[8,64,1664]{2,1,0:T(8,128)(2,1)S(1)}, bf16[8,64,1664]{2,1,0:T(8,128)(2,1)S(1)}, u32[]{:S(2)}, u32[]{:S(2)}) collective-permute-start(bf16[8,64,1664]{2,1,0:T(8,128)(2,1)S(1)} %get-tuple-element.344), channel_id=1, source_target_pairs={{0,2},{2,0},{4,6},{6,4},{8,10},{10,8},{12,14},{14,12},{16,18},{18,... | collective-permute-start | bytes 5111816 | tf_op jit(solution)/shard_map/ppermute | solution.py:162
  1003.3 45.9 %collective-permute-start.38 = (bf16[1024,1024]{1,0:T(8,128)(2,1)S(1)}, bf16[1024,1024]{1,0:T(8,128)(2,1)S(1)}, u32[]{:S(2)}, u32[]{:S(2)}) collective-permute-start(bf16[1024,1024]{1,0:T(8,128)(2,1)S(1)} %constant_dynamic-slice_fusion.5), channel_id=1, source_target_pairs={{0,1},{1,0},{2,3},{3,2},{4,5},{5,4},{6,7},{7,6},{8,9},{9,8},{10,11... | collective-permute-start | bytes 6291464 | tf_op jit(solution)/shard_map/ppermute | solution.py:65
  1008.7 50.6 %collective-permute-start.44 = (bf16[2,3,64,512]{3,2,0,1:T(8,128)(2,1)S(1)}, bf16[2,3,64,512]{3,2,0,1:T(8,128)(2,1)S(1)}, u32[]{:S(2)}, u32[]{:S(2)}) collective-permute-start(bf16[2,3,64,512]{3,2,0,1:T(8,128)(2,1)S(1)} %get-tuple-element.199), channel_id=1, source_target_pairs={{0,16},{2,18},{4,20},{6,22},{8,24},{10,26},{12,28},{14,30},{16,0},... | collective-permute-start | bytes 1179656 | tf_op jit(solution)/shard_map/ppermute | solution.py:162
  1010.1 49.2 %collective-permute-start.45 = (bf16[2,3,64,512]{3,2,0,1:T(8,128)(2,1)S(1)}, bf16[2,3,64,512]{3,2,0,1:T(8,128)(2,1)S(1)}, u32[]{:S(2)}, u32[]{:S(2)}) collective-permute-start(bf16[2,3,64,512]{3,2,0,1:T(8,128)(2,1)S(1)} %get-tuple-element.200), channel_id=1, source_target_pairs={{0,8},{2,10},{4,12},{6,14},{8,16},{10,18},{12,20},{14,22},{16,24},... | collective-permute-start | bytes 1179656 | tf_op jit(solution)/shard_map/ppermute | solution.py:162
  1012.2 18.6 %collective-permute-start.40 = (bf16[4,64,1664]{2,1,0:T(8,128)(2,1)S(1)}, bf16[4,64,1664]{2,1,0:T(8,128)(2,1)S(1)}, u32[]{:S(2)}, u32[]{:S(2)}) collective-permute-start(bf16[4,64,1664]{2,1,0:T(8,128)(2,1)S(1)} %fusion.49), channel_id=1, source_target_pairs={{0,4},{2,6},{4,0},{6,2},{8,12},{10,14},{12,8},{14,10},{16,20},{18,... | collective-permute-start | bytes 2555912 | tf_op jit(solution)/shard_map/ppermute | solution.py:162
  1031.1 20.6 %collective-permute-start.41 = (bf16[64,1664]{1,0:T(8,128)(2,1)S(1)}, bf16[64,1664]{1,0:T(8,128)(2,1)S(1)}, u32[]{:S(2)}, u32[]{:S(2)}) collective-permute-start(bf16[64,1664]{1,0:T(8,128)(2,1)S(1)} %get-tuple-element.330), channel_id=1, source_target_pairs={{0,16},{2,18},{4,20},{6,22},{8,24},{10,26},{12,28},{14,30},{16,0},... | collective-permute-start | bytes 638984 | tf_op jit(solution)/shard_map/ppermute | solution.py:162
  1032.7 21.2 %collective-permute-start.43 = (bf16[64,1664]{1,0:T(8,128)(2,1)S(1)}, bf16[64,1664]{1,0:T(8,128)(2,1)S(1)}, u32[]{:S(2)}, u32[]{:S(2)}) collective-permute-start(bf16[64,1664]{1,0:T(8,128)(2,1)S(1)} %get-tuple-element.331), channel_id=1, source_target_pairs={{0,24},{2,26},{4,28},{6,30},{8,0},{10,2},{12,4},{14,6},{16,8},{18,... | collective-permute-start | bytes 638984 | tf_op jit(solution)/shard_map/ppermute | solution.py:162
  1049.1 10.0 collective-permute-start.42
  1051.7 12.2 %collective-permute-start.46 = (bf16[2,3,64,512]{3,2,0,1:T(8,128)(2,1)S(1)}, bf16[2,3,64,512]{3,2,0,1:T(8,128)(2,1)S(1)}, u32[]{:S(2)}, u32[]{:S(2)}) collective-permute-start(bf16[2,3,64,512]{3,2,0,1:T(8,128)(2,1)S(1)} %get-tuple-element.201), channel_id=1, source_target_pairs={{0,24},{2,26},{4,28},{6,30},{8,0},{10,2},{12,4},{14,6},{16,8},{18,... | collective-permute-start | bytes 1179656 | tf_op jit(solution)/shard_map/ppermute | solution.py:162
  1070.0 5.6 collective-permute-start.47
  (124 other events, 1815.3 us)
Sparse Core Ops, SparseCore 0:
  11.9 4.6 sort.12.cloned.1.call-done
  (1 shorter events, 0.0 us)
Sparse Core Ops, SparseCore 1:
  14.0 267.4 all-gather.1

commit v3 on v2

--- a/solution.py
+++ b/solution.py
@@ -54,6 +54,28 @@
         return swapped
     first = lax.axis_index("tensor") == 0
     return jnp.concatenate([jnp.where(first, x, swapped), jnp.where(first, swapped, x)], axis=0)
+
+
+def leave_rows(x):
+    n = lax.axis_size("tensor")
+    rows = x.shape[0] // n
+    if n != 2:
+        return None, x
+    rank = lax.axis_index("tensor")
+    return (
+        lax.dynamic_slice_in_dim(x, rank * rows, rows, 0),
+        lax.dynamic_slice_in_dim(x, (1 - rank) * rows, rows, 0),
+    )
+
+
+def swap_sums(x):
+    if lax.axis_size("tensor") != 2:
+        return lax.psum_scatter(x, "tensor", scatter_dimension=0, tiled=True)
+    return lax.ppermute(x, "tensor", [(0, 1), (1, 0)])
+
+
+def add_rows_of(own, swapped):
+    return swapped.astype(F32) if own is None else own.astype(F32) + swapped.astype(F32)
 
 
 def scatter_rows(x, axis="tensor"):
@@ -185,8 +207,29 @@
         return total
 
 
+class Joined:
+    def __init__(self, *reduces):
+        self.reduces = [r for r in reduces if r is not None]
+
+    def sends(self):
+        self.axis = (1, 1, 0)[self.reduces[0].stage]
+        self.sizes, lists = [], [r.sends() for r in self.reduces]
+        if not lists[0]:
+            return []
+        self.sizes = [a[0].shape[self.axis] for a in lists]
+        return [jnp.concatenate(parts, axis=self.axis) for parts in zip(*lists)]
+
+    def move(self, sent):
+        return self.reduces[0].move(sent)
+
+    def take(self, got):
+        begin = 0
+        for r, size in zip(self.reduces, self.sizes or [0] * len(self.reduces)):
+            r.take([lax.slice_in_dim(a, begin, begin + size, axis=self.axis) for a in got])
+            begin += size
+
+
 def phase(work, inputs, reduces):
-    reduces = [r for r in reduces if r is not None]
     sends = [r.sends() for r in reduces]
     (inputs, sends) = lax.optimization_barrier((list(inputs), sends))
     results = work(*inputs)
@@ -319,8 +362,8 @@
         p = jnp.where(mask_of(start, j, i, bq), jnp.exp(s - lse), 0.0)
         dp = dot(v_ref[0, at_key, :], dos, 1, 0)
         ds = (p * (dp - inner)).astype(BF16)
-        dv_sum[:, at_key] += dot(dos, p.astype(BF16), 1, 1)
-        dk_sum[:, at_key] += dot(qs, ds, 1, 1)
+        dv_sum[at_key, :] += dot(p.astype(BF16), dos, 1, 1)
+        dk_sum[at_key, :] += dot(ds, qs, 1, 1)
         return dq + dot(kt_ref[:, at_key], ds, 1, 0)
 
     dq = lax.fori_loop(low[i], i + 1, step, jnp.zeros((HEAD_SIZE, 2 * bq), F32))
@@ -340,8 +383,8 @@
 
     @pl.when(i == pl.num_programs(1) - 1)
     def _():
-        dk_ref[...] = turn_back(dk_sum[...], cos_ref[...], sin_ref[...])
-        dv_ref[...] = dv_sum[...].astype(BF16)
+        dk_ref[...] = turn_back(dk_sum[...].T, cos_ref[...], sin_ref[...])
+        dv_ref[...] = dv_sum[...].T.astype(BF16)
 
 
 def attend_back(first, heads, q_t, do_t, o_t, lse, k, v, k_t, start, cosine, sine, low):
@@ -372,7 +415,7 @@
                 pl.BlockSpec((2 * HEAD_SIZE, BLOCK), lambda h, i, low: (h, i)), grad, grad,
             ],
             scratch_shapes=[
-                pltpu.VMEM((HEAD_SIZE, rows), F32), pltpu.VMEM((HEAD_SIZE, rows), F32),
+                pltpu.VMEM((rows, HEAD_SIZE), F32), pltpu.VMEM((rows, HEAD_SIZE), F32),
             ],
         ),
         out_shape=[
@@ -717,88 +760,105 @@
     each = expert_local // calls
     parity = (me % 2).astype(jnp.int32).reshape(1)
     slots = table * (width // 128)
-    out_part, dx_part = 0.0, 0.0
-    dg, sums = [], []
+    parts, sums = [], []
     for call in range(calls):
         picked = slice(call * each, (call + 1) * each)
-        made = []
-
-        def work(counted, picked=picked, call=call, made=made):
-            *outs, mark = expert_call(
-                slots[picked].reshape(-1), counted, parity, hidden_two, grad_all, slot_gate,
-                big, call * each, each,
+
+        def work(counted, picked=picked, call=call):
+            return list(
+                expert_call(
+                    slots[picked].reshape(-1), counted, parity, hidden_two, grad_all, slot_gate,
+                    big, call * each, each,
+                )[:5]
             )
-            made.extend(outs)
-            return [mark]
-
-        phase(work, [count[picked]], sums)
-        keep, send, out_p, dx_p, dg_p = made
+
+        keep, send, out_p, dx_p, dg_p = phase(work, [count[picked]], sums)
         sums.append(Reduce(keep, send))
-        out_part = out_part + out_p.astype(F32)
-        dx_part = dx_part + dx_p.astype(F32)
-        dg.append(dg_p[:, :, 0])
+        parts.append((out_p, dx_p, dg_p))
 
     two_a, two_b = sums[2].split(3, 1)
 
-    dg = jnp.where(filled, jnp.concatenate(dg, axis=0), 0.0)
-
-    def over_x(sent, sent_out, dg):
+    def total_of(*flat):
+        outs, backs, dgs = flat[:calls], flat[calls : 2 * calls], flat[2 * calls :]
+        out_part = functools.reduce(jnp.add, [o.astype(F32) for o in outs]).astype(BF16)
+        dx_part = functools.reduce(jnp.add, [o.astype(F32) for o in backs]).astype(BF16)
+        dg = jnp.where(filled, jnp.concatenate([d[:, :, 0] for d in dgs], axis=0), 0.0)
         dg = jnp.where(is_low, dg[:, :, None], 0.0).astype(BF16)
         dg = jnp.einsum("esh,esl->ehl", is_high, dg, preferred_element_type=F32)
         dg = dg.reshape(expert_local, rows)
         d_dense = lax.dynamic_update_slice_in_dim(
-            jnp.zeros((rows, EXPERTS), F32), dg.T, rank * expert_local, 1
+            jnp.zeros((rows, 128), BF16), dg.T.astype(BF16), rank * expert_local, 1
         )
-        return [scatter_rows(sent), scatter_rows(d_dense), sent_out]
-
-    d_rows, d_gates, out_part = phase(
-        over_x, [dx_part.astype(BF16), out_part.astype(BF16), dg],
-        [sums[1], two_a, sums[3]],
-    )
+        own, sent = leave_rows(jnp.concatenate([dx_part, d_dense], axis=1))
+        return [out_part, sent] + ([] if own is None else [own])
+
+    out_part, sent, *own = phase(total_of, [a for p in zip(*parts) for a in p], [sums[3]])
     three_a, three_b = sums[3].split(2, 2)
+    (swapped,) = phase(lambda sent: [swap_sums(sent)], [sent], [sums[1], two_a])
+    d_both = add_rows_of(own[0] if own else None, swapped)
+    d_rows, d_gates = d_both[:, :width], d_both[:, width : width + EXPERTS]
     gates_own = lax.dynamic_slice_in_dim(gates_f, own_row, local_rows, 0)
     d_logits = gates_own * (d_gates - jnp.sum(d_gates * gates_own, axis=-1, keepdims=True))
     router_grad = jnp.dot(hidden_rows.astype(F32).T, d_logits, precision=exact_mode)
     d_rows = d_rows + jnp.dot(d_logits, router_weight.astype(F32).T, precision=exact_mode)
     d_norm_two, gain_two_grad = rms_back(d_rows, residual_two, inverse_two, gain_two)
     d_residual = cotangent.astype(F32) + d_norm_two
-    (d_all,) = phase(
-        lambda sent: [gather_rows(sent)], [d_residual.astype(BF16)], [two_a, two_b, three_a]
-    )
+    d_sent = d_residual.astype(BF16)
+    (swapped,) = phase(
+        lambda sent: [swap_rows(sent)], [d_sent], [two_a, Joined(two_b, three_a)]
+    )
+    d_all = join_rows(d_sent, swapped)
 
     do_t = dot(out_weight_t, d_all, 0, 1).astype(BF16)
 
-    def back(do_t, out_part):
+    moe_own, moe_sent = leave_rows(out_part)
+
+    def back(do_t, sent):
         parts = attend_back(
             0, kv_heads, q_t, do_t, o_t, lse, k, v, k_t, start, cosine, sine, low
         )
-        return list(parts) + [scatter_rows(out_part)]
-
-    dq_t, dk_t, dv_t, moe_rows = phase(
-        back, [do_t, out_part], [two_b, three_a, three_b]
-    )
+        return list(parts) + [swap_sums(sent)]
+
+    dq_t, dk_t, dv_t, swapped = phase(
+        back, [do_t, moe_sent], [Joined(two_b, three_a)] + [r for r in [three_b] if r is not None]
+    )
+    moe_rows = add_rows_of(moe_own, swapped)
     output = (residual_two + moe_rows).astype(BF16)
     d_qkv_t = jnp.concatenate([dq_t, dk_t, dv_t], axis=0)
-    grad_out_t = dot(d_all, o_t, 0, 1).astype(BF16)
-    grad_qkv = dot(hidden_one, d_qkv_t, 0, 1).astype(BF16)
     d_hidden_part = dot(d_qkv_t, qkv_weight, 0, 1)
-    gain_one_grad = jnp.sum(d_hidden_part * inputs_all.astype(F32) * inverse_all, axis=0)
-    misc = jnp.concatenate(
-        [router_grad, gain_one_grad[:, None], gain_two_grad[:, None]], axis=1
-    ).astype(BF16)
-    misc = jnp.pad(misc, ((0, 0), (0, -misc.shape[1] % 128)))
-    small_grad = jnp.concatenate([grad_qkv, grad_out_t, misc], axis=1)
-    small_grad = small_grad.reshape(dp // 2, 2, shard_rows, small_grad.shape[1])
-    even = parity[0] == 0
-    first, second = small_grad[:, 0], small_grad[:, 1]
-    small = Reduce(jnp.where(even, first, second), jnp.where(even, second, first))
+    end_own, end_sent = leave_rows(d_hidden_part.astype(BF16))
+    halves = 2 if tensor == 2 else 1
+    size = end_sent.shape[0] // halves
+
+    def grads(d_qkv_t, d_part, sent):
+        grad_out_t = dot(d_all, o_t, 0, 1).astype(BF16)
+        grad_qkv = dot(hidden_one, d_qkv_t, 0, 1).astype(BF16)
+        gain_one_grad = jnp.sum(d_part * inputs_all.astype(F32) * inverse_all, axis=0)
+        misc = jnp.concatenate(
+            [router_grad, gain_one_grad[:, None], gain_two_grad[:, None]], axis=1
+        ).astype(BF16)
+        misc = jnp.pad(misc, ((0, 0), (0, -misc.shape[1] % 128)))
+        small_grad = jnp.concatenate([grad_qkv, grad_out_t, misc], axis=1)
+        small_grad = small_grad.reshape(dp // 2, 2, shard_rows, small_grad.shape[1])
+        even = parity[0] == 0
+        first, second = small_grad[:, 0], small_grad[:, 1]
+        return [
+            jnp.where(even, first, second), jnp.where(even, second, first), swap_sums(sent),
+        ]
+
+    keep, send, swapped = phase(
+        grads, [d_qkv_t, d_hidden_part, end_sent[:size]],
+        [r for r in [three_b] if r is not None],
+    )
+    small = Reduce(keep, send)
 
     def end(sent):
         for _ in range(3):
             small.take(small.move(small.sends()))
-        return [scatter_rows(sent), small.result()]
-
-    d_hidden_one, small_sum = phase(end, [d_hidden_part.astype(BF16)], [three_b])
+        return [small.result()] + ([swap_sums(sent)] if halves == 2 else [])
+
+    small_sum, *rest = phase(end, [end_sent[size:]], [])
+    d_hidden_one = add_rows_of(end_own, jnp.concatenate([swapped] + rest, axis=0))
     d_norm_one, _ = rms_back(
         d_hidden_one, inputs_f, lax.dynamic_slice_in_dim(inverse_all, own_row, local_rows, 0),
         gain_one,

time: 1090 us -> 1030 us (0.945)
  waiting for transfers between devices: 331 us -> 252 us
  Pallas kernels: 382 us -> 337 us
  local copies, waits for them, and re-layouts: 93.2 us -> 121 us
  starting transfers between devices: 97.7 us -> 122 us
    ppermute x5 -> x1, waiting for transfers between devices: 90.6 us -> 47.1 us  [scatter_rows(): lax.ppermute(lax.dynamic_slice_in_dim(x, (1 - rank) * rows, rows, 0), axi...]
    pallas_call x4, Pallas kernels: 280 us -> 241 us  [expert_call(): pl.pallas_call(expert_kernel, grid_spec=pltpu.PrefetchScalarGridSpec(num_...]
    ppermute x3 -> x2, waiting for transfers between devices: 69.1 us -> 37.6 us  [gather_rows(): other = lax.ppermute(x, axis, [(0, 1), (1, 0)])]
    ppermute x0 -> x4, starting transfers between devices: none -> 21.1 us  [swap_sums(): return lax.ppermute(x, 'tensor', [(0, 1), (1, 0)])]
    optimization_barrier x0 -> x4, local copies, waits for them, and re-layouts: none -> 11 us  [phase(): inputs, sends = lax.optimization_barrier((list(inputs), sends))]
    ppermute x33 -> x29, starting transfers between devices: 79.9 us -> 86 us  [move(): return [lax.ppermute(a, 'dp', p) for a, p in zip(sent, pairs)]]
    ppermute x33 -> x29, waiting for transfers between devices: 109 us -> 107 us  [move(): return [lax.ppermute(a, 'dp', p) for a, p in zip(sent, pairs)]]
  transfers between devices with their start and end apart: 49 -> 45, of which waited for: 21 -> 16; matrix products, arithmetic and copies ran while one was open for 14% -> 19% of each run, Pallas kernels for 29% -> 28%
where the time goes in v3:
time: 1030 us; the launch traced here: 1020 us
  Pallas kernels  337 us (33%)
  waiting for transfers between devices  252 us (24%)
  other arithmetic  128 us (12%)
  starting transfers between devices  122 us (12%)
  local copies, waits for them, and re-layouts  121 us (12%)
  matrix products  45.9 us (4%)
  between operations  17.6 us (2%)
    pallas_call x4, Pallas kernels, expert_call(): pl.pallas_call(expert_kernel, grid_spec=pltpu.PrefetchScalarGridSpec(num_...  241 us
    ppermute x29, waiting for transfers between devices, move(): return [lax.ppermute(a, 'dp', p) for a, p in zip(sent, pairs)]  107 us
    ppermute x29, starting transfers between devices, move(): return [lax.ppermute(a, 'dp', p) for a, p in zip(sent, pairs)]  86 us
    pallas_call x1, Pallas kernels, attend_back(): pl.pallas_call(attend_back_kernel, grid_spec=pltpu.PrefetchScalarGridSpec...  51.6 us
    ppermute x1, waiting for transfers between devices, scatter_rows(): lax.ppermute(lax.dynamic_slice_in_dim(x, (1 - rank) * rows, rows, 0), axi...  47.1 us
    pallas_call x1, Pallas kernels, attend(): pl.pallas_call(attend_kernel, grid_spec=pltpu.PrefetchScalarGridSpec(num_...  44.2 us
    ppermute x2, waiting for transfers between devices, gather_rows(): other = lax.ppermute(x, axis, [(0, 1), (1, 0)])  37.6 us
    dot_general x7, matrix products, dot(): lax.dot_general(a, b, (((ca,), (cb,)), ((), ())), preferred_element_type=...  37.4 us
  transfers between devices with their start and end apart: 45, of which 16 were waited for; matrix products, arithmetic and copies ran while one was open for 19% of the time, Pallas kernels for 28%

profile of v3, /device:TPU:0, one launch (start us, length us, event | category | flops | bytes accessed | tf_op | source)
XLA Modules:
  0.0 1023.5 jit_solution(10242359593580498237)
XLA Ops:
  14.9 5.1 collective-permute-start.1
  22.7 14.6 %collective-permute-done = bf16[64,1664]{1,0:T(8,128)(2,1)} collective-permute-done((bf16[64,1664]{1,0:T(8,128)(2,1)S(1)}, bf16[64,1664]{1,0:T(8,128)(2,1)}, u32[]{:S(2)}, u32[]{:S(2)}) %collective-permute-start) | collective-permute-done | bytes 213024 | tf_op jit(solution)/shard_map/ppermute | solution.py:122
  39.2 6.1 collective-permute-done.2
  48.2 37.0 %collective-permute-done.3 = bf16[4,64,1664]{2,1,0:T(8,128)(2,1)} collective-permute-done((bf16[4,64,1664]{2,1,0:T(8,128)(2,1)S(1)}, bf16[4,64,1664]{2,1,0:T(8,128)(2,1)}, u32[]{:S(2)}, u32[]{:S(2)}) %collective-permute-start.3) | collective-permute-done | bytes 852000 | tf_op jit(solution)/shard_map/ppermute | solution.py:124
  92.1 5.0 fusion.25
  110.0 44.2 %attend.1 = (bf16[512,2048]{1,0:T(8,128)(2,1)}, f32[4,2,2048]{2,1,0:T(2,128)}) custom-call(s32[8]{0:T(128)} %and_select_fusion.low, bf16[512,2048]{1,0:T(8,128)(2,1)} %bitcast.273, bf16[4,2048,64]{2,1,0:T(8,128)(2,1)} %bitcast.275, bf16[256,2048]{1,0:T(8,128)(2,1)} %slice.329.v_ref, s32[1,2048]{1,0:T(1,128)} %bitcast.324), custom_call_target="tpu_custom_call" | custom-call | flops 1 | bytes 150000000 | tf_op jit(solution)/shard_map/attend/pallas_call | solution.py:311
  154.2 4.4 convolution_convert_fusion
  163.0 47.1 %collective-permute-done.7 = bf16[1024,1024]{1,0:T(8,128)(2,1)} collective-permute-done((bf16[1024,1024]{1,0:T(8,128)(2,1)}, bf16[1024,1024]{1,0:T(8,128)(2,1)}, u32[]{:S(2)}, u32[]{:S(2)}) %collective-permute-start.7) | collective-permute-done | bytes 2097184 | tf_op jit(solution)/shard_map/ppermute | solution.py:87
  224.8 37.6 %collective-permute-done.8 = bf16[1024,1024]{1,0:T(8,128)(2,1)} collective-permute-done((bf16[1024,1024]{1,0:T(8,128)(2,1)S(1)}, bf16[1024,1024]{1,0:T(8,128)(2,1)}, u32[]{:S(2)}, u32[]{:S(2)}) %collective-permute-start.8) | collective-permute-done | bytes 2097184 | tf_op jit(solution)/shard_map/ppermute | solution.py:41
  271.4 4.0 copy.345.gate_ref
  275.4 4.1 pad_maximum_fusion.1.x_hbm
  281.4 45.6 %experts.4 = (bf16[8,4,3,64,512]{4,3,2,1,0:T(8,128)(2,1)}, bf16[8,4,3,64,512]{4,3,2,1,0:T(8,128)(2,1)}, bf16[2048,1024]{1,0:T(8,128)(2,1)}, bf16[2048,1024]{1,0:...) custom-call(s32[3072]{0:T(1024)} %reshape.814.table, s32[4]{0:T(128)} %get-tuple-element.451.count, ...), custom_call_target="tpu_custom_call" | custom-call | flops 1 | bytes 150000000 | tf_op jit(solution)/shard_map/experts/pallas_call | solution.py:615
  327.1 4.3 collective-permute-start.9
  332.0 68.9 %experts.5 = (bf16[8,4,3,64,512]{4,3,2,1,0:T(8,128)(2,1)}, bf16[8,4,3,64,512]{4,3,2,1,0:T(8,128)(2,1)}, bf16[2048,1024]{1,0:T(8,128)(2,1)}, bf16[2048,1024]{1,0:...) custom-call(s32[3072]{0:T(1024)} %reshape.819.table, s32[4]{0:T(128)} %get-tuple-element.159.count, ...), custom_call_target="tpu_custom_call" | custom-call | flops 1 | bytes 150000000 | tf_op jit(solution)/shard_map/experts/pallas_call | solution.py:615
  400.9 5.9 fusion.12
  409.5 5.0 collective-permute-start.10
  418.5 68.4 %experts.6 = (bf16[8,4,3,64,512]{4,3,2,1,0:T(8,128)(2,1)}, bf16[8,4,3,64,512]{4,3,2,1,0:T(8,128)(2,1)}, bf16[2048,1024]{1,0:T(8,128)(2,1)}, bf16[2048,1024]{1,0:...) custom-call(s32[3072]{0:T(1024)} %reshape.820.table, s32[4]{0:T(128)} %get-tuple-element.170.count, ...), custom_call_target="tpu_custom_call" | custom-call | flops 1 | bytes 150000000 | tf_op jit(solution)/shard_map/experts/pallas_call | solution.py:615
  490.0 6.1 fusion.13
  496.0 4.0 fusion.40
  503.1 4.9 collective-permute-start.12
  512.4 58.3 %experts.7 = (bf16[8,4,3,64,512]{4,3,2,1,0:T(8,128)(2,1)}, bf16[8,4,3,64,512]{4,3,2,1,0:T(8,128)(2,1)}, bf16[2048,1024]{1,0:T(8,128)(2,1)}, bf16[2048,1024]{1,0:...) custom-call(s32[3072]{0:T(1024)} %reshape.823.table, s32[4]{0:T(128)} %get-tuple-element.183.count, ...), custom_call_target="tpu_custom_call" | custom-call | flops 1 | bytes 150000000 | tf_op jit(solution)/shard_map/experts/pallas_call | solution.py:615
  572.2 5.2 slice.203
  577.4 4.8 constant_dynamic-slice_fusion
  591.8 5.0 slice.204
  597.8 5.2 dynamic_update_slice.38
  608.4 4.0 fusion.37
  613.4 6.5 add_convert_fusion
  621.7 6.7 add_convert_fusion.1
  628.3 19.8 %collective-permute-start.18 = (bf16[1024,1152]{1,0:T(8,128)(2,1)}, bf16[1024,1152]{1,0:T(8,128)(2,1)}, u32[]{:S(2)}, u32[]{:S(2)}) collective-permute-start(bf16[1024,1152]{1,0:T(8,128)(2,1)} %get-tuple-element.223), channel_id=1, source_target_pairs={{0,1},{1,0},{2,3},{3,2},{4,5},{5,4},{6,7},{7,6},{8,9},{9,8},{10,11... | collective-permute-start | bytes 7077896 | tf_op jit(solution)/shard_map/ppermute | solution.py:74
  663.0 4.5 collective-permute-start.20
  671.9 43.8 %collective-permute-done.19 = bf16[4,3,64,512]{3,2,0,1:T(8,128)(2,1)} collective-permute-done((bf16[4,3,64,512]{3,2,0,1:T(8,128)(2,1)}, bf16[4,3,64,512]{3,2,0,1:T(8,128)(2,1)}, u32[]{:S(2)}, u32[]{:S(2)}) %collective-permute-start.19) | collective-permute-done | bytes 786464 | tf_op jit(solution)/shard_map/ppermute | solution.py:184
  718.7 4.0 multiply_reduce_fusion
  731.1 17.9 %collective-permute-start.24 = (bf16[3,3,64,512]{3,2,0,1:T(8,128)(2,1)S(1)}, bf16[3,3,64,512]{3,2,0,1:T(8,128)(2,1)S(1)}, u32[]{:S(2)}, u32[]{:S(2)}) collective-permute-start(bf16[3,3,64,512]{3,2,0,1:T(8,128)(2,1)S(1)} %get-tuple-element.233), channel_id=1, source_target_pairs={{0,16},{2,18},{4,20},{6,22},{8,24},{10,26},{12,28},{14,30},{16,0},... | collective-permute-start | bytes 1769480 | tf_op jit(solution)/shard_map/ppermute | solution.py:184
  756.4 31.2 %collective-permute-done.24 = bf16[3,3,64,512]{3,2,0,1:T(8,128)(2,1)S(1)} collective-permute-done((bf16[3,3,64,512]{3,2,0,1:T(8,128)(2,1)S(1)}, bf16[3,3,64,512]{3,2,0,1:T(8,128)(2,1)S(1)}, u32[]{:S(2)}, u32[]{:S(2)}) %collective-permute-start.24) | collective-permute-done | bytes 589856 | tf_op jit(solution)/shard_map/ppermute | solution.py:184
  795.6 4.9 convolution_convert_fusion.1.do_ref
  812.7 9.9 collective-permute-start.30
  826.6 51.6 %attend_back.1 = (bf16[512,2048]{1,0:T(8,128)(2,1)}, bf16[256,2048]{1,0:T(8,128)(2,1)}, bf16[256,2048]{1,0:T(8,128)(2,1)}) custom-call(s32[8]{0:T(128)} %and_select_fusion.low, bf16[512,2048]{1,0:T(8,128)(2,1)} %bitcast.274, bf16[512,2048]{1,0:T(8,128)(2,1)} %convolution_convert_fusion.1.do_ref, bf16[512,2048]{1,0:T(8,128)(2,1)} %get-tuple-element.150.o_ref, ...), custom_call_target="tpu_custom_call" | custom-call | flops 1 | bytes 150000000 | tf_op jit(solution)/shard_map/attend_back/pallas_call | solution.py:397
  878.2 5.7 fusion.43
  888.7 6.7 fusion.23
  895.4 7.3 copy.389
  908.7 8.1 convolution_convert_fusion.2
  922.6 9.3 copy.396
  931.9 5.4 fusion.4
  939.3 4.4 copy.397
  963.0 15.0 %collective-permute-done.38 = bf16[4,64,1664]{2,1,0:T(8,128)(2,1)S(1)} collective-permute-done((bf16[4,64,1664]{2,1,0:T(8,128)(2,1)S(1)}, bf16[4,64,1664]{2,1,0:T(8,128)(2,1)S(1)}, u32[]{:S(2)}, u32[]{:S(2)}) %collective-permute-start.38) | collective-permute-done | bytes 852000 | tf_op jit(solution)/shard_map/ppermute | solution.py:184
  978.2 7.5 collective-permute-start.39
  989.5 11.3 %collective-permute-done.39 = bf16[64,1664]{1,0:T(8,128)(2,1)S(1)} collective-permute-done((bf16[64,1664]{1,0:T(8,128)(2,1)S(1)}, bf16[64,1664]{1,0:T(8,128)(2,1)S(1)}, u32[]{:S(2)}, u32[]{:S(2)}) %collective-permute-start.39) | collective-permute-done | bytes 213024 | tf_op jit(solution)/shard_map/ppermute | solution.py:184
  1006.0 7.8 fusion.10
  (438 shorter events, 211.9 us)
Async XLA Ops:
  8.0 209.3 %sort.10.cloned.1.call-start = ((), (), s32[]{:S(2)}) async-start(), calls=%async_computation.1 | async-start | bytes 393248 | tf_op jit(solution)/shard_map/jit(sort)/sort | solution.py:722
  10.3 271.1 %all-gather.2.cloned.1.call-start = ((), (), s32[]{:S(2)}) async-start(), calls=%async_computation | async-start | bytes 53477376 | tf_op jit(solution)/shard_map/all_gather | solution.py:698
  14.9 23.4 %collective-permute-start.1 = (bf16[64,1664]{1,0:T(8,128)(2,1)S(1)}, bf16[64,1664]{1,0:T(8,128)(2,1)}, u32[]{:S(2)}, u32[]{:S(2)}) collective-permute-start(bf16[64,1664]{1,0:T(8,128)(2,1)S(1)} %pad.8), channel_id=1, source_target_pairs={{0,24},{2,26},{4,28},{6,30},{8,0},{10,2},{12,4},{14,6},{16,8},{18,... | collective-permute-start | bytes 638984 | tf_op jit(solution)/shard_map/ppermute | solution.py:122
  20.0 17.3 %collective-permute-start = (bf16[64,1664]{1,0:T(8,128)(2,1)S(1)}, bf16[64,1664]{1,0:T(8,128)(2,1)}, u32[]{:S(2)}, u32[]{:S(2)}) collective-permute-start(bf16[64,1664]{1,0:T(8,128)(2,1)S(1)} %pad.8), channel_id=1, source_target_pairs={{0,8},{2,10},{4,12},{6,14},{8,16},{10,18},{12,20},{14,22},{16,24},... | collective-permute-start | bytes 638984 | tf_op jit(solution)/shard_map/ppermute | solution.py:122
  20.0 25.3 %collective-permute-start.2 = (bf16[64,1664]{1,0:T(8,128)(2,1)S(1)}, bf16[64,1664]{1,0:T(8,128)(2,1)}, u32[]{:S(2)}, u32[]{:S(2)}) collective-permute-start(bf16[64,1664]{1,0:T(8,128)(2,1)S(1)} %pad.8), channel_id=1, source_target_pairs={{0,16},{2,18},{4,20},{6,22},{8,24},{10,26},{12,28},{14,30},{16,0},... | collective-permute-start | bytes 638984 | tf_op jit(solution)/shard_map/ppermute | solution.py:122
  21.0 67.1 %collective-permute-start.5 = (bf16[1024,1024]{1,0:T(8,128)(2,1)S(1)}, bf16[1024,1024]{1,0:T(8,128)(2,1)}, u32[]{:S(2)}, u32[]{:S(2)}) collective-permute-start(bf16[1024,1024]{1,0:T(8,128)(2,1)S(1)} %copy-done.6), channel_id=1, source_target_pairs={{0,1},{1,0},{2,3},{3,2},{4,5},{5,4},{6,7},{7,6},{8,9},{9,8},{10,11... | collective-permute-start | bytes 6291464 | tf_op jit(solution)/shard_map/ppermute | solution.py:41
  46.3 38.8 %collective-permute-start.3 = (bf16[4,64,1664]{2,1,0:T(8,128)(2,1)S(1)}, bf16[4,64,1664]{2,1,0:T(8,128)(2,1)}, u32[]{:S(2)}, u32[]{:S(2)}) collective-permute-start(bf16[4,64,1664]{2,1,0:T(8,128)(2,1)S(1)} %bitcast_dynamic-update-slice_fusion.4), channel_id=1, source_target_pairs={{0,4},{2,6},{4,0},{6,2},{8,12},{10,14},{12,8},{14,10},{16,20},{18,... | collective-permute-start | bytes 2555912 | tf_op jit(solution)/shard_map/ppermute | solution.py:124
  86.4 4.7 collective-permute-start.4
  102.9 51.3 %collective-permute-start.6 = (bf16[1024,1024]{1,0:T(8,128)(2,1)}, bf16[1024,1024]{1,0:T(8,128)(2,1)}, u32[]{:S(2)}, u32[]{:S(2)}) collective-permute-start(bf16[1024,1024]{1,0:T(8,128)(2,1)} %param.27), channel_id=1, source_target_pairs={{0,1},{1,0},{2,3},{3,2},{4,5},{5,4},{6,7},{7,6},{8,9},{9,8},{10,11... | collective-permute-start | bytes 6291464 | tf_op jit(solution)/shard_map/ppermute | solution.py:49
  162.1 48.1 %collective-permute-start.7 = (bf16[1024,1024]{1,0:T(8,128)(2,1)}, bf16[1024,1024]{1,0:T(8,128)(2,1)}, u32[]{:S(2)}, u32[]{:S(2)}) collective-permute-start(bf16[1024,1024]{1,0:T(8,128)(2,1)} %constant_dynamic-slice_fusion.43), channel_id=1, source_target_pairs={{0,1},{1,0},{2,3},{3,2},{4,5},{5,4},{6,7},{7,6},{8,9},{9,8},{10,11... | collective-permute-start | bytes 6291464 | tf_op jit(solution)/shard_map/ppermute | solution.py:87
  215.3 47.0 %collective-permute-start.8 = (bf16[1024,1024]{1,0:T(8,128)(2,1)S(1)}, bf16[1024,1024]{1,0:T(8,128)(2,1)}, u32[]{:S(2)}, u32[]{:S(2)}) collective-permute-start(bf16[1024,1024]{1,0:T(8,128)(2,1)S(1)} %multiply_convert_fusion), channel_id=1, source_target_pairs={{0,1},{1,0},{2,3},{3,2},{4,5},{5,4},{6,7},{7,6},{8,9},{9,8},{10,11... | collective-permute-start | bytes 6291464 | tf_op jit(solution)/shard_map/ppermute | solution.py:41
  327.1 73.8 %collective-permute-start.9 = (bf16[8,4,3,64,512]{4,3,2,1,0:T(8,128)(2,1)}, bf16[8,4,3,64,512]{4,3,2,1,0:T(8,128)(2,1)}, u32[]{:S(2)}, u32[]{:S(2)}) collective-permute-start(bf16[8,4,3,64,512]{4,3,2,1,0:T(8,128)(2,1)} %get-tuple-element.165), channel_id=1, source_target_pairs={{0,2},{2,0},{4,6},{6,4},{8,10},{10,8},{12,14},{14,12},{16,18},{18,... | collective-permute-start | bytes 18874376 | tf_op jit(solution)/shard_map/ppermute | solution.py:184
  406.8 83.2 %collective-permute-start.11 = (bf16[8,4,3,64,512]{4,3,2,1,0:T(8,128)(2,1)}, bf16[8,4,3,64,512]{4,3,2,1,0:T(8,128)(2,1)}, u32[]{:S(2)}, u32[]{:S(2)}) collective-permute-start(bf16[8,4,3,64,512]{4,3,2,1,0:T(8,128)(2,1)} %get-tuple-element.177), channel_id=1, source_target_pairs={{0,2},{2,0},{4,6},{6,4},{8,10},{10,8},{12,14},{14,12},{16,18},{18,... | collective-permute-start | bytes 18874376 | tf_op jit(solution)/shard_map/ppermute | solution.py:184
  409.5 80.5 %collective-permute-start.10 = (bf16[4,4,3,64,512]{4,3,1,2,0:T(8,128)(2,1)}, bf16[4,4,3,64,512]{4,3,1,2,0:T(8,128)(2,1)}, u32[]{:S(2)}, u32[]{:S(2)}) collective-permute-start(bf16[4,4,3,64,512]{4,3,1,2,0:T(8,128)(2,1)} %fusion.12), channel_id=1, source_target_pairs={{0,4},{2,6},{4,0},{6,2},{8,12},{10,14},{12,8},{14,10},{16,20},{18,... | collective-permute-start | bytes 9437192 | tf_op jit(solution)/shard_map/ppermute | solution.py:184
  500.0 72.2 %collective-permute-start.16 = (bf16[8,4,3,64,512]{4,3,2,1,0:T(8,128)(2,1)}, bf16[8,4,3,64,512]{4,3,2,1,0:T(8,128)(2,1)}, u32[]{:S(2)}, u32[]{:S(2)}) collective-permute-start(bf16[8,4,3,64,512]{4,3,2,1,0:T(8,128)(2,1)} %get-tuple-element.193), channel_id=1, source_target_pairs={{0,2},{2,0},{4,6},{6,4},{8,10},{10,8},{12,14},{14,12},{16,18},{18,... | collective-permute-start | bytes 18874376 | tf_op jit(solution)/shard_map/ppermute | solution.py:184
  500.0 72.2 %collective-permute-start.15 = (bf16[4,4,3,64,512]{4,3,1,2,0:T(8,128)(2,1)}, bf16[4,4,3,64,512]{4,3,1,2,0:T(8,128)(2,1)}, u32[]{:S(2)}, u32[]{:S(2)}) collective-permute-start(bf16[4,4,3,64,512]{4,3,1,2,0:T(8,128)(2,1)} %fusion.13), channel_id=1, source_target_pairs={{0,4},{2,6},{4,0},{6,2},{8,12},{10,14},{12,8},{14,10},{16,20},{18,... | collective-permute-start | bytes 9437192 | tf_op jit(solution)/shard_map/ppermute | solution.py:184
  503.1 67.6 %collective-permute-start.12 = (bf16[4,3,64,512]{3,2,0,1:T(8,128)(2,1)}, bf16[4,3,64,512]{3,2,0,1:T(8,128)(2,1)S(1)}, u32[]{:S(2)}, u32[]{:S(2)}) collective-permute-start(bf16[4,3,64,512]{3,2,0,1:T(8,128)(2,1)} %get-tuple-element.189), channel_id=1, source_target_pairs={{0,16},{2,18},{4,20},{6,22},{8,24},{10,26},{12,28},{14,30},{16,0},... | collective-permute-start | bytes 2359304 | tf_op jit(solution)/shard_map/ppermute | solution.py:184
  508.0 62.8 %collective-permute-start.13 = (bf16[4,3,64,512]{3,2,0,1:T(8,128)(2,1)}, bf16[4,3,64,512]{3,2,0,1:T(8,128)(2,1)}, u32[]{:S(2)}, u32[]{:S(2)}) collective-permute-start(bf16[4,3,64,512]{3,2,0,1:T(8,128)(2,1)} %get-tuple-element.190), channel_id=1, source_target_pairs={{0,8},{2,10},{4,12},{6,14},{8,16},{10,18},{12,20},{14,22},{16,24},... | collective-permute-start | bytes 2359304 | tf_op jit(solution)/shard_map/ppermute | solution.py:184
  508.0 62.8 %collective-permute-start.14 = (bf16[4,3,64,512]{3,2,0,1:T(8,128)(2,1)}, bf16[4,3,64,512]{3,2,0,1:T(8,128)(2,1)}, u32[]{:S(2)}, u32[]{:S(2)}) collective-permute-start(bf16[4,3,64,512]{3,2,0,1:T(8,128)(2,1)} %get-tuple-element.191), channel_id=1, source_target_pairs={{0,24},{2,26},{4,28},{6,30},{8,0},{10,2},{12,4},{14,6},{16,8},{18,... | collective-permute-start | bytes 2359304 | tf_op jit(solution)/shard_map/ppermute | solution.py:184
  572.2 56.1 %collective-permute-start.17 = (bf16[8,4,3,64,512]{4,3,2,1,0:T(8,128)(2,1)}, bf16[8,4,3,64,512]{4,3,2,1,0:T(8,128)(2,1)}, u32[]{:S(2)}, u32[]{:S(2)}) collective-permute-start(bf16[8,4,3,64,512]{4,3,2,1,0:T(8,128)(2,1)} %get-tuple-element.216), channel_id=1, source_target_pairs={{0,2},{2,0},{4,6},{6,4},{8,10},{10,8},{12,14},{14,12},{16,18},{18,... | collective-permute-start | bytes 18874376 | tf_op jit(solution)/shard_map/ppermute | solution.py:184
  628.3 124.5 %copy-start.13 = (bf16[2048,1024]{1,0:T(8,128)(2,1)}, bf16[2048,1024]{1,0:T(8,128)(2,1)S(1)}, u32[]{:S(2)}) copy-start(bf16[2048,1024]{1,0:T(8,128)(2,1)S(1)} %add_convert_fusion.1) | copy-start | bytes 12582916
  628.3 87.9 %collective-permute-start.18 = (bf16[1024,1152]{1,0:T(8,128)(2,1)}, bf16[1024,1152]{1,0:T(8,128)(2,1)}, u32[]{:S(2)}, u32[]{:S(2)}) collective-permute-start(bf16[1024,1152]{1,0:T(8,128)(2,1)} %get-tuple-element.223), channel_id=1, source_target_pairs={{0,1},{1,0},{2,3},{3,2},{4,5},{5,4},{6,7},{7,6},{8,9},{9,8},{10,11... | collective-permute-start | bytes 7077896 | tf_op jit(solution)/shard_map/ppermute | solution.py:74
  648.1 68.1 %collective-permute-start.22 = (bf16[4,3,3,64,512]{4,3,1,2,0:T(8,128)(2,1)}, bf16[4,3,3,64,512]{4,3,1,2,0:T(8,128)(2,1)}, u32[]{:S(2)}, u32[]{:S(2)}) collective-permute-start(bf16[4,3,3,64,512]{4,3,1,2,0:T(8,128)(2,1)} %fusion.21), channel_id=1, source_target_pairs={{0,4},{2,6},{4,0},{6,2},{8,12},{10,14},{12,8},{14,10},{16,20},{18,... | collective-permute-start | bytes 7077896 | tf_op jit(solution)/shard_map/ppermute | solution.py:184
  651.4 140.1 %copy-start.25 = (bf16[8,1,3,64,512]{4,3,2,1,0:T(8,128)(2,1)}, bf16[8,1,3,64,512]{4,3,2,1,0:T(8,128)(2,1)S(1)}, u32[]{:S(2)}) copy-start(bf16[8,1,3,64,512]{4,3,2,1,0:T(8,128)(2,1)S(1)} %slice.207) | copy-start | bytes 4718596
  660.2 55.4 %collective-permute-start.19 = (bf16[4,3,64,512]{3,2,0,1:T(8,128)(2,1)}, bf16[4,3,64,512]{3,2,0,1:T(8,128)(2,1)}, u32[]{:S(2)}, u32[]{:S(2)}) collective-permute-start(bf16[4,3,64,512]{3,2,0,1:T(8,128)(2,1)} %get-tuple-element.224), channel_id=1, source_target_pairs={{0,16},{2,18},{4,20},{6,22},{8,24},{10,26},{12,28},{14,30},{16,0},... | collective-permute-start | bytes 2359304 | tf_op jit(solution)/shard_map/ppermute | solution.py:184
  663.0 52.7 %collective-permute-start.20 = (bf16[4,3,64,512]{3,2,0,1:T(8,128)(2,1)}, bf16[4,3,64,512]{3,2,0,1:T(8,128)(2,1)}, u32[]{:S(2)}, u32[]{:S(2)}) collective-permute-start(bf16[4,3,64,512]{3,2,0,1:T(8,128)(2,1)} %get-tuple-element.225), channel_id=1, source_target_pairs={{0,8},{2,10},{4,12},{6,14},{8,16},{10,18},{12,20},{14,22},{16,24},... | collective-permute-start | bytes 2359304 | tf_op jit(solution)/shard_map/ppermute | solution.py:184
  667.5 48.8 %collective-permute-start.21 = (bf16[4,3,64,512]{3,2,0,1:T(8,128)(2,1)}, bf16[4,3,64,512]{3,2,0,1:T(8,128)(2,1)}, u32[]{:S(2)}, u32[]{:S(2)}) collective-permute-start(bf16[4,3,64,512]{3,2,0,1:T(8,128)(2,1)} %get-tuple-element.226), channel_id=1, source_target_pairs={{0,24},{2,26},{4,28},{6,30},{8,0},{10,2},{12,4},{14,6},{16,8},{18,... | collective-permute-start | bytes 2359304 | tf_op jit(solution)/shard_map/ppermute | solution.py:184
  729.1 59.5 %collective-permute-start.27 = (bf16[4,3,3,64,512]{4,3,2,1,0:T(8,128)(2,1)S(1)}, bf16[4,3,3,64,512]{4,3,2,1,0:T(8,128)(2,1)S(1)}, u32[]{:S(2)}, u32[]{:S(2)}) collective-permute-start(bf16[4,3,3,64,512]{4,3,2,1,0:T(8,128)(2,1)S(1)} %pad_maximum_fusion.8), channel_id=1, source_target_pairs={{0,4},{2,6},{4,0},{6,2},{8,12},{10,14},{12,8},{14,10},{16,20},{18,... | collective-permute-start | bytes 7077896 | tf_op jit(solution)/shard_map/ppermute | solution.py:184
  729.5 58.9 %collective-permute-start.23 = (bf16[1024,1024]{1,0:T(8,128)(2,1)S(1)}, bf16[1024,1024]{1,0:T(8,128)(2,1)S(1)}, u32[]{:S(2)}, u32[]{:S(2)}) collective-permute-start(bf16[1024,1024]{1,0:T(8,128)(2,1)S(1)} %fusion.100), channel_id=1, source_target_pairs={{0,1},{1,0},{2,3},{3,2},{4,5},{5,4},{6,7},{7,6},{8,9},{9,8},{10,11... | collective-permute-start | bytes 6291464 | tf_op jit(solution)/shard_map/ppermute | solution.py:49
  731.1 56.5 %collective-permute-start.24 = (bf16[3,3,64,512]{3,2,0,1:T(8,128)(2,1)S(1)}, bf16[3,3,64,512]{3,2,0,1:T(8,128)(2,1)S(1)}, u32[]{:S(2)}, u32[]{:S(2)}) collective-permute-start(bf16[3,3,64,512]{3,2,0,1:T(8,128)(2,1)S(1)} %get-tuple-element.233), channel_id=1, source_target_pairs={{0,16},{2,18},{4,20},{6,22},{8,24},{10,26},{12,28},{14,30},{16,0},... | collective-permute-start | bytes 1769480 | tf_op jit(solution)/shard_map/ppermute | solution.py:184
  749.0 38.6 %collective-permute-start.25 = (bf16[3,3,64,512]{3,2,0,1:T(8,128)(2,1)S(1)}, bf16[3,3,64,512]{3,2,0,1:T(8,128)(2,1)S(1)}, u32[]{:S(2)}, u32[]{:S(2)}) collective-permute-start(bf16[3,3,64,512]{3,2,0,1:T(8,128)(2,1)S(1)} %get-tuple-element.234), channel_id=1, source_target_pairs={{0,8},{2,10},{4,12},{6,14},{8,16},{10,18},{12,20},{14,22},{16,24},... | collective-permute-start | bytes 1769480 | tf_op jit(solution)/shard_map/ppermute | solution.py:184
  749.0 39.5 %collective-permute-start.26 = (bf16[3,3,64,512]{3,2,0,1:T(8,128)(2,1)S(1)}, bf16[3,3,64,512]{3,2,0,1:T(8,128)(2,1)S(1)}, u32[]{:S(2)}, u32[]{:S(2)}) collective-permute-start(bf16[3,3,64,512]{3,2,0,1:T(8,128)(2,1)S(1)} %get-tuple-element.235), channel_id=1, source_target_pairs={{0,24},{2,26},{4,28},{6,30},{8,0},{10,2},{12,4},{14,6},{16,8},{18,... | collective-permute-start | bytes 1769480 | tf_op jit(solution)/shard_map/ppermute | solution.py:184
  800.5 83.4 %collective-permute-start.28 = (bf16[1024,1024]{1,0:T(8,128)(2,1)}, bf16[1024,1024]{1,0:T(8,128)(2,1)}, u32[]{:S(2)}, u32[]{:S(2)}) collective-permute-start(bf16[1024,1024]{1,0:T(8,128)(2,1)} %constant_dynamic-slice_fusion.17), channel_id=1, source_target_pairs={{0,1},{1,0},{2,3},{3,2},{4,5},{5,4},{6,7},{7,6},{8,9},{9,8},{10,11... | collective-permute-start | bytes 6291464 | tf_op jit(solution)/shard_map/ppermute | solution.py:74
  800.9 82.9 %collective-permute-start.32 = (bf16[4,2,3,64,512]{4,3,1,2,0:T(8,128)(2,1)}, bf16[4,2,3,64,512]{4,3,1,2,0:T(8,128)(2,1)}, u32[]{:S(2)}, u32[]{:S(2)}) collective-permute-start(bf16[4,2,3,64,512]{4,3,1,2,0:T(8,128)(2,1)} %fusion.28), channel_id=1, source_target_pairs={{0,4},{2,6},{4,0},{6,2},{8,12},{10,14},{12,8},{14,10},{16,20},{18,... | collective-permute-start | bytes 4718600 | tf_op jit(solution)/shard_map/ppermute | solution.py:184
  810.2 73.7 %collective-permute-start.31 = (bf16[3,3,64,512]{3,2,0,1:T(8,128)(2,1)}, bf16[3,3,64,512]{3,2,0,1:T(8,128)(2,1)}, u32[]{:S(2)}, u32[]{:S(2)}) collective-permute-start(bf16[3,3,64,512]{3,2,0,1:T(8,128)(2,1)} %copy.388), channel_id=1, source_target_pairs={{0,24},{2,26},{4,28},{6,30},{8,0},{10,2},{12,4},{14,6},{16,8},{18,... | collective-permute-start | bytes 1769480 | tf_op jit(solution)/shard_map/ppermute | solution.py:184
  812.7 71.2 %collective-permute-start.30 = (bf16[3,3,64,512]{3,2,0,1:T(8,128)(2,1)}, bf16[3,3,64,512]{3,2,0,1:T(8,128)(2,1)}, u32[]{:S(2)}, u32[]{:S(2)}) collective-permute-start(bf16[3,3,64,512]{3,2,0,1:T(8,128)(2,1)} %copy.387), channel_id=1, source_target_pairs={{0,8},{2,10},{4,12},{6,14},{8,16},{10,18},{12,20},{14,22},{16,24},... | collective-permute-start | bytes 1769480 | tf_op jit(solution)/shard_map/ppermute | solution.py:184
  822.6 61.3 %collective-permute-start.29 = (bf16[3,3,64,512]{3,2,0,1:T(8,128)(2,1)S(1)}, bf16[3,3,64,512]{3,2,0,1:T(8,128)(2,1)}, u32[]{:S(2)}, u32[]{:S(2)}) collective-permute-start(bf16[3,3,64,512]{3,2,0,1:T(8,128)(2,1)S(1)} %copy.386), channel_id=1, source_target_pairs={{0,16},{2,18},{4,20},{6,22},{8,24},{10,26},{12,28},{14,30},{16,0},... | collective-permute-start | bytes 1769480 | tf_op jit(solution)/shard_map/ppermute | solution.py:184
  916.9 27.9 %collective-permute-start.34 = (bf16[2,3,64,512]{3,2,0,1:T(8,128)(2,1)}, bf16[2,3,64,512]{3,2,0,1:T(8,128)(2,1)}, u32[]{:S(2)}, u32[]{:S(2)}) collective-permute-start(bf16[2,3,64,512]{3,2,0,1:T(8,128)(2,1)} %get-tuple-element.257), channel_id=1, source_target_pairs={{0,16},{2,18},{4,20},{6,22},{8,24},{10,26},{12,28},{14,30},{16,0},... | collective-permute-start | bytes 1179656 | tf_op jit(solution)/shard_map/ppermute | solution.py:184
  918.3 26.5 %collective-permute-start.35 = (bf16[2,3,64,512]{3,2,0,1:T(8,128)(2,1)}, bf16[2,3,64,512]{3,2,0,1:T(8,128)(2,1)}, u32[]{:S(2)}, u32[]{:S(2)}) collective-permute-start(bf16[2,3,64,512]{3,2,0,1:T(8,128)(2,1)} %get-tuple-element.258), channel_id=1, source_target_pairs={{0,8},{2,10},{4,12},{6,14},{8,16},{10,18},{12,20},{14,22},{16,24},... | collective-permute-start | bytes 1179656 | tf_op jit(solution)/shard_map/ppermute | solution.py:184
  920.3 26.6 %collective-permute-start.36 = (bf16[2,3,64,512]{3,2,0,1:T(8,128)(2,1)}, bf16[2,3,64,512]{3,2,0,1:T(8,128)(2,1)}, u32[]{:S(2)}, u32[]{:S(2)}) collective-permute-start(bf16[2,3,64,512]{3,2,0,1:T(8,128)(2,1)} %get-tuple-element.259), channel_id=1, source_target_pairs={{0,24},{2,26},{4,28},{6,30},{8,0},{10,2},{12,4},{14,6},{16,8},{18,... | collective-permute-start | bytes 1179656 | tf_op jit(solution)/shard_map/ppermute | solution.py:184
  922.2 25.2 %collective-permute-start.33 = (bf16[512,1024]{1,0:T(8,128)(2,1)}, bf16[512,1024]{1,0:T(8,128)(2,1)}, u32[]{:S(2)}, u32[]{:S(2)}) collective-permute-start(bf16[512,1024]{1,0:T(8,128)(2,1)} %get-tuple-element.256), channel_id=1, source_target_pairs={{0,1},{1,0},{2,3},{3,2},{4,5},{5,4},{6,7},{7,6},{8,9},{9,8},{10,11... | collective-permute-start | bytes 3145736 | tf_op jit(solution)/shard_map/ppermute | solution.py:74
  947.4 9.1 collective-permute-start.37
  954.5 46.5 %collective-permute-start.42 = (bf16[512,1024]{1,0:T(8,128)(2,1)S(1)}, bf16[512,1024]{1,0:T(8,128)(2,1)S(1)}, u32[]{:S(2)}, u32[]{:S(2)}) collective-permute-start(bf16[512,1024]{1,0:T(8,128)(2,1)S(1)} %copy-done.71), channel_id=1, source_target_pairs={{0,1},{1,0},{2,3},{3,2},{4,5},{5,4},{6,7},{7,6},{8,9},{9,8},{10,11... | collective-permute-start | bytes 3145736 | tf_op jit(solution)/shard_map/ppermute | solution.py:74
  956.7 21.2 %collective-permute-start.38 = (bf16[4,64,1664]{2,1,0:T(8,128)(2,1)S(1)}, bf16[4,64,1664]{2,1,0:T(8,128)(2,1)S(1)}, u32[]{:S(2)}, u32[]{:S(2)}) collective-permute-start(bf16[4,64,1664]{2,1,0:T(8,128)(2,1)S(1)} %fusion.56), channel_id=1, source_target_pairs={{0,4},{2,6},{4,0},{6,2},{8,12},{10,14},{12,8},{14,10},{16,20},{18,... | collective-permute-start | bytes 2555912 | tf_op jit(solution)/shard_map/ppermute | solution.py:184
  978.2 22.6 %collective-permute-start.39 = (bf16[64,1664]{1,0:T(8,128)(2,1)S(1)}, bf16[64,1664]{1,0:T(8,128)(2,1)S(1)}, u32[]{:S(2)}, u32[]{:S(2)}) collective-permute-start(bf16[64,1664]{1,0:T(8,128)(2,1)S(1)} %get-tuple-element.390), channel_id=1, source_target_pairs={{0,16},{2,18},{4,20},{6,22},{8,24},{10,26},{12,28},{14,30},{16,0},... | collective-permute-start | bytes 638984 | tf_op jit(solution)/shard_map/ppermute | solution.py:184
  985.7 15.1 %collective-permute-start.41 = (bf16[64,1664]{1,0:T(8,128)(2,1)S(1)}, bf16[64,1664]{1,0:T(8,128)(2,1)S(1)}, u32[]{:S(2)}, u32[]{:S(2)}) collective-permute-start(bf16[64,1664]{1,0:T(8,128)(2,1)S(1)} %get-tuple-element.391), channel_id=1, source_target_pairs={{0,24},{2,26},{4,28},{6,30},{8,0},{10,2},{12,4},{14,6},{16,8},{18,... | collective-permute-start | bytes 638984 | tf_op jit(solution)/shard_map/ppermute | solution.py:184
  986.9 13.9 %collective-permute-start.40 = (bf16[64,1664]{1,0:T(8,128)(2,1)S(1)}, bf16[64,1664]{1,0:T(8,128)(2,1)S(1)}, u32[]{:S(2)}, u32[]{:S(2)}) collective-permute-start(bf16[64,1664]{1,0:T(8,128)(2,1)S(1)} %get-tuple-element.392), channel_id=1, source_target_pairs={{0,8},{2,10},{4,12},{6,14},{8,16},{10,18},{12,20},{14,22},{16,24},... | collective-permute-start | bytes 638984 | tf_op jit(solution)/shard_map/ppermute | solution.py:184
  1004.5 10.0 collective-permute-start.43
  (109 other events, 970.3 us)
Sparse Core Ops, SparseCore 0:
  11.9 4.6 sort.12.cloned.1.call-done
  (1 shorter events, 0.0 us)
Sparse Core Ops, SparseCore 1:
  13.9 267.4 all-gather.1
